TPU v7x, 256 devices: a whole 4x4x8 slice. The times are simulated.
256 devices in a mesh: ctx: 64 (over z, x, core), tp: 4 (over y).
Axes of the slice: x: 4, y: 4, z: 8, core: 2. Of those that a mesh axis runs over, the one named last changes fastest.
Arguments:
- query: bfloat16 [16384, 8192], P('ctx', 'tp'), may hold values from -26 to 26
- key_in: bfloat16 [16384, 8192], P('ctx', 'tp'), may hold values from -6 to 6
- value_in: bfloat16 [16384, 8192], P('ctx', 'tp'), may hold values from -6 to 6
- out_grad: bfloat16 [16384, 8192], P('ctx', 'tp'), may hold values from -6 to 6
- mr_filter: bfloat16 [128, 512], P(None, 'tp'), may hold values from -0.5 to 0.5
- se_filter: bfloat16 [7, 8192], P(None, 'tp'), may hold values from -2 to 2
- gain: float32 [8192], P('tp'), may hold values from 0.1 to 1.9
Outputs:
- query_grad: bfloat16 [16384, 8192], P('ctx', 'tp')
- key_grad: bfloat16 [16384, 8192], P('ctx', 'tp')
- value_grad: bfloat16 [16384, 8192], P('ctx', 'tp')
- mr_filter_grad: float32 [128, 512], P(None, 'tp')
- se_filter_grad: float32 [7, 8192], P(None, 'tp')
- gain_grad: float32 [8192], P('tp')
All inputs are finite; a program needn't handle non-finite values.
Results may differ from a plain program's by a relative error of at most 0.0057.
Values may be sent and summed in bfloat16 or wider, within the bound.
No kernel may reach another device: no remote copies, remote signals or barrier semaphores. Data moves between devices by JAX's collectives and lax.ppermute only.
A program may use at most 128 MiB of HBM per device.

v0:
```python
import jax
import jax.numpy as jnp
from jax import lax
from jax.sharding import PartitionSpec as P

D = 8192
GROUP = 16
MR_LEN = 128
SE_LEN = 7


EPS = 1e-06


def shifted(x, axis, by):
    peers = lax.axis_size(axis)
    pairs = [(i, i + by) for i in range(peers) if 0 <= i + by < peers]
    return lax.ppermute(x, axis, pairs)


def filter_tables(mr_filter):
    row_ids = jnp.arange(MR_LEN)[:, None]
    col_ids = jnp.arange(MR_LEN)[None, :]
    index = (row_ids - col_ids) % MR_LEN
    spread = mr_filter.T[:, index]
    blank = jnp.zeros_like(spread)
    return (
        jnp.where(row_ids >= col_ids, spread, blank),
        jnp.where(row_ids < col_ids, spread, blank),
    )


def medium_conv(extended, present, earlier):
    count = extended.shape[0] - MR_LEN
    channels = extended.shape[1]
    blocks = extended.reshape(-1, MR_LEN, channels // GROUP, GROUP)
    result = jnp.einsum("grm,bmgi->brgi", present, blocks[1:], preferred_element_type=jnp.float32)
    result = result + jnp.einsum(
        "grm,bmgi->brgi", earlier, blocks[:-1], preferred_element_type=jnp.float32
    )
    return result.reshape(count, channels)


def medium_corr(extended, present, earlier):
    count = extended.shape[0] - MR_LEN
    channels = extended.shape[1]
    blocks = extended.reshape(-1, MR_LEN, channels // GROUP, GROUP)
    result = jnp.einsum("grm,brgi->bmgi", present, blocks[:-1], preferred_element_type=jnp.float32)
    result = result + jnp.einsum(
        "grm,brgi->bmgi", earlier, blocks[1:], preferred_element_type=jnp.float32
    )
    return result.reshape(count, channels)


def diagonal_sums(current, previous):
    groups = current.shape[0]
    front = jnp.pad(current.reshape(groups, MR_LEN * MR_LEN), ((0, 0), (MR_LEN, 0))).reshape(
        groups, MR_LEN, MR_LEN + 1
    )
    back = jnp.pad(previous.reshape(groups, MR_LEN * MR_LEN), ((0, 0), (0, MR_LEN))).reshape(
        groups, MR_LEN, MR_LEN + 1
    )
    sums = jnp.sum(front[:, :, 1:] + back[:, :, 1:], axis=1)
    return jnp.flip(sums, axis=1).T


def medium_filter_grad(grads, extended):
    channels = extended.shape[1]
    grad_blocks = grads.reshape(-1, MR_LEN, channels // GROUP, GROUP)
    blocks = extended.reshape(-1, MR_LEN, channels // GROUP, GROUP)
    current = jnp.einsum(
        "brgi,bmgi->grm", grad_blocks, blocks[1:], preferred_element_type=jnp.float32
    )
    previous = jnp.einsum(
        "brgi,bmgi->grm", grad_blocks, blocks[:-1], preferred_element_type=jnp.float32
    )
    row_ids = jnp.arange(MR_LEN)[:, None]
    col_ids = jnp.arange(MR_LEN)[None, :]
    current = jnp.where(row_ids >= col_ids, current, jnp.zeros_like(current))
    previous = jnp.where(row_ids < col_ids, previous, jnp.zeros_like(previous))
    return diagonal_sums(current, previous)


def short_conv(padded, se_filter, count):
    total = jnp.zeros((count, padded.shape[1]), jnp.float32)
    for tap in range(SE_LEN):
        start = SE_LEN - 1 - tap
        total = total + se_filter[tap].astype(jnp.float32) * padded[start : start + count].astype(
            jnp.float32
        )
    return total


def short_corr(padded, se_filter, count):
    total = jnp.zeros((count, padded.shape[1]), jnp.float32)
    for tap in range(SE_LEN):
        total = total + se_filter[tap].astype(jnp.float32) * padded[tap : tap + count]
    return total


def short_filter_grad(grads, padded):
    count = grads.shape[0]
    rows_out = []
    for tap in range(SE_LEN):
        start = SE_LEN - 1 - tap
        rows_out.append(jnp.sum(grads * padded[start : start + count].astype(jnp.float32), axis=0))
    return jnp.stack(rows_out)


def local(query, key_in, value_in, out_grad, mr_filter, se_filter, gain):
    tok_rows, channels = query.shape
    tail_rows = MR_LEN + SE_LEN - 2
    tokens_all = tok_rows * lax.axis_size("ctx")
    gated = (key_in.astype(jnp.float32) * value_in.astype(jnp.float32)).astype(jnp.bfloat16)
    key_tail, value_tail = shifted((key_in[-tail_rows:], value_in[-tail_rows:]), "ctx", 1)
    gated_prior = (key_tail.astype(jnp.float32) * value_tail.astype(jnp.float32)).astype(
        jnp.bfloat16
    )
    gated_wide = jnp.concatenate([gated_prior, gated])
    short_wide = short_conv(gated_wide, se_filter, tok_rows + MR_LEN - 1).astype(jnp.bfloat16)
    short_prior = short_wide[: MR_LEN - 1]
    short_mix = short_wide[MR_LEN - 1 :]
    gated_pad = jnp.concatenate([gated_prior[-(SE_LEN - 1) :], gated])
    short_ext = jnp.concatenate([jnp.zeros((1, channels), jnp.bfloat16), short_prior, short_mix])
    present, earlier = filter_tables(mr_filter)
    medium_mix = medium_conv(short_ext, present, earlier)
    query_wide = query.astype(jnp.float32)
    mixed = query_wide * medium_mix
    out_wide = out_grad.astype(jnp.float32)
    norm_grad = out_wide * gain
    square_sum, inner = lax.psum(
        (jnp.sum(mixed * mixed, axis=1), jnp.sum(norm_grad * mixed, axis=1)), "tp"
    )
    inv_rms = lax.rsqrt(square_sum / D + EPS)
    mixed_grad = inv_rms[:, None] * norm_grad - mixed * (inv_rms**3 * inner / D)[:, None]
    query_grad = (mixed_grad * medium_mix).astype(jnp.bfloat16)
    medium_grad = (mixed_grad * query_wide).astype(jnp.bfloat16)
    gain_local = jnp.sum(out_wide * mixed * inv_rms[:, None], axis=0)
    blank_row = jnp.zeros((1, channels), jnp.bfloat16)
    head_rows = shifted(medium_grad[: MR_LEN - 1], "ctx", -1)
    grad_ext = jnp.concatenate([medium_grad, head_rows, blank_row])
    short_grad = medium_corr(grad_ext, present, earlier)
    short_head = shifted(short_grad[: SE_LEN - 1].astype(jnp.bfloat16), "ctx", -1).astype(
        jnp.float32
    )
    short_pad = jnp.concatenate([short_grad, short_head])
    gated_grad = short_corr(short_pad, se_filter, tok_rows)
    key_grad = (gated_grad * value_in.astype(jnp.float32)).astype(jnp.bfloat16)
    value_grad = (gated_grad * key_in.astype(jnp.float32)).astype(jnp.bfloat16)
    se_local = short_filter_grad(short_grad, gated_pad)
    mr_local = medium_filter_grad(medium_grad, short_ext)
    mr_total, se_total, gain_total = lax.psum((mr_local, se_local, gain_local), "ctx")
    root_tokens = jnp.sqrt(jnp.float32(tokens_all))
    mr_filter_grad = mr_total / jnp.sqrt(jnp.float32(tokens_all * GROUP))
    return (
        query_grad,
        key_grad,
        value_grad,
        mr_filter_grad,
        se_total / root_tokens,
        gain_total / root_tokens,
    )


def solution(mesh):
    return jax.shard_map(
        local,
        mesh=mesh,
        in_specs=(
            P("ctx", "tp"),
            P("ctx", "tp"),
            P("ctx", "tp"),
            P("ctx", "tp"),
            P(None, "tp"),
            P(None, "tp"),
            P("tp"),
        ),
        out_specs=(
            P("ctx", "tp"),
            P("ctx", "tp"),
            P("ctx", "tp"),
            P(None, "tp"),
            P(None, "tp"),
            P("tp"),
        ),
        check_vma=False,
    )
```

profile of v0, /device:TPU:1, one launch (start us, length us, event | category | flops | bytes accessed | tf_op | source)
XLA Modules:
  0.0 576.1 jit_solution(15958738503211018791)
XLA Ops:
  7.3 2.1 slice.137
  9.4 4.5 collective-permute-start.1
  13.9 2.0 slice.136
  15.9 1.9 collective-permute-start
  18.0 1.3 copy.65
  21.1 2.3 copy.73
  23.3 57.4 %gather_fusion = bf16[16384,128]{1,0:T(8,128)(2,1)} fusion(bf16[128,128]{0,1:T(8,128)(2,1)S(1)} %bitcast.108, s32[16384]{0:T(1024)S(1)} %fusion.67), kind=kCustom, calls=%fused_computation | custom fusion | bytes 8454144 | tf_op jit(solution)/shard_map/gather | solution.py:25
  80.7 6.7 %copy.68 = bf16[128,128,128]{1,0,2:T(8,128)(2,1)} copy(bf16[128,128,128]{2,1,0:T(8,128)(2,1)} %bitcast.116) | data formatting | bytes 8388608 | tf_op jit(solution)/shard_map/gather | solution.py:25
  87.5 1.5 fusion.15
  89.0 2.5 multiply_convert_fusion
  91.5 1.4 copy.67
  92.9 7.7 %add_convert_fusion = bf16[383,2048]{0,1:T(8,128)(2,1)S(1)} fusion(bf16[133,2048]{0,1:T(8,128)(2,1)S(1)} %copy.67, bf16[256,2048]{0,1:T(8,128)(2,1)S(1)} %fusion.15, f32[2048]{0:T(1024)S(1)} %bitcast.130, f32[2048]{0:T(1024)S(1)} %bitcast.132, f32[2048]{0:T(1024)S(1)} %bitcast.122, f32[2048]{0:T(1024)S(1)} %bitcast.124, f32[2048]{0:T(1024)S(1)} %bitcast.126, ...), kind=kLoop, calls=%fused_computation.37 | loop fusion | flops 32944128 | bytes 3219456 | tf_op jit(solution)/shard_map/convert_element_type | solution.py:120
  100.6 1.8 fusion.78
  102.8 1.7 slice.154
  104.5 4.9 fusion.3
  109.4 2.3 add_bitcast_fusion.1
  111.7 1.1 copy.72
  113.2 8.7 %psum.35 = f32[256]{0:T(256)S(1)} all-reduce(f32[256]{0:T(256)S(1)} %multiply_reduce_fusion.7), channel_id=1, replica_groups=mesh['ctx'=64,'tp'=4] {'tp'}, use_global_device_ids=true, to_apply=%region_1.2 | all-reduce | flops 256 | bytes 2048 | tf_op jit(solution)/shard_map/psum | solution.py:131
  121.9 2.7 fusion.18
  124.6 6.2 %psum.36 = f32[256]{0:T(256)S(1)} all-reduce(f32[256]{0:T(256)S(1)} %get-tuple-element.25), channel_id=1, replica_groups=mesh['ctx'=64,'tp'=4] {'tp'}, use_global_device_ids=true, to_apply=%region_3.4 | all-reduce | flops 256 | bytes 2048 | tf_op jit(solution)/shard_map/psum | solution.py:131
  130.8 2.9 fusion.13
  135.5 1.3 slice.155
  136.9 4.5 bitcast_select_fusion.1
  141.4 4.6 bitcast_select_fusion
  146.0 7.0 %collective-permute-start.2 = (bf16[127,2048]{0,1:T(8,128)(2,1)}, bf16[127,2048]{0,1:T(8,128)(2,1)}, u32[]{:S(2)}, u32[]{:S(2)}) collective-permute-start(bf16[127,2048]{0,1:T(8,128)(2,1)} %slice.190), channel_id=1, source_target_pairs={{4,0},{8,4},{12,8},{16,12},{20,16},{24,20},{28,24},{32,28},{36,32}... | collective-permute-start | bytes 1560584 | tf_op jit(solution)/shard_map/ppermute | solution.py:18
  153.0 9.3 %copy.91 = f32[128,128,128]{0,2,1:T(8,128)} copy(f32[128,128,128]{2,1,0:T(8,128)} %bitcast_select_fusion.1) | data formatting | bytes 16777216 | tf_op jit(solution)/shard_map/reshape | solution.py:57
  162.3 7.7 %pad.9 = f32[128,16512]{0,1:T(8,128)} pad(f32[128,16384]{0,1:T(8,128)} %bitcast.110, f32[]{:T(128)} %constant.34.clone.1), padding=0_0x128_0 | pad | bytes 16842756 | tf_op jit(solution)/shard_map/jit(_pad)/pad | solution.py:57
  170.0 9.1 %reshape.102 = f32[128,128,129]{0,2,1:T(8,128)} reshape(f32[128,16512]{0,1:T(8,128)} %pad.9) | data formatting | bytes 16908288 | tf_op jit(solution)/shard_map/reshape | solution.py:57
  179.1 9.3 %copy.92 = f32[128,128,128]{0,2,1:T(8,128)} copy(f32[128,128,128]{2,1,0:T(8,128)} %bitcast_select_fusion) | data formatting | bytes 16777216 | tf_op jit(solution)/shard_map/reshape | solution.py:60
  188.4 7.7 %pad.10 = f32[128,16512]{0,1:T(8,128)} pad(f32[128,16384]{0,1:T(8,128)} %bitcast.109, f32[]{:T(128)} %constant.34.clone.1), padding=0_0x0_128 | pad | bytes 16842756 | tf_op jit(solution)/shard_map/jit(_pad)/pad | solution.py:60
  196.1 9.0 %reshape.104 = f32[128,128,129]{0,2,1:T(8,128)} reshape(f32[128,16512]{0,1:T(8,128)} %pad.10) | data formatting | bytes 16908288 | tf_op jit(solution)/shard_map/reshape | solution.py:60
  205.2 7.1 %fusion = f32[128,128]{0,1:T(8,128)S(1)} fusion(f32[128,128,129]{0,2,1:T(8,128)} %reshape.104, f32[128,128,129]{0,2,1:T(8,128)} %reshape.102), kind=kLoop, calls=%fused_computation.2 | loop fusion | flops 4177920 | bytes 16842752 | tf_op jit(solution)/shard_map/reduce_sum | solution.py:63
  215.0 1.4 copy.84
  216.4 164.9 %all-reduce.7.cloned.1.call-done = f32[128,128]{1,0:T(8,128)} async-done(((f32[128,128]{1,0:T(8,128)}), f32[128,128]{1,0:T(8,128)}) %all-reduce.7.cloned.1.call-update) | async-done | bytes 65552 | tf_op jit(solution)/shard_map/psum | solution.py:152
  381.3 1.5 broadcast_multiply_fusion.1
  382.8 1.3 fusion.56
  384.4 3.5 fusion.1
  387.9 1.2 add_bitcast_fusion
  391.3 2.7 collective-permute-start.3
  393.9 5.1 multiply_reduce_fusion
  399.8 2.4 collective-permute-done.3
  402.2 1.1 convert_element_type.130
  403.3 8.9 %fusion.14 = (bf16[256,2048]{0,1:T(8,128)(2,1)}, f32[256,2048]{0,1:T(8,128)S(1)}) fusion(bf16[256,2048]{0,1:T(8,128)(2,1)S(1)} %copy-done.12, f32[6,2048]{0,1:T(8,128)S(1)} %convert_element_type.130, f32[256,2048]{0,1:T(8,128)S(1)} %bitcast.118, f32[2048]{0:T(1024)S(1)} %bitcast.131, f32[2048]{0:T(1024)S(1)} %bitcast.133, f32[2048]{0:T(1024)S(1)} %bitcast.123, ...), kind=kLoop, calls=%fused_computation.55 | loop fusion | flops 11534336 | bytes 6397952 | tf_op jit(solution)/shard_map/convert_element_type | solution.py:149
  413.5 1.4 copy.86
  414.9 1.4 copy.85
  416.3 150.1 %all-reduce.9.cloned.1.call-done = (f32[7,2048]{1,0:T(8,128)}, f32[2048]{0:T(1024)}) async-done(((f32[7,2048]{1,0:T(8,128)}, f32[2048]{0:T(1024)}), (f32[7,2048]{1,0:T(8,128)}, f32[2048]{0:T(1024)})) %all-reduce.9.cloned.1.call-update) | async-done | bytes 65552 | tf_op jit(solution)/shard_map/psum | solution.py:152
  566.4 1.5 broadcast_multiply_fusion
  567.9 1.3 broadcast_multiply_fusion.2
  (75 shorter events, 11.5 us)
Async XLA Ops:
  7.2 16.2 %copy-start = (bf16[128,128]{1,0:T(8,128)(2,1)S(1)}, bf16[128,128]{1,0:T(8,128)(2,1)}, u32[]{:S(2)}) copy-start(bf16[128,128]{1,0:T(8,128)(2,1)} %param.11) | copy-start | bytes 98308
  7.2 12.1 %copy-start.18 = (bf16[256,2048]{1,0:T(8,128)(2,1)S(1)}, bf16[256,2048]{1,0:T(8,128)(2,1)}, u32[]{:S(2)}) copy-start(bf16[256,2048]{1,0:T(8,128)(2,1)} %param.9) | copy-start | bytes 3145732
  7.2 10.8 %copy-start.17 = (bf16[256,2048]{1,0:T(8,128)(2,1)S(1)}, bf16[256,2048]{1,0:T(8,128)(2,1)}, u32[]{:S(2)}) copy-start(bf16[256,2048]{1,0:T(8,128)(2,1)} %param.8) | copy-start | bytes 3145732
  7.2 10.7 %copy-start.21 = (bf16[7,2048]{1,0:T(8,128)(2,1)S(1)}, bf16[7,2048]{1,0:T(8,128)(2,1)}, u32[]{:S(2)}) copy-start(bf16[7,2048]{1,0:T(8,128)(2,1)} %param.12) | copy-start | bytes 86020
  7.2 374.1 %all-reduce.7.cloned.1.call-start = ((), (), s32[]{:S(2)}) async-start(), calls=%async_computation | async-start | bytes 131072 | tf_op jit(solution)/shard_map/psum | solution.py:152
  9.4 79.6 %collective-permute-start.1 = (bf16[133,2048]{1,0:T(8,128)(2,1)}, bf16[133,2048]{1,0:T(8,128)(2,1)}, u32[]{:S(2)}, u32[]{:S(2)}) collective-permute-start(bf16[133,2048]{1,0:T(8,128)(2,1)} %slice.137), channel_id=1, source_target_pairs={{0,4},{4,8},{8,12},{12,16},{16,20},{20,24},{24,28},{28,32},{32,36}... | collective-permute-start | bytes 1634312 | tf_op jit(solution)/shard_map/ppermute | solution.py:18
  15.9 73.1 %collective-permute-start = (bf16[133,2048]{1,0:T(8,128)(2,1)}, bf16[133,2048]{1,0:T(8,128)(2,1)}, u32[]{:S(2)}, u32[]{:S(2)}) collective-permute-start(bf16[133,2048]{1,0:T(8,128)(2,1)} %slice.136), channel_id=1, source_target_pairs={{0,4},{4,8},{8,12},{12,16},{16,20},{20,24},{24,28},{28,32},{32,36}... | collective-permute-start | bytes 1634312 | tf_op jit(solution)/shard_map/ppermute | solution.py:18
  19.3 1.2 copy-start.20
  20.5 66.9 %copy-start.10 = (bf16[256,2048]{0,1:T(8,128)(2,1)}, bf16[256,2048]{0,1:T(8,128)(2,1)S(1)}, u32[]{:S(2)}) copy-start(bf16[256,2048]{0,1:T(8,128)(2,1)S(1)} %copy.66) | copy-start | bytes 3145732
  89.0 11.7 %copy-start.6 = (bf16[256,2048]{0,1:T(8,128)(2,1)}, bf16[256,2048]{0,1:T(8,128)(2,1)S(1)}, u32[]{:S(2)}) copy-start(bf16[256,2048]{0,1:T(8,128)(2,1)S(1)} %fusion.15) | copy-start | bytes 3145732
  102.7 6.6 %copy-start.8 = (bf16[2,128,128,16]{1,0,3,2:T(2,128)(2,1)}, bf16[2,128,128,16]{1,0,3,2:T(2,128)(2,1)S(1)}, u32[]{:S(2)}) copy-start(bf16[2,128,128,16]{1,0,3,2:T(2,128)(2,1)S(1)} %slice.152) | copy-start | bytes 3145732
  104.5 4.9 copy-start.13
  104.5 4.9 copy-start.2
  112.8 9.1 %copy-start.22 = (f32[2048]{0:T(1024)S(1)}, f32[2048]{0:T(1024)}, u32[]{:S(2)}) copy-start(f32[2048]{0:T(1024)} %param.13) | copy-start | bytes 24580
  133.7 1.0 copy-start.4
  133.7 3.2 copy-start.9
  136.9 4.6 copy-start.14
  146.0 236.8 %collective-permute-start.2 = (bf16[127,2048]{0,1:T(8,128)(2,1)}, bf16[127,2048]{0,1:T(8,128)(2,1)}, u32[]{:S(2)}, u32[]{:S(2)}) collective-permute-start(bf16[127,2048]{0,1:T(8,128)(2,1)} %slice.190), channel_id=1, source_target_pairs={{4,0},{8,4},{12,8},{16,12},{20,16},{24,20},{28,24},{32,28},{36,32}... | collective-permute-start | bytes 1560584 | tf_op jit(solution)/shard_map/ppermute | solution.py:18
  205.2 9.8 %copy-start.15 = (bf16[256,2048]{0,1:T(8,128)(2,1)S(1)}, bf16[256,2048]{0,1:T(8,128)(2,1)}, u32[]{:S(2)}) copy-start(bf16[256,2048]{0,1:T(8,128)(2,1)} %get-tuple-element.38) | copy-start | bytes 3145732
  212.2 170.6 %copy-start.5 = (bf16[256,2048]{0,1:T(8,128)(2,1)S(1)}, bf16[256,2048]{0,1:T(8,128)(2,1)}, u32[]{:S(2)}) copy-start(bf16[256,2048]{0,1:T(8,128)(2,1)} %copy-done.4) | copy-start | bytes 3145732
  212.9 353.5 %all-reduce.9.cloned.1.call-start = ((), (), s32[]{:S(2)}) async-start(), calls=%async_computation.1 | async-start | bytes 147456 | tf_op jit(solution)/shard_map/psum | solution.py:152
  384.4 3.5 copy-start.3
  390.2 3.7 copy-start.7
  390.2 3.7 copy-start.19
  391.3 12.1 %copy-start.12 = (bf16[256,2048]{0,1:T(8,128)(2,1)S(1)}, bf16[256,2048]{0,1:T(8,128)(2,1)}, u32[]{:S(2)}) copy-start(bf16[256,2048]{0,1:T(8,128)(2,1)} %copy.65) | copy-start | bytes 3145732
  391.3 10.9 %collective-permute-start.3 = (bf16[6,2048]{0,1:T(8,128)(2,1)}, bf16[6,2048]{0,1:T(8,128)(2,1)}, u32[]{:S(2)}, u32[]{:S(2)}) collective-permute-start(bf16[6,2048]{0,1:T(8,128)(2,1)} %slice.377), channel_id=1, source_target_pairs={{4,0},{8,4},{12,8},{16,12},{20,16},{24,20},{28,24},{32,28},{36,32}... | collective-permute-start | bytes 73736 | tf_op jit(solution)/shard_map/ppermute | solution.py:18
  403.3 8.9 %copy-start.11 = (bf16[256,2048]{0,1:T(8,128)(2,1)S(1)}, bf16[256,2048]{0,1:T(8,128)(2,1)}, u32[]{:S(2)}) copy-start(bf16[256,2048]{0,1:T(8,128)(2,1)} %copy-done.10) | copy-start | bytes 3145732
  412.3 1.2 copy-start.16
  412.5 156.7 %copy-start.1 = (bf16[128,128]{1,0:T(8,128)(2,1)S(1)}, bf16[128,128]{1,0:T(8,128)(2,1)}, u32[]{:S(2)}) copy-start(bf16[128,128]{1,0:T(8,128)(2,1)} %param.11) | copy-start | bytes 98308
Sparse Core Ops, SparseCore 0:
  213.0 168.2 all-reduce.6
  399.9 166.4 all-reduce.8
where the time goes:
time: 578 us; the launch traced here: 576 us
  waiting for transfers between devices  317 us (55%)
  local copies, waits for them, and re-layouts  146 us (25%)
  other arithmetic  45.9 us (8%)
  matrix products  21 us (4%)
  starting transfers between devices  16.1 us (3%)
  blocking collectives  14.9 us (3%)
  between operations  14.4 us (2%)
    psum x2, waiting for transfers between devices, local(): lax.psum((mr_local, se_local, gain_local), 'ctx')  315 us
    gather x2, local copies, waits for them, and re-layouts, filter_tables(): spread = mr_filter.T[:, index]  64.1 us
    ppermute x4, starting transfers between devices, shifted(): return lax.ppermute(x, axis, pairs)  16 us
    psum x2, blocking collectives, local(): lax.psum((jnp.sum(mixed * mixed, axis=1), jnp.sum(norm_grad * mixed, axis...  14.9 us
    unnamed x54, local copies, waits for them, and re-layouts  11.7 us
  transfers between devices with their start and end apart: 6, of which 3 were waited for; matrix products, arithmetic and copies ran while one was open for 27% of the time, Pallas kernels for 0%

commit v1 on v0

v1 whole, which is shorter than its diff:
```python
import functools

import jax
import jax.numpy as jnp
from jax import lax
from jax.experimental import pallas as pl
from jax.experimental.pallas import tpu as pltpu
from jax.sharding import PartitionSpec as P

D = 8192
GROUP = 16
MR_LEN = 128
SE_LEN = 7
EPS = 1e-06

LANES = 128
HALO = 144
S = 32
W = S + MR_LEN
GT = LANES // GROUP
F32 = jnp.float32
BF16 = jnp.bfloat16


def params(limit=48):
    return pltpu.CompilerParams(vmem_limit_bytes=limit * 1024 * 1024)


def shifted(x, by):
    peers = lax.axis_size("ctx")
    return lax.ppermute(x, "ctx", [(i, i + by) for i in range(peers) if 0 <= i + by < peers])


def group_of_lane(rows):
    return lax.broadcasted_iota(jnp.int32, (rows, LANES), 1) // GROUP


def toeplitz(table, windows):
    results = []
    which = group_of_lane(S)
    for first in range(0, len(windows), 2):
        pair = windows[first : first + 2]
        rhs = jnp.concatenate(pair, axis=1) if len(pair) == 2 else pair[0]
        out = jnp.dot(table, rhs, preferred_element_type=F32)
        for n in range(len(pair)):
            total = out[:S, n * LANES : (n + 1) * LANES]
            for g in range(1, GT):
                part = out[g * S : (g + 1) * S, n * LANES : (n + 1) * LANES]
                total = jnp.where(which == g, part, total)
            results.append(total)
    return results


def table_kernel(front_ref, back_ref, front_out, back_out, scratch):
    for source, target in ((front_ref, front_out), (back_ref, back_out)):
        row = source[...]
        for s in range(S):
            turned = pltpu.roll(row, s, 1) if s else row
            for n in range(2):
                scratch[pl.ds(n * GT * S + s, GT, stride=S), :] = turned[:, n * LANES : (n + 1) * LANES]
        for n in range(2):
            at = slice(n * LANES, (n + 1) * LANES)
            target[:, at] = scratch[n * GT * S : (n + 1) * GT * S, :].astype(BF16)


def tables(front, back):
    groups = front.shape[0]
    tiles = groups // GT
    spec_in = pl.BlockSpec((GT, 2 * LANES), lambda i: (i, 0))
    spec_out = pl.BlockSpec((GT * S, 2 * LANES), lambda i: (i, 0))
    shape = jax.ShapeDtypeStruct((groups * S, 2 * LANES), BF16)
    return pl.pallas_call(
        table_kernel,
        grid=(tiles,),
        in_specs=[spec_in, spec_in],
        out_specs=[spec_out, spec_out],
        out_shape=[shape, shape],
        scratch_shapes=[pltpu.VMEM((2 * GT * S, LANES), F32)],
        compiler_params=params(),
        name="filter_tables",
    )(front, back)


def forward_kernel(
    halo_ref,
    key_ref,
    value_ref,
    query_ref,
    out_grad_ref,
    se_ref,
    gain_ref,
    table_ref,
    medium_out,
    short_out,
    sums_out,
    gated_ref,
    square_ref,
    inner_ref,
):
    tok = key_ref.shape[0]
    step = pl.program_id(0)
    gated_ref[:HALO, :] = halo_ref[...].astype(F32)
    gated = (key_ref[...].astype(F32) * value_ref[...].astype(F32)).astype(BF16)
    gated_ref[HALO:, :] = gated.astype(F32)
    rows = tok + MR_LEN
    base = HALO - MR_LEN
    short = jnp.zeros((rows, LANES), F32)
    for tap in range(SE_LEN):
        short = short + se_ref[tap : tap + 1, :] * gated_ref[base - tap : base - tap + rows, :]
    short_out[...] = short.astype(BF16)
    table = table_ref[:, :W]
    windows = [short_out[S * b : S * b + W, :] for b in range(tok // S)]
    parts = toeplitz(table, windows)
    gain = gain_ref[...]

    @pl.when(step == 0)
    def _():
        square_ref[...] = jnp.zeros_like(square_ref)
        inner_ref[...] = jnp.zeros_like(inner_ref)

    for b, medium in enumerate(parts):
        at = slice(S * b, S * b + S)
        medium_out[at, :] = medium
        mixed = query_ref[at, :].astype(F32) * medium
        norm_grad = out_grad_ref[at, :].astype(F32) * gain
        square_ref[at, :] += mixed * mixed
        inner_ref[at, :] += norm_grad * mixed

    @pl.when(step == pl.num_programs(0) - 1)
    def _():
        square = jnp.sum(square_ref[...].T, axis=0, keepdims=True)
        inner = jnp.sum(inner_ref[...].T, axis=0, keepdims=True)
        sums_out[0:1, :] = square
        sums_out[1:2, :] = inner


def forward(halo, key_in, value_in, query, out_grad, se, gain, table):
    tok, channels = key_in.shape
    tiles = channels // LANES
    col = lambda rows: pl.BlockSpec((rows, LANES), lambda i: (0, i))
    return pl.pallas_call(
        forward_kernel,
        grid=(tiles,),
        in_specs=[
            col(HALO),
            col(tok),
            col(tok),
            col(tok),
            col(tok),
            col(8),
            col(1),
            pl.BlockSpec((GT * S, 2 * LANES), lambda i: (i, 0)),
        ],
        out_specs=[col(tok), col(tok + MR_LEN), pl.BlockSpec((2, tok), lambda i: (0, 0))],
        out_shape=[
            jax.ShapeDtypeStruct((tok, channels), F32),
            jax.ShapeDtypeStruct((tok + MR_LEN, channels), BF16),
            jax.ShapeDtypeStruct((2, tok), F32),
        ],
        scratch_shapes=[
            pltpu.VMEM((HALO + tok, LANES), F32),
            pltpu.VMEM((tok, LANES), F32),
            pltpu.VMEM((tok, LANES), F32),
        ],
        compiler_params=params(),
        name="forward",
    )(halo, key_in, value_in, query, out_grad, se, gain, table)


def spread_sums(sums, scale_ref, slope_ref, rows):
    square = jnp.broadcast_to(sums[0:1, :], (LANES, sums.shape[1])).T[:rows]
    inner = jnp.broadcast_to(sums[1:2, :], (LANES, sums.shape[1])).T[:rows]
    inv = lax.rsqrt(square / D + EPS)
    scale_ref[...] = inv
    slope_ref[...] = inv * inv * inv * inner / D


def head_kernel(sums_ref, query_ref, out_grad_ref, medium_ref, gain_ref, head_out, scale_ref, slope_ref):
    @pl.when(pl.program_id(0) == 0)
    def _():
        spread_sums(sums_ref[...], scale_ref, slope_ref, HALO)

    for n in range(query_ref.shape[1] // LANES):
        at = slice(n * LANES, (n + 1) * LANES)
        query = query_ref[:, at].astype(F32)
        norm_grad = out_grad_ref[:, at].astype(F32) * gain_ref[:, at]
        mixed = query * medium_ref[:, at]
        mixed_grad = scale_ref[...] * norm_grad - mixed * slope_ref[...]
        head_out[:, at] = (mixed_grad * query).astype(BF16)


def head(sums, query, out_grad, medium, gain):
    tok, channels = query.shape
    width = 512
    col = lambda rows: pl.BlockSpec((rows, width), lambda i: (0, i))
    return pl.pallas_call(
        head_kernel,
        grid=(channels // width,),
        in_specs=[pl.BlockSpec((2, tok), lambda i: (0, 0)), col(HALO), col(HALO), col(HALO), col(1)],
        out_specs=col(HALO),
        out_shape=jax.ShapeDtypeStruct((HALO, channels), BF16),
        scratch_shapes=[pltpu.VMEM((HALO, LANES), F32), pltpu.VMEM((HALO, LANES), F32)],
        compiler_params=params(),
        name="head_rows",
    )(sums, query, out_grad, medium, gain)


def wide_kernel(halo_ref, key_ref, value_ref, table_ref, wide_out, gated_ref):
    tok = key_ref.shape[0]
    lead = W - HALO
    gated_ref[:lead, :] = jnp.zeros((lead, LANES), BF16)
    gated_ref[lead:W, :] = halo_ref[...]
    gated_ref[W:, :] = (key_ref[...].astype(F32) * value_ref[...].astype(F32)).astype(BF16)
    windows = [gated_ref[S * b : S * b + W, :] for b in range(tok // S + 1)]
    for b, part in enumerate(toeplitz(table_ref[:, :W], windows)):
        wide_out[S * b : S * b + S, :] = part


def wide(halo, key_in, value_in, table):
    tok, channels = key_in.shape
    col = lambda rows: pl.BlockSpec((rows, LANES), lambda i: (0, i))
    return pl.pallas_call(
        wide_kernel,
        grid=(channels // LANES,),
        in_specs=[col(HALO), col(tok), col(tok), pl.BlockSpec((GT * S, 2 * LANES), lambda i: (i, 0))],
        out_specs=col(tok + S),
        out_shape=jax.ShapeDtypeStruct((tok + S, channels), F32),
        scratch_shapes=[pltpu.VMEM((W + tok, LANES), BF16)],
        compiler_params=params(),
        name="wide_gated",
    )(halo, key_in, value_in, table)


def grads_kernel(
    sums_ref,
    query_ref,
    out_grad_ref,
    medium_ref,
    gain_ref,
    short_ref,
    wide_ref,
    query_grad_out,
    medium_grad_out,
    packed_out,
    scale_ref,
    slope_ref,
    cross_ref,
):
    tok = query_ref.shape[0]

    @pl.when(pl.program_id(0) == 0)
    def _():
        spread_sums(sums_ref[...], scale_ref, slope_ref, tok)

    query = query_ref[...].astype(F32)
    out_grad = out_grad_ref[...].astype(F32)
    medium = medium_ref[...]
    inv = scale_ref[...]
    norm_grad = out_grad * gain_ref[...]
    mixed = query * medium
    mixed_grad = inv * norm_grad - mixed * slope_ref[...]
    query_grad_out[...] = (mixed_grad * medium).astype(BF16)
    medium_grad = (mixed_grad * query).astype(BF16)
    medium_grad_out[...] = medium_grad
    gain_row = jnp.sum(out_grad * mixed * inv, axis=0, keepdims=True)
    wide_grad = medium_grad.astype(F32)
    for tap in range(SE_LEN):
        packed_out[GT + tap : GT + tap + 1, :] = jnp.sum(
            wide_grad * wide_ref[S - tap : S - tap + tok, :], axis=0, keepdims=True
        )
    packed_out[GT + SE_LEN : GT + SE_LEN + 1, :] = gain_row
    blocks = tok // S
    lhs_rows = jnp.concatenate([medium_grad[S * b : S * b + S, :] for b in range(blocks)], axis=1)
    which = lax.broadcasted_iota(jnp.int32, lhs_rows.shape, 1) % LANES // GROUP
    lhs = jnp.concatenate(
        [jnp.where(which == g, lhs_rows, jnp.zeros_like(lhs_rows)) for g in range(GT)], axis=0
    )
    rhs = jnp.concatenate([short_ref[S * b : S * b + W, :] for b in range(blocks)], axis=1)
    cross = lax.dot_general(lhs, rhs, (((1,), (1,)), ((), ())), preferred_element_type=F32)
    cross_ref[: GT * S, :] = cross[:, :LANES]
    cross_ref[GT * S :, :S] = cross[:, LANES:]
    total = jnp.zeros((GT, 2 * LANES), F32)
    for s in range(S):
        part = jnp.concatenate(
            [cross_ref[pl.ds(n * GT * S + s, GT, stride=S), :] for n in range(2)], axis=1
        )
        total = total + pltpu.roll(part, 2 * LANES - 1 - s, 1)
    packed_out[:GT, :] = total[:, :LANES]


def grads(sums, query, out_grad, medium, gain, short, wide_rows):
    tok, channels = query.shape
    tiles = channels // LANES
    col = lambda rows: pl.BlockSpec((rows, LANES), lambda i: (0, i))
    return pl.pallas_call(
        grads_kernel,
        grid=(tiles,),
        in_specs=[
            pl.BlockSpec((2, tok), lambda i: (0, 0)),
            col(tok),
            col(tok),
            col(tok),
            col(1),
            col(tok + MR_LEN),
            col(tok + S),
        ],
        out_specs=[col(tok), col(tok), pl.BlockSpec((2 * GT, LANES), lambda i: (i, 0))],
        out_shape=[
            jax.ShapeDtypeStruct((tok, channels), BF16),
            jax.ShapeDtypeStruct((tok, channels), BF16),
            jax.ShapeDtypeStruct((2 * GT * tiles, LANES), F32),
        ],
        scratch_shapes=[
            pltpu.VMEM((tok, LANES), F32),
            pltpu.VMEM((tok, LANES), F32),
            pltpu.VMEM((2 * GT * S, LANES), F32),
        ],
        compiler_params=params(),
        name="gradients",
    )(sums, query, out_grad, medium, gain, short, wide_rows)


def backward_kernel(
    grad_ref, halo_ref, se_ref, key_ref, value_ref, table_ref, key_out, value_out, ext_ref, short_ref
):
    tok = key_ref.shape[0]
    ext_ref[:tok, :] = grad_ref[...]
    ext_ref[tok : tok + HALO, :] = halo_ref[...]
    ext_ref[tok + HALO :, :] = jnp.zeros((W - HALO, LANES), BF16)
    windows = [ext_ref[S * b : S * b + W, :] for b in range(tok // S + 1)]
    for b, part in enumerate(toeplitz(table_ref[:, :W], windows)):
        short_ref[S * b : S * b + S, :] = part
    total = jnp.zeros((tok, LANES), F32)
    for tap in range(SE_LEN):
        total = total + se_ref[tap : tap + 1, :] * short_ref[tap : tap + tok, :]
    key_out[...] = (total * value_ref[...].astype(F32)).astype(BF16)
    value_out[...] = (total * key_ref[...].astype(F32)).astype(BF16)


def backward(medium_grad, halo, se, key_in, value_in, table):
    tok, channels = key_in.shape
    col = lambda rows: pl.BlockSpec((rows, LANES), lambda i: (0, i))
    shape = jax.ShapeDtypeStruct((tok, channels), BF16)
    return pl.pallas_call(
        backward_kernel,
        grid=(channels // LANES,),
        in_specs=[
            col(tok),
            col(HALO),
            col(8),
            col(tok),
            col(tok),
            pl.BlockSpec((GT * S, 2 * LANES), lambda i: (i, 0)),
        ],
        out_specs=[col(tok), col(tok)],
        out_shape=[shape, shape],
        scratch_shapes=[pltpu.VMEM((tok + W, LANES), BF16), pltpu.VMEM((tok + S, LANES), F32)],
        compiler_params=params(),
        name="backward",
    )(medium_grad, halo, se, key_in, value_in, table)


def finish_kernel(tokens, packed_ref, mr_out, se_out, gain_out):
    tiles = packed_ref.shape[0] // (2 * GT)
    rows = jnp.concatenate([packed_ref[2 * GT * i : 2 * GT * i + GT, :] for i in range(tiles)], axis=0)
    row_ids = lax.broadcasted_iota(jnp.int32, (MR_LEN, MR_LEN), 0)
    col_ids = lax.broadcasted_iota(jnp.int32, (MR_LEN, MR_LEN), 1)
    flip = jnp.where(row_ids + col_ids == MR_LEN - 1, 1.0, 0.0).astype(F32)
    mr_out[...] = lax.dot_general(
        flip, rows, (((1,), (1,)), ((), ())), preferred_element_type=F32, precision=lax.Precision.HIGHEST
    ) * (1.0 / (tokens * GROUP) ** 0.5)
    for i in range(tiles):
        at = slice(i * LANES, (i + 1) * LANES)
        low = 2 * GT * i + GT
        se_out[:, at] = packed_ref[low : low + SE_LEN, :] * (1.0 / tokens**0.5)
        gain_out[:, at] = packed_ref[low + SE_LEN : low + SE_LEN + 1, :] * (1.0 / tokens**0.5)


def finish(packed, tokens, channels):
    return pl.pallas_call(
        functools.partial(finish_kernel, tokens),
        out_shape=[
            jax.ShapeDtypeStruct((MR_LEN, channels // GROUP), F32),
            jax.ShapeDtypeStruct((SE_LEN, channels), F32),
            jax.ShapeDtypeStruct((1, channels), F32),
        ],
        compiler_params=params(),
        name="finish",
    )(packed)


def sum_over_ctx(packed):
    peers = lax.axis_size("ctx")
    parts = packed.reshape(peers, packed.shape[0] // peers, packed.shape[1])
    mine = jnp.sum(lax.all_to_all(parts, "ctx", 0, 0), axis=0)
    everyone = lax.all_to_all(jnp.broadcast_to(mine[None], parts.shape), "ctx", 0, 0)
    return everyone.reshape(packed.shape)


def local(query, key_in, value_in, out_grad, mr_filter, se_filter, gain):
    tok, channels = query.shape
    tokens_all = tok * lax.axis_size("ctx")
    tail = (key_in[-HALO:].astype(F32) * value_in[-HALO:].astype(F32)).astype(BF16)
    gated_halo = shifted(tail, 1)
    taps = mr_filter.astype(F32).T
    front = jnp.pad(jnp.flip(taps, axis=1), ((0, 0), (1, LANES - 1)))
    back = jnp.pad(taps, ((0, 0), (0, LANES)))
    front_table, back_table = tables(front, back)
    se = jnp.pad(se_filter.astype(F32), ((0, 1), (0, 0)))
    gain_row = gain[None, :]
    medium, short, sums = forward(
        gated_halo, key_in, value_in, query, out_grad, se, gain_row, front_table
    )
    sums = lax.psum(sums, "tp")
    wide_rows = wide(gated_halo, key_in, value_in, front_table)
    head_rows = head(sums, query, out_grad, medium, gain_row)
    grad_halo = shifted(head_rows, -1)
    query_grad, medium_grad, packed = grads(
        sums, query, out_grad, medium, gain_row, short, wide_rows
    )
    packed = sum_over_ctx(packed)
    key_grad, value_grad = backward(medium_grad, grad_halo, se, key_in, value_in, back_table)
    mr_grad, se_grad, gain_grad = finish(packed, tokens_all, channels)
    return query_grad, key_grad, value_grad, mr_grad, se_grad, gain_grad[0]


def solution(mesh):
    return jax.shard_map(
        local,
        mesh=mesh,
        in_specs=(
            P("ctx", "tp"),
            P("ctx", "tp"),
            P("ctx", "tp"),
            P("ctx", "tp"),
            P(None, "tp"),
            P(None, "tp"),
            P("tp"),
        ),
        out_specs=(
            P("ctx", "tp"),
            P("ctx", "tp"),
            P("ctx", "tp"),
            P(None, "tp"),
            P(None, "tp"),
            P("tp"),
        ),
        check_vma=False,
    )
```

time: 578 us -> 133 us (0.23)
  waiting for transfers between devices: 317 us -> 0.01 us
  local copies, waits for them, and re-layouts: 146 us -> 14.7 us
  Pallas kernels: 0 us -> 59.1 us
  other arithmetic: 45.9 us -> 2.44 us
  blocking collectives: 14.9 us -> 46.7 us
  matrix products: 21 us -> 0 us
  between operations: 14.4 us -> 0.79 us
  starting transfers between devices: 16.1 us -> 7.45 us
    psum x2 -> x0, waiting for transfers between devices: 315 us -> none  [local(): lax.psum((mr_local, se_local, gain_local), 'ctx')]
    gather x2 -> x0, local copies, waits for them, and re-layouts: 64.1 us -> none  [filter_tables(): spread = mr_filter.T[:, index]]
    pallas_call x0 -> x7, Pallas kernels: none -> 59.1 us  [the longest x1 14.5 us: grads(): pl.pallas_call(grads_kernel, grid=(tiles,), in_specs=[pl.BlockSpec((2, to...]
    all_to_all x0 -> x2, blocking collectives: none -> 38 us  [the longest x1 23.1 us: sum_over_ctx(): mine = jnp.sum(lax.all_to_all(parts, 'ctx', 0, 0), axis=0)]
    reshape x4 -> x0, local copies, waits for them, and re-layouts: 36.8 us -> none  [the longest x1 9.32 us: diagonal_sums(): current.reshape(groups, MR_LEN * MR_LEN)]
    convert_element_type x7 -> x1, other arithmetic: 24.9 us -> 2.34 us  [local(): (key_in[-HALO:].astype(F32) * value_in[-HALO:].astype(F32)).astype(BF16)]
    dot_general x6 -> x0, matrix products: 21 us -> none  [the longest x1 4.87 us: medium_conv(): jnp.einsum('grm,bmgi->brgi', earlier, blocks[:-1], preferred_element_type...]
    pad x2, local copies, waits for them, and re-layouts: 15.4 us -> 0.11 us  [the longest x1 0.09 us: local(): front = jnp.pad(jnp.flip(taps, axis=1), ((0, 0), (1, LANES - 1)))]
  transfers between devices with their start and end apart: 6 -> 2, of which waited for: 3 -> 0; matrix products, arithmetic and copies ran while one was open for 27% -> 1% of each run, Pallas kernels for 0% -> 25%
where the time goes in v1:
time: 133 us; the launch traced here: 131 us
  Pallas kernels  59.1 us (44%)
  blocking collectives  46.7 us (35%)
  local copies, waits for them, and re-layouts  14.7 us (11%)
  starting transfers between devices  7.45 us (6%)
  other arithmetic  2.44 us (2%)
    all_to_all x1, blocking collectives, sum_over_ctx(): mine = jnp.sum(lax.all_to_all(parts, 'ctx', 0, 0), axis=0)  23.1 us
    all_to_all x1, blocking collectives, sum_over_ctx(): lax.all_to_all(jnp.broadcast_to(mine[None], parts.shape), 'ctx', 0, 0)  14.9 us
    pallas_call x1, Pallas kernels, grads(): pl.pallas_call(grads_kernel, grid=(tiles,), in_specs=[pl.BlockSpec((2, to...  14.5 us
    unnamed x41, local copies, waits for them, and re-layouts  14.5 us
    pallas_call x1, Pallas kernels, forward(): pl.pallas_call(forward_kernel, grid=(tiles,), in_specs=[col(HALO), col(to...  13.1 us
    pallas_call x1, Pallas kernels, backward(): pl.pallas_call(backward_kernel, grid=(channels // LANES,), in_specs=[col(...  10.8 us
    pallas_call x1, Pallas kernels, wide(): pl.pallas_call(wide_kernel, grid=(channels // LANES,), in_specs=[col(HALO...  8.99 us
    pallas_call x1, Pallas kernels, tables(): pl.pallas_call(table_kernel, grid=(tiles,), in_specs=[spec_in, spec_in],...  8.8 us
  transfers between devices with their start and end apart: 2, of which 0 were waited for; matrix products, arithmetic and copies ran while one was open for 1% of the time, Pallas kernels for 25%

profile of v1, /device:TPU:1, one launch (start us, length us, event | category | flops | bytes accessed | tf_op | source)
XLA Modules:
  0.0 131.1 jit_solution(17230067326746677585)
XLA Ops:
  0.6 0.0 copy-start
  0.6 0.0 copy-start.1
  0.7 0.0 copy-start.19
  0.7 0.0 copy-start.18
  0.7 2.3 %multiply_convert_fusion = bf16[144,2048]{1,0:T(8,128)(2,1)} fusion(bf16[256,2048]{1,0:T(8,128)(2,1)} %value_ref.5, bf16[256,2048]{1,0:T(8,128)(2,1)} %key_ref.5), kind=kLoop, calls=%fused_computation | loop fusion | flops 1179648 | bytes 1769472 | tf_op jit(solution)/shard_map/convert_element_type | solution.py:403
  3.0 4.5 %collective-permute-start = (bf16[144,2048]{1,0:T(8,128)(2,1)}, bf16[144,2048]{1,0:T(8,128)(2,1)S(1)}, u32[]{:S(2)}, u32[]{:S(2)}) collective-permute-start(bf16[144,2048]{1,0:T(8,128)(2,1)} %multiply_convert_fusion), channel_id=1, source_target_pairs={{0,4},{4,8},{8,12},{12,16},{16,20},{20,24},{24,28},{28,32},{32,36}... | collective-permute-start | bytes 1769480 | tf_op jit(solution)/shard_map/ppermute | solution.py:31
  7.5 0.9 copy.13
  8.4 0.1 rev.4
  8.5 0.1 pad.16.front_ref
  8.6 8.8 %filter_tables.1 = (bf16[4096,256]{1,0:T(8,128)(2,1)S(1)}, bf16[4096,256]{1,0:T(8,128)(2,1)S(1)}) custom-call(f32[128,256]{1,0:T(8,128)S(1)} %pad.16.front_ref, f32[128,256]{1,0:T(8,128)S(1)} %pad.17.back_ref), custom_call_target="tpu_custom_call" | custom-call | tf_op jit(solution)/shard_map/filter_tables/pallas_call | solution.py:72
  17.4 0.0 copy-start.7
  17.4 1.3 %copy-done.7 = bf16[4096,256]{1,0:T(8,128)(2,1)} copy-done((bf16[4096,256]{1,0:T(8,128)(2,1)}, bf16[4096,256]{1,0:T(8,128)(2,1)S(1)}, u32[]{:S(2)}) %copy-start.7) | copy-done | bytes 2097176
  18.8 0.0 copy-start.13
  18.8 1.3 %copy-done.13 = bf16[4096,256]{1,0:T(8,128)(2,1)} copy-done((bf16[4096,256]{1,0:T(8,128)(2,1)}, bf16[4096,256]{1,0:T(8,128)(2,1)S(1)}, u32[]{:S(2)}) %copy-start.13) | copy-done | bytes 2097176
  20.1 0.0 copy-done.19
  20.1 0.0 collective-permute-done.halo_ref
  20.1 0.0 copy-start.10
  20.1 0.8 copy-done.10
  20.9 0.0 copy-done
  20.9 0.0 copy-done.1
  20.9 0.0 copy-done.18
  20.9 1.2 copy-done.2
  22.2 0.0 copy-start.4
  22.2 1.2 copy-done.4
  23.4 0.0 copy-start.11
  23.4 1.1 copy-done.11
  24.5 13.1 %forward.1 = (f32[256,2048]{1,0:T(8,128)}, bf16[384,2048]{1,0:T(8,128)(2,1)}, f32[2,256]{1,0:T(2,128)S(1)}) custom-call(bf16[144,2048]{1,0:T(8,128)(2,1)S(1)} %copy-done.11, bf16[256,2048]{1,0:T(8,128)(2,1)S(1)} %copy-done.1, bf16[256,2048]{1,0:T(8,128)(2,1)S(1)} %copy-done, bf16[256,2048]{1,0:T(8,128)(2,1)S(1)} %copy-done.2, ...), custom_call_target="tpu_custom_call" | custom-call | tf_op jit(solution)/shard_map/forward/pallas_call | solution.py:141
  37.6 8.7 %psum.7.sums_ref = f32[2,256]{1,0:T(2,128)S(1)} all-reduce(f32[2,256]{1,0:T(2,128)S(1)} %get-tuple-element.20), channel_id=1, replica_groups=mesh['ctx'=64,'tp'=4] {'tp'}, use_global_device_ids=true, to_apply=%region_0.1 | all-reduce | flops 512 | bytes 4096 | tf_op jit(solution)/shard_map/psum | solution.py:414
  46.3 0.0 copy-done.3
  46.3 1.2 copy-done.5
  47.5 1.6 %copy-done.9 = f32[256,2048]{1,0:T(8,128)S(1)} copy-done((f32[256,2048]{1,0:T(8,128)S(1)}, f32[256,2048]{1,0:T(8,128)}, u32[]{:S(2)}) %copy-start.9) | copy-done | bytes 2097176
  49.1 1.9 %head_rows.1 = bf16[144,2048]{1,0:T(8,128)(2,1)} custom-call(f32[2,256]{1,0:T(2,128)S(1)} %psum.7.sums_ref, bf16[256,2048]{1,0:T(8,128)(2,1)S(1)} %copy-done.3, bf16[256,2048]{1,0:T(8,128)(2,1)S(1)} %copy-done.5, f32[256,2048]{1,0:T(8,128)S(1)} %copy-done.9, f32[1,2048]{1,0:T(1,128)S(1)} %bitcast.9), custom_call_target="tpu_custom_call" | custom-call | tf_op jit(solution)/shard_map/head_rows/pallas_call | solution.py:196
  51.1 3.0 %collective-permute-start.1 = (bf16[144,2048]{1,0:T(8,128)(2,1)}, bf16[144,2048]{1,0:T(8,128)(2,1)}, u32[]{:S(2)}, u32[]{:S(2)}) collective-permute-start(bf16[144,2048]{1,0:T(8,128)(2,1)} %head_rows.1), channel_id=1, source_target_pairs={{4,0},{8,4},{12,8},{16,12},{20,16},{24,20},{28,24},{32,28},{36,32}... | collective-permute-start | bytes 1769480 | tf_op jit(solution)/shard_map/ppermute | solution.py:31
  54.0 0.0 copy-done.8
  54.0 0.0 copy-done.12
  54.0 9.0 %wide_gated.1.wide_ref = f32[288,2048]{1,0:T(8,128)} custom-call(bf16[144,2048]{1,0:T(8,128)(2,1)S(1)} %copy-done.12, bf16[256,2048]{1,0:T(8,128)(2,1)S(1)} %copy-done.1, bf16[256,2048]{1,0:T(8,128)(2,1)S(1)} %copy-done, bf16[4096,256]{1,0:T(8,128)(2,1)S(1)} %copy-done.8), custom_call_target="tpu_custom_call" | custom-call | tf_op jit(solution)/shard_map/wide_gated/pallas_call | solution.py:222
  63.0 0.0 copy-done.6
  63.0 0.0 copy-done.15
  63.0 14.5 %gradients.1 = (bf16[256,2048]{1,0:T(8,128)(2,1)}, bf16[256,2048]{1,0:T(8,128)(2,1)S(1)}, f32[256,128]{1,0:T(8,128)S(1)}) custom-call(f32[2,256]{1,0:T(2,128)S(1)} %psum.7.sums_ref, bf16[256,2048]{1,0:T(8,128)(2,1)S(1)} %copy-done.3, bf16[256,2048]{1,0:T(8,128)(2,1)S(1)} %copy-done.6, f32[256,2048]{1,0:T(8,128)} %get-tuple-element.21.medium_ref, ...), custom_call_target="tpu_custom_call" | custom-call | tf_op jit(solution)/shard_map/gradients/pallas_call | solution.py:295
  77.5 1.0 copy-done.16
  78.5 23.1 %all_to_all.10 = f32[64,4,128]{2,1,0:T(4,128)S(1)} all-to-all(f32[64,4,128]{2,1,0:T(4,128)S(1)} %bitcast.7), channel_id=1, replica_groups=mesh['ctx'=64,'tp'=4] {'ctx'}, dimensions={0} | all-to-all | bytes 262144 | tf_op jit(solution)/shard_map/all_to_all | solution.py:395
  101.6 0.1 reduce_sum.9
  101.7 14.9 %all_to_all.11 = f32[64,4,128]{2,1,0:T(4,128)S(1)} all-to-all(f32[64,4,128]{2,1,0:T(4,128)S(1)} %broadcast_in_dim.10), channel_id=1, replica_groups=mesh['ctx'=64,'tp'=4] {'ctx'}, dimensions={0} | all-to-all | bytes 262144 | tf_op jit(solution)/shard_map/all_to_all | solution.py:396
  116.6 0.9 finish.1
  117.5 0.0 collective-permute-done.1.halo_ref
  117.5 1.6 %copy-done.14 = bf16[4096,256]{1,0:T(8,128)(2,1)S(1)} copy-done((bf16[4096,256]{1,0:T(8,128)(2,1)S(1)}, bf16[4096,256]{1,0:T(8,128)(2,1)}, u32[]{:S(2)}) %copy-start.14) | copy-done | bytes 2097176
  119.1 1.2 copy-done.17
  120.3 10.8 %backward.1 = (bf16[256,2048]{1,0:T(8,128)(2,1)}, bf16[256,2048]{1,0:T(8,128)(2,1)}) custom-call(bf16[256,2048]{1,0:T(8,128)(2,1)S(1)} %copy-done.17, bf16[144,2048]{1,0:T(8,128)(2,1)} %collective-permute-done.1.halo_ref, f32[8,2048]{1,0:T(8,128)S(1)} %pad_convert_fusion.se_ref, bf16[256,2048]{1,0:T(8,128)(2,1)S(1)} %copy-done.1, ...), custom_call_target="tpu_custom_call" | custom-call | tf_op jit(solution)/shard_map/backward/pallas_call | solution.py:344
  (15 shorter events, 0.1 us)
Async XLA Ops:
  0.6 20.3 %copy-start = (bf16[256,2048]{1,0:T(8,128)(2,1)S(1)}, bf16[256,2048]{1,0:T(8,128)(2,1)}, u32[]{:S(2)}) copy-start(bf16[256,2048]{1,0:T(8,128)(2,1)} %value_ref.5) | copy-start | bytes 3145732
  0.6 20.3 %copy-start.1 = (bf16[256,2048]{1,0:T(8,128)(2,1)S(1)}, bf16[256,2048]{1,0:T(8,128)(2,1)}, u32[]{:S(2)}) copy-start(bf16[256,2048]{1,0:T(8,128)(2,1)} %key_ref.5) | copy-start | bytes 3145732
  0.7 19.4 %copy-start.19 = (bf16[7,2048]{1,0:T(8,128)(2,1)S(1)}, bf16[7,2048]{1,0:T(8,128)(2,1)}, u32[]{:S(2)}) copy-start(bf16[7,2048]{1,0:T(8,128)(2,1)} %param.12) | copy-start | bytes 86020
  0.7 20.3 %copy-start.18 = (f32[2048]{0:T(1024)S(1)}, f32[2048]{0:T(1024)}, u32[]{:S(2)}) copy-start(f32[2048]{0:T(1024)} %param.13) | copy-start | bytes 24580
  3.0 17.1 %collective-permute-start = (bf16[144,2048]{1,0:T(8,128)(2,1)}, bf16[144,2048]{1,0:T(8,128)(2,1)S(1)}, u32[]{:S(2)}, u32[]{:S(2)}) collective-permute-start(bf16[144,2048]{1,0:T(8,128)(2,1)} %multiply_convert_fusion), channel_id=1, source_target_pairs={{0,4},{4,8},{8,12},{12,16},{16,20},{20,24},{24,28},{28,32},{32,36}... | collective-permute-start | bytes 1769480 | tf_op jit(solution)/shard_map/ppermute | solution.py:31
  17.4 1.3 %copy-start.7 = (bf16[4096,256]{1,0:T(8,128)(2,1)}, bf16[4096,256]{1,0:T(8,128)(2,1)S(1)}, u32[]{:S(2)}) copy-start(bf16[4096,256]{1,0:T(8,128)(2,1)S(1)} %get-tuple-element.19.table_ref) | copy-start | bytes 6291460
  18.8 1.3 %copy-start.13 = (bf16[4096,256]{1,0:T(8,128)(2,1)}, bf16[4096,256]{1,0:T(8,128)(2,1)S(1)}, u32[]{:S(2)}) copy-start(bf16[4096,256]{1,0:T(8,128)(2,1)S(1)} %get-tuple-element.25.table_ref) | copy-start | bytes 6291460
  20.1 0.8 copy-start.10
  20.9 1.2 copy-start.2
  22.2 1.2 copy-start.4
  23.4 1.1 copy-start.11
  24.5 21.9 %copy-start.3 = (bf16[256,2048]{1,0:T(8,128)(2,1)S(1)}, bf16[256,2048]{1,0:T(8,128)(2,1)}, u32[]{:S(2)}) copy-start(bf16[256,2048]{1,0:T(8,128)(2,1)} %query_ref.5) | copy-start | bytes 3145732
  46.3 1.2 copy-start.5
  47.5 1.6 %copy-start.9 = (f32[256,2048]{1,0:T(8,128)S(1)}, f32[256,2048]{1,0:T(8,128)}, u32[]{:S(2)}) copy-start(f32[256,2048]{1,0:T(8,128)} %get-tuple-element.21.medium_ref) | copy-start | bytes 6291460
  49.1 4.9 %copy-start.8 = (bf16[4096,256]{1,0:T(8,128)(2,1)S(1)}, bf16[4096,256]{1,0:T(8,128)(2,1)}, u32[]{:S(2)}) copy-start(bf16[4096,256]{1,0:T(8,128)(2,1)} %copy-done.7) | copy-start | bytes 6291460
  49.1 4.9 %copy-start.12 = (bf16[144,2048]{1,0:T(8,128)(2,1)S(1)}, bf16[144,2048]{1,0:T(8,128)(2,1)}, u32[]{:S(2)}) copy-start(bf16[144,2048]{1,0:T(8,128)(2,1)} %copy-done.10) | copy-start | bytes 1769476
  51.0 12.0 %copy-start.6 = (bf16[256,2048]{1,0:T(8,128)(2,1)S(1)}, bf16[256,2048]{1,0:T(8,128)(2,1)}, u32[]{:S(2)}) copy-start(bf16[256,2048]{1,0:T(8,128)(2,1)} %out_grad_ref.5) | copy-start | bytes 3145732
  51.0 12.0 %copy-start.15 = (bf16[384,2048]{1,0:T(8,128)(2,1)S(1)}, bf16[384,2048]{1,0:T(8,128)(2,1)}, u32[]{:S(2)}) copy-start(bf16[384,2048]{1,0:T(8,128)(2,1)} %get-tuple-element.22.short_ref) | copy-start | bytes 4718596
  51.1 66.5 %collective-permute-start.1 = (bf16[144,2048]{1,0:T(8,128)(2,1)}, bf16[144,2048]{1,0:T(8,128)(2,1)}, u32[]{:S(2)}, u32[]{:S(2)}) collective-permute-start(bf16[144,2048]{1,0:T(8,128)(2,1)} %head_rows.1), channel_id=1, source_target_pairs={{4,0},{8,4},{12,8},{16,12},{20,16},{24,20},{28,24},{32,28},{36,32}... | collective-permute-start | bytes 1769480 | tf_op jit(solution)/shard_map/ppermute | solution.py:31
  77.5 1.0 copy-start.16
  117.5 1.6 %copy-start.14 = (bf16[4096,256]{1,0:T(8,128)(2,1)S(1)}, bf16[4096,256]{1,0:T(8,128)(2,1)}, u32[]{:S(2)}) copy-start(bf16[4096,256]{1,0:T(8,128)(2,1)} %copy-done.13) | copy-start | bytes 6291460
  119.1 1.2 copy-start.17

commit v2 on v0

v2 whole, which is shorter than its diff:
```python
import functools

import jax
import jax.numpy as jnp
from jax import lax
from jax.experimental import pallas as pl
from jax.experimental.pallas import tpu as pltpu
from jax.sharding import PartitionSpec as P

D = 8192
GROUP = 16
MR_LEN = 128
SE_LEN = 7
EPS = 1e-06

LANES = 128
HALO = 144
S = 32
W = S + MR_LEN
GT = LANES // GROUP
EARLY = S + MR_LEN
F32 = jnp.float32
BF16 = jnp.bfloat16


UNROLL = 4
VMEM = pl.BlockSpec(memory_space=pltpu.VMEM)


def params(limit=24):
    return pltpu.CompilerParams(vmem_limit_bytes=limit * 1024 * 1024)


def each_tile(channels, body):
    def step(i, carry):
        for slot in range(UNROLL):
            tile = i * UNROLL + slot
            body(pl.ds(pl.multiple_of(tile * LANES, LANES), LANES), tile, slot)
        return carry

    lax.fori_loop(0, channels // LANES // UNROLL, step, 0)


def of_tile(tile, rows):
    return pl.ds(pl.multiple_of(tile * rows, rows), rows)


def call(body, name, outs, scratch, *args):
    return pl.pallas_call(
        body,
        in_specs=[VMEM] * len(args),
        out_specs=[VMEM] * len(outs),
        out_shape=[jax.ShapeDtypeStruct(shape, dtype) for shape, dtype in outs],
        scratch_shapes=scratch,
        compiler_params=params(),
        name=name,
    )(*args)


def shifted(x, by):
    peers = lax.axis_size("ctx")
    return lax.ppermute(x, "ctx", [(i, i + by) for i in range(peers) if 0 <= i + by < peers])


def group_of_lane(rows):
    return lax.broadcasted_iota(jnp.int32, (rows, LANES), 1) // GROUP


def toeplitz(table, windows):
    results = []
    which = group_of_lane(S)
    for first in range(0, len(windows), 2):
        pair = windows[first : first + 2]
        rhs = jnp.concatenate(pair, axis=1) if len(pair) == 2 else pair[0]
        out = jnp.dot(table, rhs, preferred_element_type=F32)
        for n in range(len(pair)):
            total = out[:S, n * LANES : (n + 1) * LANES]
            for g in range(1, GT):
                part = out[g * S : (g + 1) * S, n * LANES : (n + 1) * LANES]
                total = jnp.where(which == g, part, total)
            results.append(total)
    return results


def table_kernel(front_ref, back_ref, front_out, back_out):
    def one(g, carry):
        for source, target in ((front_ref, front_out), (back_ref, back_out)):
            rows = source[of_tile(g, GT), :]
            for k in range(GT):
                row = jnp.broadcast_to(rows[k : k + 1, :], (S, 2 * LANES))
                turned = pltpu.roll(row, 0, 1, stride=1, stride_axis=0).astype(BF16)
                target[of_tile(g * GT + k, S), :] = turned
        return carry

    lax.fori_loop(0, front_ref.shape[0] // GT, one, 0)


def tables(front, back):
    shape = ((front.shape[0] * S, 2 * LANES), BF16)
    return call(table_kernel, "filter_tables", [shape, shape], [], front, back)


def short_filter(se_ref, at, gated_ref, first, rows):
    total = jnp.zeros((rows, LANES), F32)
    for tap in range(SE_LEN):
        total = total + se_ref[tap : tap + 1, at] * gated_ref[first - tap : first - tap + rows, :]
    return total.astype(BF16)


def gate(key_ref, value_ref, rows, at):
    return (key_ref[rows, at].astype(F32) * value_ref[rows, at].astype(F32)).astype(BF16)


def early_kernel(
    key_ref,
    value_ref,
    query_ref,
    out_grad_ref,
    se_ref,
    gain_ref,
    table_ref,
    medium_out,
    short_out,
    wide_out,
    square_out,
    inner_out,
    gated_ref,
):
    tok, channels = key_ref.shape
    square_out[...] = jnp.zeros_like(square_out)
    inner_out[...] = jnp.zeros_like(inner_out)

    def body(at, tile, slot):
        wide_ref = gated_ref.at[slot]
        gated = gate(key_ref, value_ref, slice(None), at)
        wide_ref[...] = gated.astype(F32)
        short_out[:S, at] = jnp.zeros((S, LANES), BF16)
        short_out[S:, at] = short_filter(se_ref, at, wide_ref, S, tok - S)
        short_out[16:S, at] = short_filter(se_ref, at, wide_ref, 16, S - 16)
        table = table_ref[of_tile(tile, GT * S), :W]
        first = [t for t in range(EARLY, tok, S)]
        windows = [short_out[t - MR_LEN : t + S, at] for t in first]
        also = [t for t in range(MR_LEN, tok, S)]
        windows += [gated[t - MR_LEN : t + S, :] for t in also]
        parts = toeplitz(table, windows)
        gain = gain_ref[:, at]
        for t, medium in zip(first, parts):
            down = slice(t - EARLY, t - EARLY + S)
            medium_out[down, at] = medium
            mixed = query_ref[t : t + S, at].astype(F32) * medium
            norm_grad = out_grad_ref[t : t + S, at].astype(F32) * gain
            square_out[down, :] += mixed * mixed
            inner_out[down, :] += norm_grad * mixed
        for t, part in zip(also, parts[len(first) :]):
            wide_out[t - MR_LEN : t - MR_LEN + S, at] = part

    each_tile(channels, body)


def early(key_in, value_in, query, out_grad, se, gain, table):
    tok, channels = key_in.shape
    outs = [
        ((tok - EARLY, channels), F32),
        ((tok, channels), BF16),
        ((tok - MR_LEN, channels), F32),
        ((tok - EARLY, LANES), F32),
        ((tok - EARLY, LANES), F32),
    ]
    scratch = [pltpu.VMEM((UNROLL, tok, LANES), F32)]
    return call(early_kernel, "early", outs, scratch, key_in, value_in, query, out_grad, se, gain, table)


def window(low_ref, high_ref, b, at):
    if b * S >= EARLY:
        return high_ref[b * S - MR_LEN : b * S + S, at]
    if b == 0:
        return low_ref[:, at]
    return jnp.concatenate([low_ref[S * b :, at], high_ref[S : S * b + S, at]], axis=0)


def late_kernel(
    halo_ref,
    key_ref,
    value_ref,
    query_ref,
    out_grad_ref,
    se_ref,
    gain_ref,
    table_ref,
    high_ref,
    square_in,
    inner_in,
    medium_out,
    low_out,
    sums_out,
    gated_ref,
    square_ref,
    inner_ref,
):
    channels = key_ref.shape[1]
    square_ref[:EARLY, :] = jnp.zeros((EARLY, LANES), F32)
    inner_ref[:EARLY, :] = jnp.zeros((EARLY, LANES), F32)
    square_ref[EARLY:, :] = square_in[...]
    inner_ref[EARLY:, :] = inner_in[...]

    def body(at, tile, slot):
        rows = gated_ref.at[slot]
        rows[:HALO, :] = halo_ref[:, at].astype(F32)
        rows[HALO:, :] = gate(key_ref, value_ref, slice(0, S), at).astype(F32)
        low_out[:, at] = short_filter(se_ref, at, rows, HALO - MR_LEN, MR_LEN + S)
        table = table_ref[of_tile(tile, GT * S), :W]
        windows = [window(low_out, high_ref, b, at) for b in range(EARLY // S)]
        gain = gain_ref[:, at]
        for b, medium in enumerate(toeplitz(table, windows)):
            down = slice(S * b, S * b + S)
            medium_out[down, at] = medium
            mixed = query_ref[down, at].astype(F32) * medium
            norm_grad = out_grad_ref[down, at].astype(F32) * gain
            square_ref[down, :] += mixed * mixed
            inner_ref[down, :] += norm_grad * mixed

    each_tile(channels, body)
    sums_out[0:1, :] = jnp.sum(square_ref[...].T, axis=0, keepdims=True)
    sums_out[1:2, :] = jnp.sum(inner_ref[...].T, axis=0, keepdims=True)


def late(halo, key_in, value_in, query, out_grad, se, gain, table, short_high, square, inner):
    tok, channels = key_in.shape
    outs = [((EARLY, channels), F32), ((MR_LEN + S, channels), BF16), ((2, tok), F32)]
    scratch = [
        pltpu.VMEM((UNROLL, HALO + S, LANES), F32),
        pltpu.VMEM((tok, LANES), F32),
        pltpu.VMEM((tok, LANES), F32),
    ]
    return call(
        late_kernel,
        "late",
        outs,
        scratch,
        halo,
        key_in,
        value_in,
        query,
        out_grad,
        se,
        gain,
        table,
        short_high,
        square,
        inner,
    )


def spread_sums(parts, scale_ref, slope_ref, rows):
    sums = functools.reduce(jnp.add, [part[...] for part in parts])
    square = jnp.broadcast_to(sums[0:1, :], (LANES, sums.shape[1])).T[:rows]
    inner = jnp.broadcast_to(sums[1:2, :], (LANES, sums.shape[1])).T[:rows]
    inv = lax.rsqrt(square / D + EPS)
    scale_ref[...] = inv
    slope_ref[...] = inv * inv * inv * inner / D


def head_kernel(query_ref, out_grad_ref, medium_ref, gain_ref, *rest):
    sums, (head_out, scale_ref, slope_ref) = rest[:-3], rest[-3:]
    spread_sums(sums, scale_ref, slope_ref, HALO)

    def body(at, tile, slot):
        query = query_ref[:HALO, at].astype(F32)
        norm_grad = out_grad_ref[:HALO, at].astype(F32) * gain_ref[:, at]
        mixed = query * medium_ref[:HALO, at]
        mixed_grad = scale_ref[...] * norm_grad - mixed * slope_ref[...]
        head_out[:, at] = (mixed_grad * query).astype(BF16)

    each_tile(query_ref.shape[1], body)


def head(sums, query, out_grad, medium_low, gain):
    outs = [((HALO, query.shape[1]), BF16)]
    scratch = [pltpu.VMEM((HALO, LANES), F32), pltpu.VMEM((HALO, LANES), F32)]
    return call(head_kernel, "head_rows", outs, scratch, query, out_grad, medium_low, gain, *sums)[0]


def wide_kernel(halo_ref, key_ref, value_ref, table_ref, wide_out, gated_ref):
    lead = W - HALO

    def body(at, tile, slot):
        rows = gated_ref.at[slot]
        rows[:lead, :] = jnp.zeros((lead, LANES), BF16)
        rows[lead:W, :] = halo_ref[:, at]
        rows[W:, :] = gate(key_ref, value_ref, slice(0, MR_LEN), at)
        windows = [rows[S * b : S * b + W, :] for b in range(MR_LEN // S + 1)]
        for b, part in enumerate(toeplitz(table_ref[of_tile(tile, GT * S), :W], windows)):
            wide_out[S * b : S * b + S, at] = part

    each_tile(key_ref.shape[1], body)


def wide(halo, key_in, value_in, table):
    outs = [((MR_LEN + S, key_in.shape[1]), F32)]
    scratch = [pltpu.VMEM((UNROLL, W + MR_LEN, LANES), BF16)]
    return call(wide_kernel, "wide_gated", outs, scratch, halo, key_in, value_in, table)[0]


def grads_kernel(
    query_ref,
    out_grad_ref,
    medium_low_ref,
    medium_high_ref,
    gain_ref,
    short_low_ref,
    short_high_ref,
    wide_low_ref,
    wide_high_ref,
    *rest,
):
    query_grad_out, medium_grad_out, packed_out, scale_ref, slope_ref, cross_ref, wide_ref = rest[-7:]
    tok, channels = query_ref.shape
    spread_sums(rest[:-7], scale_ref, slope_ref, tok)
    blocks = tok // S
    side = GT * S

    def body(at, tile, slot):
        query = query_ref[:, at].astype(F32)
        out_grad = out_grad_ref[:, at].astype(F32)
        medium = jnp.concatenate([medium_low_ref[:, at], medium_high_ref[:, at]], axis=0)
        inv = scale_ref[...]
        norm_grad = out_grad * gain_ref[:, at]
        mixed = query * medium
        mixed_grad = inv * norm_grad - mixed * slope_ref[...]
        query_grad_out[:, at] = (mixed_grad * medium).astype(BF16)
        medium_grad = (mixed_grad * query).astype(BF16)
        medium_grad_out[:, at] = medium_grad
        gain_row = jnp.sum(out_grad * mixed * inv, axis=0, keepdims=True)
        wide_grad = medium_grad.astype(F32)
        rows = wide_ref.at[slot]
        rows[: MR_LEN + S, :] = wide_low_ref[:, at]
        rows[MR_LEN + S :, :] = wide_high_ref[:, at]
        lines = [
            jnp.sum(wide_grad * rows[S - tap : S - tap + tok, :], axis=0, keepdims=True)
            for tap in range(SE_LEN)
        ]
        lhs_rows = jnp.concatenate([medium_grad[S * b : S * b + S, :] for b in range(blocks)], axis=1)
        which = lax.broadcasted_iota(jnp.int32, lhs_rows.shape, 1) % LANES // GROUP
        lhs = jnp.concatenate(
            [jnp.where(which == g, lhs_rows, jnp.zeros_like(lhs_rows)) for g in range(GT)], axis=0
        )
        rhs = jnp.concatenate(
            [window(short_low_ref, short_high_ref, b, at) for b in range(blocks)], axis=1
        )
        cross = lax.dot_general(lhs, rhs, (((1,), (1,)), ((), ())), preferred_element_type=F32)
        held = cross_ref.at[slot]
        held[:side, :] = cross[:, :LANES]
        held[side:, :S] = cross[:, LANES:]
        total = jnp.zeros((GT, 2 * LANES), F32)
        for s in range(S):
            part = jnp.concatenate(
                [held[pl.ds(m * side + s, GT, stride=S), :] for m in range(2)], axis=1
            )
            total = total + pltpu.roll(part, 2 * LANES - 1 - s, 1)
        packed_out[of_tile(tile, 2 * GT), :] = jnp.concatenate(
            [total[:, :LANES]] + lines + [gain_row], axis=0
        )

    each_tile(channels, body)


def grads(sums, query, out_grad, medium_low, medium_high, gain, short_low, short_high, wide_low, wide_high):
    tok, channels = query.shape
    outs = [
        ((tok, channels), BF16),
        ((tok, channels), BF16),
        ((2 * GT * channels // LANES, LANES), F32),
    ]
    scratch = [
        pltpu.VMEM((tok, LANES), F32),
        pltpu.VMEM((tok, LANES), F32),
        pltpu.VMEM((UNROLL, 2 * GT * S, LANES), F32),
        pltpu.VMEM((UNROLL, tok + S, LANES), F32),
    ]
    return call(
        grads_kernel,
        "gradients",
        outs,
        scratch,
        query,
        out_grad,
        medium_low,
        medium_high,
        gain,
        short_low,
        short_high,
        wide_low,
        wide_high,
        *sums,
    )


def backward_kernel(
    grad_ref, halo_ref, se_ref, key_ref, value_ref, table_ref, key_out, value_out, ext_ref, short_ref
):
    tok = key_ref.shape[0]

    def body(at, tile, slot):
        ext = ext_ref.at[slot]
        short = short_ref.at[slot]
        ext[:tok, :] = grad_ref[:, at]
        ext[tok : tok + HALO, :] = halo_ref[:, at]
        ext[tok + HALO :, :] = jnp.zeros((W - HALO, LANES), BF16)
        windows = [ext[S * b : S * b + W, :] for b in range(tok // S + 1)]
        for b, part in enumerate(toeplitz(table_ref[of_tile(tile, GT * S), :W], windows)):
            short[S * b : S * b + S, :] = part
        total = jnp.zeros((tok, LANES), F32)
        for tap in range(SE_LEN):
            total = total + se_ref[tap : tap + 1, at] * short[tap : tap + tok, :]
        key_out[:, at] = (total * value_ref[:, at].astype(F32)).astype(BF16)
        value_out[:, at] = (total * key_ref[:, at].astype(F32)).astype(BF16)

    each_tile(key_ref.shape[1], body)


def backward(medium_grad, halo, se, key_in, value_in, table):
    tok, channels = key_in.shape
    outs = [((tok, channels), BF16), ((tok, channels), BF16)]
    scratch = [
        pltpu.VMEM((UNROLL, tok + W, LANES), BF16),
        pltpu.VMEM((UNROLL, tok + S, LANES), F32),
    ]
    return call(backward_kernel, "backward", outs, scratch, medium_grad, halo, se, key_in, value_in, table)


def finish_kernel(tokens, packed_ref, mr_out, se_out, gain_out):
    tiles = packed_ref.shape[0] // (2 * GT)
    rows = jnp.concatenate([packed_ref[2 * GT * i : 2 * GT * i + GT, :] for i in range(tiles)], axis=0)
    row_ids = lax.broadcasted_iota(jnp.int32, (MR_LEN, MR_LEN), 0)
    col_ids = lax.broadcasted_iota(jnp.int32, (MR_LEN, MR_LEN), 1)
    flip = jnp.where(row_ids + col_ids == MR_LEN - 1, 1.0, 0.0).astype(F32)
    mr_out[...] = lax.dot_general(
        flip, rows, (((1,), (1,)), ((), ())), preferred_element_type=F32, precision=lax.Precision.HIGHEST
    ) * (1.0 / (tokens * GROUP) ** 0.5)
    for i in range(tiles):
        at = slice(i * LANES, (i + 1) * LANES)
        low = 2 * GT * i + GT
        se_out[:, at] = packed_ref[low : low + SE_LEN, :] * (1.0 / tokens**0.5)
        gain_out[:, at] = packed_ref[low + SE_LEN : low + SE_LEN + 1, :] * (1.0 / tokens**0.5)


def finish(packed, tokens, channels):
    return pl.pallas_call(
        functools.partial(finish_kernel, tokens),
        out_shape=[
            jax.ShapeDtypeStruct((MR_LEN, channels // GROUP), F32),
            jax.ShapeDtypeStruct((SE_LEN, channels), F32),
            jax.ShapeDtypeStruct((1, channels), F32),
        ],
        compiler_params=params(),
        name="finish",
    )(packed)


def from_peers(x, axis):
    peers = lax.axis_size(axis)
    return [lax.ppermute(x, axis, [(i, (i + k) % peers) for i in range(peers)]) for k in range(1, peers)]


def sum_over_ctx(packed, beside):
    peers = lax.axis_size("ctx")
    parts = packed.reshape(peers, packed.shape[0] // peers, packed.shape[1])
    arrived, other = lax.optimization_barrier((lax.all_to_all(parts, "ctx", 0, 0), beside()))
    mine = jnp.sum(arrived, axis=0)
    everyone = lax.all_to_all(jnp.broadcast_to(mine[None], parts.shape), "ctx", 0, 0)
    return everyone.reshape(packed.shape), other


def local(query, key_in, value_in, out_grad, mr_filter, se_filter, gain):
    tok, channels = query.shape
    tokens_all = tok * lax.axis_size("ctx")
    tail = (key_in[-HALO:].astype(F32) * value_in[-HALO:].astype(F32)).astype(BF16)
    gated_halo = shifted(tail, 1)
    taps = mr_filter.astype(F32).T
    front = jnp.pad(jnp.flip(taps, axis=1), ((0, 0), (1, LANES - 1)))
    back = jnp.pad(taps, ((0, 0), (0, LANES)))
    front_table, back_table = tables(front, back)
    se = jnp.pad(se_filter.astype(F32), ((0, 1), (0, 0)))
    gain_row = gain[None, :]
    medium_high, short_high, wide_high, square, inner = early(
        key_in, value_in, query, out_grad, se, gain_row, front_table
    )
    medium_low, short_low, sums = late(
        gated_halo,
        key_in,
        value_in,
        query,
        out_grad,
        se,
        gain_row,
        front_table,
        short_high,
        square,
        inner,
    )
    sums = [sums] + from_peers(sums, "tp")
    wide_low = wide(gated_halo, key_in, value_in, front_table)
    sums, wide_low = lax.optimization_barrier((sums, wide_low))
    head_rows = head(sums, query, out_grad, medium_low, gain_row)
    grad_halo = shifted(head_rows, -1)
    query_grad, medium_grad, packed = grads(
        sums,
        query,
        out_grad,
        medium_low,
        medium_high,
        gain_row,
        short_low,
        short_high,
        wide_low,
        wide_high,
    )
    packed, (key_grad, value_grad) = sum_over_ctx(
        packed, lambda: backward(medium_grad, grad_halo, se, key_in, value_in, back_table)
    )
    mr_grad, se_grad, gain_grad = finish(packed, tokens_all, channels)
    return query_grad, key_grad, value_grad, mr_grad, se_grad, gain_grad[0]


def solution(mesh):
    return jax.shard_map(
        local,
        mesh=mesh,
        in_specs=(
            P("ctx", "tp"),
            P("ctx", "tp"),
            P("ctx", "tp"),
            P("ctx", "tp"),
            P(None, "tp"),
            P(None, "tp"),
            P("tp"),
        ),
        out_specs=(
            P("ctx", "tp"),
            P("ctx", "tp"),
            P("ctx", "tp"),
            P(None, "tp"),
            P(None, "tp"),
            P("tp"),
        ),
        check_vma=False,
    )
```

time: 578 us -> 85.8 us (0.15)
  waiting for transfers between devices: 317 us -> 2.75 us
  local copies, waits for them, and re-layouts: 146 us -> 8.64 us
  other arithmetic: 45.9 us -> 2.44 us
  Pallas kernels: 0 us -> 27.8 us
  matrix products: 21 us -> 0 us
  between operations: 14.4 us -> 0.86 us
  starting transfers between devices: 16.1 us -> 24.5 us
    psum x2 -> x0, waiting for transfers between devices: 315 us -> none  [local(): lax.psum((mr_local, se_local, gain_local), 'ctx')]
    gather x2 -> x0, local copies, waits for them, and re-layouts: 64.1 us -> none  [filter_tables(): spread = mr_filter.T[:, index]]
    reshape x4 -> x0, local copies, waits for them, and re-layouts: 36.8 us -> none  [the longest x1 9.32 us: diagonal_sums(): current.reshape(groups, MR_LEN * MR_LEN)]
    pallas_call x0 -> x8, Pallas kernels: none -> 27.8 us  [the longest x7 26.9 us: call(): pl.pallas_call(body, in_specs=[VMEM] * len(args), out_specs=[VMEM] * len(...]
    convert_element_type x7 -> x1, other arithmetic: 24.9 us -> 2.34 us  [local(): (key_in[-HALO:].astype(F32) * value_in[-HALO:].astype(F32)).astype(BF16)]
    dot_general x6 -> x0, matrix products: 21 us -> none  [the longest x1 4.87 us: medium_conv(): jnp.einsum('grm,bmgi->brgi', earlier, blocks[:-1], preferred_element_type...]
    all_to_all x0 -> x1, blocking collectives: none -> 18.5 us  [sum_over_ctx(): lax.all_to_all(jnp.broadcast_to(mine[None], parts.shape), 'ctx', 0, 0)]
    pad x2, local copies, waits for them, and re-layouts: 15.4 us -> 0.11 us  [the longest x1 0.09 us: local(): front = jnp.pad(jnp.flip(taps, axis=1), ((0, 0), (1, LANES - 1)))]
  transfers between devices with their start and end apart: 6 -> 6, of which waited for: 3 -> 1; matrix products, arithmetic and copies ran while one was open for 27% -> 1% of each run, Pallas kernels for 0% -> 27%
where the time goes in v2:
time: 85.8 us; the launch traced here: 85.4 us
  Pallas kernels  27.8 us (32%)
  starting transfers between devices  24.5 us (29%)
  blocking collectives  18.5 us (22%)
  local copies, waits for them, and re-layouts  8.64 us (10%)
  waiting for transfers between devices  2.75 us (3%)
  other arithmetic  2.44 us (3%)
  between operations  0.86 us (1%)
    pallas_call x7, Pallas kernels, call(): pl.pallas_call(body, in_specs=[VMEM] * len(args), out_specs=[VMEM] * len(...  26.9 us
    all_to_all x1, blocking collectives, sum_over_ctx(): lax.all_to_all(jnp.broadcast_to(mine[None], parts.shape), 'ctx', 0, 0)  18.5 us
    all_to_all x1, starting transfers between devices, sum_over_ctx(): lax.all_to_all(parts, 'ctx', 0, 0)  13 us
    unnamed x21, local copies, waits for them, and re-layouts  8.43 us
    ppermute x2, starting transfers between devices, shifted(): lax.ppermute(x, 'ctx', [(i, i + by) for i in range(peers) if 0 <= i + by...  6.42 us
    ppermute x3, starting transfers between devices, from_peers(): lax.ppermute(x, axis, [(i, (i + k) % peers) for i in range(peers)])  5.06 us
    all_to_all x1, waiting for transfers between devices, sum_over_ctx(): lax.all_to_all(parts, 'ctx', 0, 0)  2.74 us
    convert_element_type x1, other arithmetic, local(): (key_in[-HALO:].astype(F32) * value_in[-HALO:].astype(F32)).astype(BF16)  2.34 us
  transfers between devices with their start and end apart: 6, of which 1 were waited for; matrix products, arithmetic and copies ran while one was open for 1% of the time, Pallas kernels for 27%

profile of v2, /device:TPU:1, one launch (start us, length us, event | category | flops | bytes accessed | tf_op | source)
XLA Modules:
  0.0 85.4 jit_solution(13359216439292275327)
XLA Ops:
  0.6 0.0 copy-start
  0.6 0.0 copy-start.1
  0.7 0.0 copy-start.9
  0.7 0.0 copy-start.8
  0.7 2.3 %multiply_convert_fusion = bf16[144,2048]{1,0:T(8,128)(2,1)} fusion(bf16[256,2048]{1,0:T(8,128)(2,1)} %value_ref.7, bf16[256,2048]{1,0:T(8,128)(2,1)} %key_ref.7), kind=kLoop, calls=%fused_computation | loop fusion | flops 1179648 | bytes 1769472 | tf_op jit(solution)/shard_map/convert_element_type | solution.py:477
  3.0 4.5 %collective-permute-start = (bf16[144,2048]{1,0:T(8,128)(2,1)}, bf16[144,2048]{1,0:T(8,128)(2,1)S(1)}, u32[]{:S(2)}, u32[]{:S(2)}) collective-permute-start(bf16[144,2048]{1,0:T(8,128)(2,1)} %multiply_convert_fusion), channel_id=1, source_target_pairs={{0,4},{4,8},{8,12},{12,16},{16,20},{20,24},{24,28},{28,32},{32,36}... | collective-permute-start | bytes 1769480 | tf_op jit(solution)/shard_map/ppermute | solution.py:62
  7.5 0.9 %copy.13 = bf16[128,128]{0,1:T(8,128)(2,1)S(1)} copy(bf16[128,128]{1,0:T(8,128)(2,1)} %param.11) | data formatting | bytes 65536 | tf_op args[4]
  8.4 0.1 rev.4
  8.5 0.1 pad.16.front_ref
  8.6 2.2 %filter_tables.1 = (bf16[4096,256]{1,0:T(8,128)(2,1)S(1)}, bf16[4096,256]{1,0:T(8,128)(2,1)S(1)}) custom-call(f32[128,256]{1,0:T(8,128)S(1)} %pad.16.front_ref, f32[128,256]{1,0:T(8,128)S(1)} %pad.17.back_ref), custom_call_target="tpu_custom_call" | custom-call | tf_op jit(solution)/shard_map/filter_tables/pallas_call | solution.py:49
  10.9 0.0 copy-start.4
  10.9 1.3 %copy-done.4 = bf16[4096,256]{1,0:T(8,128)(2,1)} copy-done((bf16[4096,256]{1,0:T(8,128)(2,1)}, bf16[4096,256]{1,0:T(8,128)(2,1)S(1)}, u32[]{:S(2)}) %copy-start.4) | copy-done | bytes 2097176
  12.2 0.0 copy-done.9
  12.2 0.0 copy-done
  12.2 0.0 copy-done.1
  12.2 0.0 copy-done.8
  12.2 0.0 copy-start.2
  12.2 1.2 %copy-done.2 = bf16[256,2048]{1,0:T(8,128)(2,1)S(1)} copy-done((bf16[256,2048]{1,0:T(8,128)(2,1)S(1)}, bf16[256,2048]{1,0:T(8,128)(2,1)}, u32[]{:S(2)}) %copy-start.2) | copy-done | bytes 1048600
  13.5 0.0 copy-start.3
  13.5 1.2 %copy-done.3 = bf16[256,2048]{1,0:T(8,128)(2,1)S(1)} copy-done((bf16[256,2048]{1,0:T(8,128)(2,1)S(1)}, bf16[256,2048]{1,0:T(8,128)(2,1)}, u32[]{:S(2)}) %copy-start.3) | copy-done | bytes 1048600
  14.7 4.5 %early.1 = (f32[96,2048]{1,0:T(8,128)S(1)}, bf16[256,2048]{1,0:T(8,128)(2,1)S(1)}, f32[128,2048]{1,0:T(8,128)S(1)}, f32[96,128]{1,0:T(8,128)S(1)}, f32[96,128]{1,0:T(8,128)S(1)}) custom-call(bf16[256,2048]{1,0:T(8,128)(2,1)S(1)} %copy-done.1, bf16[256,2048]{1,0:T(8,128)(2,1)S(1)} %copy-done, bf16[256,2048]{1,0:T(8,128)(2,1)S(1)} %copy-done.2, ...), custom_call_target="tpu_custom_call" | custom-call | tf_op jit(solution)/shard_map/early/pallas_call | solution.py:49
  19.2 0.0 collective-permute-done.halo_ref
  19.2 3.1 %late.1 = (f32[160,2048]{1,0:T(8,128)S(1)}, bf16[160,2048]{1,0:T(8,128)(2,1)S(1)}, f32[2,256]{1,0:T(2,128)S(1)}) custom-call(bf16[144,2048]{1,0:T(8,128)(2,1)S(1)} %collective-permute-done.halo_ref, bf16[256,2048]{1,0:T(8,128)(2,1)S(1)} %copy-done.1, bf16[256,2048]{1,0:T(8,128)(2,1)S(1)} %copy-done, bf16[256,2048]{1,0:T(8,128)(2,1)S(1)} %copy-done.2, ...), custom_call_target="tpu_custom_call" | custom-call | tf_op jit(solution)/shard_map/late/pallas_call | solution.py:49
  22.3 1.4 %collective-permute-start.1 = (f32[2,256]{1,0:T(2,128)S(1)}, f32[2,256]{1,0:T(2,128)S(1)}, u32[]{:S(2)}, u32[]{:S(2)}) collective-permute-start(f32[2,256]{1,0:T(2,128)S(1)} %get-tuple-element.42.rest_0_), channel_id=1, source_target_pairs={{0,1},{1,2},{2,3},{3,0},{4,5},{5,6},{6,7},{7,4},{8,9},{9,10},{10,1... | collective-permute-start | bytes 6152 | tf_op jit(solution)/shard_map/ppermute | solution.py:462
  23.7 2.6 %collective-permute-start.2 = (f32[2,256]{1,0:T(2,128)S(1)}, f32[2,256]{1,0:T(2,128)S(1)}, u32[]{:S(2)}, u32[]{:S(2)}) collective-permute-start(f32[2,256]{1,0:T(2,128)S(1)} %get-tuple-element.42.rest_0_), channel_id=1, source_target_pairs={{0,2},{1,3},{2,0},{3,1},{4,6},{5,7},{6,4},{7,5},{8,10},{9,11},{10,... | collective-permute-start | bytes 6152 | tf_op jit(solution)/shard_map/ppermute | solution.py:462
  26.3 1.1 %collective-permute-start.3 = (f32[2,256]{1,0:T(2,128)S(1)}, f32[2,256]{1,0:T(2,128)S(1)}, u32[]{:S(2)}, u32[]{:S(2)}) collective-permute-start(f32[2,256]{1,0:T(2,128)S(1)} %get-tuple-element.42.rest_0_), channel_id=1, source_target_pairs={{0,3},{1,0},{2,1},{3,2},{4,7},{5,4},{6,5},{7,6},{8,11},{9,8},{10,9... | collective-permute-start | bytes 6152 | tf_op jit(solution)/shard_map/ppermute | solution.py:462
  27.4 2.4 %wide_gated.1.wide_low_ref = f32[160,2048]{1,0:T(8,128)S(1)} custom-call(bf16[144,2048]{1,0:T(8,128)(2,1)S(1)} %collective-permute-done.halo_ref, bf16[256,2048]{1,0:T(8,128)(2,1)S(1)} %copy-done.1, bf16[256,2048]{1,0:T(8,128)(2,1)S(1)} %copy-done, bf16[4096,256]{1,0:T(8,128)(2,1)S(1)} %get-tuple-element.32.table_ref), custom_call_target="tpu_custom_call" | custom-call | tf_op jit(solution)/shard_map/wide_gated/pallas_call | solution.py:49
  29.8 0.0 collective-permute-done.1.rest_1_
  29.8 0.0 collective-permute-done.2.rest_2_
  29.8 0.0 collective-permute-done.3.rest_3_
  29.8 0.9 %head_rows.1 = bf16[144,2048]{1,0:T(8,128)(2,1)S(1)} custom-call(bf16[256,2048]{1,0:T(8,128)(2,1)S(1)} %copy-done.2, bf16[256,2048]{1,0:T(8,128)(2,1)S(1)} %copy-done.3, f32[160,2048]{1,0:T(8,128)S(1)} %get-tuple-element.36.medium_low_ref.medium_ref, f32[1,2048]{1,0:T(1,128)S(1)} %bitcast.9, f32[2,256]{1,0:T(2,128)S(1)} %get-tuple-element.42.rest_0_, ...), custom_call_target="tpu_custom_call" | custom-call | tf_op jit(solution)/shard_map/head_rows/pallas_call | solution.py:49
  30.7 1.9 %collective-permute-start.4 = (bf16[144,2048]{1,0:T(8,128)(2,1)S(1)}, bf16[144,2048]{1,0:T(8,128)(2,1)S(1)}, u32[]{:S(2)}, u32[]{:S(2)}) collective-permute-start(bf16[144,2048]{1,0:T(8,128)(2,1)S(1)} %head_rows.1), channel_id=1, source_target_pairs={{4,0},{8,4},{12,8},{16,12},{20,16},{24,20},{28,24},{32,28},{36,32}... | collective-permute-start | bytes 1769480 | tf_op jit(solution)/shard_map/ppermute | solution.py:62
  32.6 8.2 %gradients.1 = (bf16[256,2048]{1,0:T(8,128)(2,1)}, bf16[256,2048]{1,0:T(8,128)(2,1)S(1)}, f32[256,128]{1,0:T(8,128)}) custom-call(bf16[256,2048]{1,0:T(8,128)(2,1)S(1)} %copy-done.2, bf16[256,2048]{1,0:T(8,128)(2,1)S(1)} %copy-done.3, f32[160,2048]{1,0:T(8,128)S(1)} %get-tuple-element.36.medium_low_ref.medium_ref, ...), custom_call_target="tpu_custom_call" | custom-call | tf_op jit(solution)/shard_map/gradients/pallas_call | solution.py:49
  40.8 0.0 copy-start.6
  40.8 1.0 %copy-done.6 = bf16[256,2048]{1,0:T(8,128)(2,1)} copy-done((bf16[256,2048]{1,0:T(8,128)(2,1)}, bf16[256,2048]{1,0:T(8,128)(2,1)S(1)}, u32[]{:S(2)}) %copy-start.6) | copy-done | bytes 1048600
  41.8 13.0 %all-to-all-start = ((f32[64,4,128]{2,1,0:T(4,128)}), f32[64,4,128]{2,1,0:T(4,128)S(1)}, u32[]{:S(2)}, u32[]{:S(2)}) async-start(f32[64,4,128]{2,1,0:T(4,128)} %bitcast.2), calls=%async_computation | async-start | bytes 262144 | tf_op jit(solution)/shard_map/all_to_all | solution.py:468
  54.8 0.0 collective-permute-done.4.halo_ref
  54.8 0.0 copy-start.5
  54.8 1.6 %copy-done.5 = bf16[4096,256]{1,0:T(8,128)(2,1)S(1)} copy-done((bf16[4096,256]{1,0:T(8,128)(2,1)S(1)}, bf16[4096,256]{1,0:T(8,128)(2,1)}, u32[]{:S(2)}) %copy-start.5) | copy-done | bytes 2097176
  56.4 0.0 copy-start.7
  56.4 1.2 %copy-done.7 = bf16[256,2048]{1,0:T(8,128)(2,1)S(1)} copy-done((bf16[256,2048]{1,0:T(8,128)(2,1)S(1)}, bf16[256,2048]{1,0:T(8,128)(2,1)}, u32[]{:S(2)}) %copy-start.7) | copy-done | bytes 1048600
  57.6 5.5 %backward.1 = (bf16[256,2048]{1,0:T(8,128)(2,1)}, bf16[256,2048]{1,0:T(8,128)(2,1)}) custom-call(bf16[256,2048]{1,0:T(8,128)(2,1)S(1)} %copy-done.7, bf16[144,2048]{1,0:T(8,128)(2,1)S(1)} %collective-permute-done.4.halo_ref, f32[8,2048]{1,0:T(8,128)S(1)} %pad_convert_fusion.se_ref, bf16[256,2048]{1,0:T(8,128)(2,1)S(1)} %copy-done.1, ...), custom_call_target="tpu_custom_call" | custom-call | tf_op jit(solution)/shard_map/backward/pallas_call | solution.py:49
  63.2 2.7 %all-to-all-done = f32[64,4,128]{2,1,0:T(4,128)S(1)} async-done(((f32[64,4,128]{2,1,0:T(4,128)}), f32[64,4,128]{2,1,0:T(4,128)S(1)}, u32[]{:S(2)}, u32[]{:S(2)}) %all-to-all-start) | async-done | bytes 131104 | tf_op jit(solution)/shard_map/all_to_all | solution.py:468
  65.9 0.1 reduce_sum.9
  66.0 18.5 %all_to_all.10 = f32[64,4,128]{2,1,0:T(4,128)S(1)} all-to-all(f32[64,4,128]{2,1,0:T(4,128)S(1)} %broadcast_in_dim.10), channel_id=1, replica_groups=mesh['ctx'=64,'tp'=4] {'ctx'}, dimensions={0} | all-to-all | bytes 262144 | tf_op jit(solution)/shard_map/all_to_all | solution.py:470
  84.5 0.9 %finish.1 = (f32[128,128]{1,0:T(8,128)}, f32[7,2048]{1,0:T(8,128)}, f32[1,2048]{1,0:T(1,128)}) custom-call(f32[256,128]{1,0:T(8,128)S(1)} %bitcast.6), custom_call_target="tpu_custom_call" | custom-call | tf_op jit(solution)/shard_map/finish/pallas_call | solution.py:448
  (4 shorter events, 0.1 us)
Async XLA Ops:
  0.6 11.6 %copy-start = (bf16[256,2048]{1,0:T(8,128)(2,1)S(1)}, bf16[256,2048]{1,0:T(8,128)(2,1)}, u32[]{:S(2)}) copy-start(bf16[256,2048]{1,0:T(8,128)(2,1)} %value_ref.7) | copy-start | bytes 3145732
  0.6 11.6 %copy-start.1 = (bf16[256,2048]{1,0:T(8,128)(2,1)S(1)}, bf16[256,2048]{1,0:T(8,128)(2,1)}, u32[]{:S(2)}) copy-start(bf16[256,2048]{1,0:T(8,128)(2,1)} %key_ref.7) | copy-start | bytes 3145732
  0.7 11.5 %copy-start.9 = (bf16[7,2048]{1,0:T(8,128)(2,1)S(1)}, bf16[7,2048]{1,0:T(8,128)(2,1)}, u32[]{:S(2)}) copy-start(bf16[7,2048]{1,0:T(8,128)(2,1)} %param.12) | copy-start | bytes 86020
  0.7 11.6 %copy-start.8 = (f32[2048]{0:T(1024)S(1)}, f32[2048]{0:T(1024)}, u32[]{:S(2)}) copy-start(f32[2048]{0:T(1024)} %param.13) | copy-start | bytes 24580
  3.0 16.2 %collective-permute-start = (bf16[144,2048]{1,0:T(8,128)(2,1)}, bf16[144,2048]{1,0:T(8,128)(2,1)S(1)}, u32[]{:S(2)}, u32[]{:S(2)}) collective-permute-start(bf16[144,2048]{1,0:T(8,128)(2,1)} %multiply_convert_fusion), channel_id=1, source_target_pairs={{0,4},{4,8},{8,12},{12,16},{16,20},{20,24},{24,28},{28,32},{32,36}... | collective-permute-start | bytes 1769480 | tf_op jit(solution)/shard_map/ppermute | solution.py:62
  10.9 1.3 %copy-start.4 = (bf16[4096,256]{1,0:T(8,128)(2,1)}, bf16[4096,256]{1,0:T(8,128)(2,1)S(1)}, u32[]{:S(2)}) copy-start(bf16[4096,256]{1,0:T(8,128)(2,1)S(1)} %get-tuple-element.49.table_ref) | copy-start | bytes 6291460
  12.2 1.2 %copy-start.2 = (bf16[256,2048]{1,0:T(8,128)(2,1)S(1)}, bf16[256,2048]{1,0:T(8,128)(2,1)}, u32[]{:S(2)}) copy-start(bf16[256,2048]{1,0:T(8,128)(2,1)} %query_ref.7) | copy-start | bytes 3145732
  13.5 1.2 %copy-start.3 = (bf16[256,2048]{1,0:T(8,128)(2,1)S(1)}, bf16[256,2048]{1,0:T(8,128)(2,1)}, u32[]{:S(2)}) copy-start(bf16[256,2048]{1,0:T(8,128)(2,1)} %out_grad_ref.7) | copy-start | bytes 3145732
  22.3 7.4 %collective-permute-start.1 = (f32[2,256]{1,0:T(2,128)S(1)}, f32[2,256]{1,0:T(2,128)S(1)}, u32[]{:S(2)}, u32[]{:S(2)}) collective-permute-start(f32[2,256]{1,0:T(2,128)S(1)} %get-tuple-element.42.rest_0_), channel_id=1, source_target_pairs={{0,1},{1,2},{2,3},{3,0},{4,5},{5,6},{6,7},{7,4},{8,9},{9,10},{10,1... | collective-permute-start | bytes 6152 | tf_op jit(solution)/shard_map/ppermute | solution.py:462
  23.7 6.1 %collective-permute-start.2 = (f32[2,256]{1,0:T(2,128)S(1)}, f32[2,256]{1,0:T(2,128)S(1)}, u32[]{:S(2)}, u32[]{:S(2)}) collective-permute-start(f32[2,256]{1,0:T(2,128)S(1)} %get-tuple-element.42.rest_0_), channel_id=1, source_target_pairs={{0,2},{1,3},{2,0},{3,1},{4,6},{5,7},{6,4},{7,5},{8,10},{9,11},{10,... | collective-permute-start | bytes 6152 | tf_op jit(solution)/shard_map/ppermute | solution.py:462
  26.3 3.5 %collective-permute-start.3 = (f32[2,256]{1,0:T(2,128)S(1)}, f32[2,256]{1,0:T(2,128)S(1)}, u32[]{:S(2)}, u32[]{:S(2)}) collective-permute-start(f32[2,256]{1,0:T(2,128)S(1)} %get-tuple-element.42.rest_0_), channel_id=1, source_target_pairs={{0,3},{1,0},{2,1},{3,2},{4,7},{5,4},{6,5},{7,6},{8,11},{9,8},{10,9... | collective-permute-start | bytes 6152 | tf_op jit(solution)/shard_map/ppermute | solution.py:462
  30.7 24.1 %collective-permute-start.4 = (bf16[144,2048]{1,0:T(8,128)(2,1)S(1)}, bf16[144,2048]{1,0:T(8,128)(2,1)S(1)}, u32[]{:S(2)}, u32[]{:S(2)}) collective-permute-start(bf16[144,2048]{1,0:T(8,128)(2,1)S(1)} %head_rows.1), channel_id=1, source_target_pairs={{4,0},{8,4},{12,8},{16,12},{20,16},{24,20},{28,24},{32,28},{36,32}... | collective-permute-start | bytes 1769480 | tf_op jit(solution)/shard_map/ppermute | solution.py:62
  40.8 1.0 %copy-start.6 = (bf16[256,2048]{1,0:T(8,128)(2,1)}, bf16[256,2048]{1,0:T(8,128)(2,1)S(1)}, u32[]{:S(2)}) copy-start(bf16[256,2048]{1,0:T(8,128)(2,1)S(1)} %get-tuple-element.48.grad_ref) | copy-start | bytes 3145732
  41.8 24.1 %all-to-all-start = ((f32[64,4,128]{2,1,0:T(4,128)}), f32[64,4,128]{2,1,0:T(4,128)S(1)}, u32[]{:S(2)}, u32[]{:S(2)}) async-start(f32[64,4,128]{2,1,0:T(4,128)} %bitcast.2), calls=%async_computation | async-start | bytes 262144 | tf_op jit(solution)/shard_map/all_to_all | solution.py:468
  54.8 1.6 %copy-start.5 = (bf16[4096,256]{1,0:T(8,128)(2,1)S(1)}, bf16[4096,256]{1,0:T(8,128)(2,1)}, u32[]{:S(2)}) copy-start(bf16[4096,256]{1,0:T(8,128)(2,1)} %copy-done.4) | copy-start | bytes 6291460
  56.4 1.2 %copy-start.7 = (bf16[256,2048]{1,0:T(8,128)(2,1)S(1)}, bf16[256,2048]{1,0:T(8,128)(2,1)}, u32[]{:S(2)}) copy-start(bf16[256,2048]{1,0:T(8,128)(2,1)} %copy-done.6) | copy-start | bytes 3145732

commit v3 on v2

--- a/solution.py
+++ b/solution.py
@@ -17,18 +17,24 @@
 HALO = 144
 S = 32
 W = S + MR_LEN
+SG = 16
 GT = LANES // GROUP
 EARLY = S + MR_LEN
 F32 = jnp.float32
 BF16 = jnp.bfloat16
 
 
-UNROLL = 4
+UNROLL = 8
+TAIL_PARTS = 4
 VMEM = pl.BlockSpec(memory_space=pltpu.VMEM)
 
 
 def params(limit=24):
     return pltpu.CompilerParams(vmem_limit_bytes=limit * 1024 * 1024)
+
+
+def cost(micros):
+    return pl.CostEstimate(flops=int(micros * 1e9), bytes_accessed=0, transcendentals=0)
 
 
 def each_tile(channels, body):
@@ -45,7 +51,7 @@
     return pl.ds(pl.multiple_of(tile * rows, rows), rows)
 
 
-def call(body, name, outs, scratch, *args):
+def call(body, name, micros, outs, scratch, *args):
     return pl.pallas_call(
         body,
         in_specs=[VMEM] * len(args),
@@ -53,6 +59,7 @@
         out_shape=[jax.ShapeDtypeStruct(shape, dtype) for shape, dtype in outs],
         scratch_shapes=scratch,
         compiler_params=params(),
+        cost_estimate=cost(micros),
         name=name,
     )(*args)
 
@@ -82,33 +89,80 @@
     return results
 
 
-def table_kernel(front_ref, back_ref, front_out, back_out):
+def table_kernel(taps_ref, front_out, back_out, rows_ref):
+    taps = taps_ref[...]
+    row_ids = lax.broadcasted_iota(jnp.int32, (MR_LEN, 2 * LANES), 0)
+    col_ids = lax.broadcasted_iota(jnp.int32, (MR_LEN, 2 * LANES), 1)
+    for n, place in enumerate((MR_LEN - row_ids, row_ids)):
+        pick = jnp.where(col_ids == place, 1.0, 0.0).astype(BF16)
+        rows_ref[n] = lax.dot_general(taps, pick, (((0,), (0,)), ((), ())), preferred_element_type=F32)
+
     def one(g, carry):
-        for source, target in ((front_ref, front_out), (back_ref, back_out)):
-            rows = source[of_tile(g, GT), :]
+        for n, target in enumerate((front_out, back_out)):
+            rows = rows_ref[n, of_tile(g, GT), :]
             for k in range(GT):
                 row = jnp.broadcast_to(rows[k : k + 1, :], (S, 2 * LANES))
                 turned = pltpu.roll(row, 0, 1, stride=1, stride_axis=0).astype(BF16)
                 target[of_tile(g * GT + k, S), :] = turned
         return carry
 
-    lax.fori_loop(0, front_ref.shape[0] // GT, one, 0)
-
-
-def tables(front, back):
-    shape = ((front.shape[0] * S, 2 * LANES), BF16)
-    return call(table_kernel, "filter_tables", [shape, shape], [], front, back)
+    lax.fori_loop(0, taps_ref.shape[1] // GT, one, 0)
+
+
+def tables(mr_filter):
+    groups = mr_filter.shape[1]
+    shape = ((groups * S, 2 * LANES), BF16)
+    scratch = [pltpu.VMEM((2, groups, 2 * LANES), F32)]
+    return call(table_kernel, "filter_tables", 2.4, [shape, shape], scratch, mr_filter)
 
 
 def short_filter(se_ref, at, gated_ref, first, rows):
     total = jnp.zeros((rows, LANES), F32)
+    se = se_ref[:, at].astype(F32)
     for tap in range(SE_LEN):
-        total = total + se_ref[tap : tap + 1, at] * gated_ref[first - tap : first - tap + rows, :]
+        total = total + se[tap : tap + 1, :] * gated_ref[first - tap : first - tap + rows, :]
     return total.astype(BF16)
 
 
 def gate(key_ref, value_ref, rows, at):
     return (key_ref[rows, at].astype(F32) * value_ref[rows, at].astype(F32)).astype(BF16)
+
+
+def tail_kernel(key_ref, value_ref, tail_out, held_ref, sems):
+    tok, channels = key_ref.shape
+    width = channels // TAIL_PARTS
+    copies = []
+    for n in range(TAIL_PARTS):
+        at = slice(n * width, (n + 1) * width)
+        for m, source in enumerate((key_ref, value_ref)):
+            copy = pltpu.make_async_copy(
+                source.at[tok - HALO :, at], held_ref.at[m, :, at], sems.at[m, n]
+            )
+            copy.start()
+            copies.append(copy)
+    for n in range(TAIL_PARTS):
+        copies[2 * n].wait()
+        copies[2 * n + 1].wait()
+        at = slice(n * width, (n + 1) * width)
+        tail_out[:, at] = (held_ref[0, :, at].astype(F32) * held_ref[1, :, at].astype(F32)).astype(BF16)
+
+
+def tail_rows(key_in, value_in):
+    channels = key_in.shape[1]
+    anywhere = pl.BlockSpec(memory_space=pltpu.HBM)
+    return pl.pallas_call(
+        tail_kernel,
+        in_specs=[anywhere, anywhere],
+        out_specs=VMEM,
+        out_shape=jax.ShapeDtypeStruct((HALO, channels), BF16),
+        scratch_shapes=[
+            pltpu.VMEM((2, HALO, channels), BF16),
+            pltpu.SemaphoreType.DMA((2, TAIL_PARTS)),
+        ],
+        compiler_params=params(63),
+        cost_estimate=cost(1.2),
+        name="tail_rows",
+    )(key_in, value_in)
 
 
 def early_kernel(
@@ -167,7 +221,7 @@
         ((tok - EARLY, LANES), F32),
     ]
     scratch = [pltpu.VMEM((UNROLL, tok, LANES), F32)]
-    return call(early_kernel, "early", outs, scratch, key_in, value_in, query, out_grad, se, gain, table)
+    return call(early_kernel, "early", 4.2, outs, scratch, key_in, value_in, query, out_grad, se, gain, table)
 
 
 def window(low_ref, high_ref, b, at):
@@ -235,6 +289,7 @@
     return call(
         late_kernel,
         "late",
+        2.9,
         outs,
         scratch,
         halo,
@@ -277,7 +332,7 @@
 def head(sums, query, out_grad, medium_low, gain):
     outs = [((HALO, query.shape[1]), BF16)]
     scratch = [pltpu.VMEM((HALO, LANES), F32), pltpu.VMEM((HALO, LANES), F32)]
-    return call(head_kernel, "head_rows", outs, scratch, query, out_grad, medium_low, gain, *sums)[0]
+    return call(head_kernel, "head_rows", 0.9, outs, scratch, query, out_grad, medium_low, gain, *sums)[0]
 
 
 def wide_kernel(halo_ref, key_ref, value_ref, table_ref, wide_out, gated_ref):
@@ -298,7 +353,7 @@
 def wide(halo, key_in, value_in, table):
     outs = [((MR_LEN + S, key_in.shape[1]), F32)]
     scratch = [pltpu.VMEM((UNROLL, W + MR_LEN, LANES), BF16)]
-    return call(wide_kernel, "wide_gated", outs, scratch, halo, key_in, value_in, table)[0]
+    return call(wide_kernel, "wide_gated", 2.0, outs, scratch, halo, key_in, value_in, table)[0]
 
 
 def grads_kernel(
@@ -316,8 +371,8 @@
     query_grad_out, medium_grad_out, packed_out, scale_ref, slope_ref, cross_ref, wide_ref = rest[-7:]
     tok, channels = query_ref.shape
     spread_sums(rest[:-7], scale_ref, slope_ref, tok)
-    blocks = tok // S
-    side = GT * S
+    blocks = tok // SG
+    side = GT * SG
 
     def body(at, tile, slot):
         query = query_ref[:, at].astype(F32)
@@ -339,22 +394,21 @@
             jnp.sum(wide_grad * rows[S - tap : S - tap + tok, :], axis=0, keepdims=True)
             for tap in range(SE_LEN)
         ]
-        lhs_rows = jnp.concatenate([medium_grad[S * b : S * b + S, :] for b in range(blocks)], axis=1)
+        lhs_rows = jnp.concatenate([medium_grad[SG * b : SG * b + SG, :] for b in range(blocks)], axis=1)
         which = lax.broadcasted_iota(jnp.int32, lhs_rows.shape, 1) % LANES // GROUP
         lhs = jnp.concatenate(
             [jnp.where(which == g, lhs_rows, jnp.zeros_like(lhs_rows)) for g in range(GT)], axis=0
         )
-        rhs = jnp.concatenate(
-            [window(short_low_ref, short_high_ref, b, at) for b in range(blocks)], axis=1
-        )
+        short = jnp.concatenate([short_low_ref[:, at], short_high_ref[S:, at]], axis=0)
+        rhs = jnp.concatenate([short[SG * b : SG * b + SG + MR_LEN, :] for b in range(blocks)], axis=1)
         cross = lax.dot_general(lhs, rhs, (((1,), (1,)), ((), ())), preferred_element_type=F32)
         held = cross_ref.at[slot]
         held[:side, :] = cross[:, :LANES]
-        held[side:, :S] = cross[:, LANES:]
+        held[side:, :SG] = cross[:, LANES:]
         total = jnp.zeros((GT, 2 * LANES), F32)
-        for s in range(S):
+        for s in range(SG):
             part = jnp.concatenate(
-                [held[pl.ds(m * side + s, GT, stride=S), :] for m in range(2)], axis=1
+                [held[pl.ds(m * side + s, GT, stride=SG), :] for m in range(2)], axis=1
             )
             total = total + pltpu.roll(part, 2 * LANES - 1 - s, 1)
         packed_out[of_tile(tile, 2 * GT), :] = jnp.concatenate(
@@ -374,12 +428,13 @@
     scratch = [
         pltpu.VMEM((tok, LANES), F32),
         pltpu.VMEM((tok, LANES), F32),
-        pltpu.VMEM((UNROLL, 2 * GT * S, LANES), F32),
+        pltpu.VMEM((UNROLL, 2 * GT * SG, LANES), F32),
         pltpu.VMEM((UNROLL, tok + S, LANES), F32),
     ]
     return call(
         grads_kernel,
         "gradients",
+        6.6,
         outs,
         scratch,
         query,
@@ -410,8 +465,9 @@
         for b, part in enumerate(toeplitz(table_ref[of_tile(tile, GT * S), :W], windows)):
             short[S * b : S * b + S, :] = part
         total = jnp.zeros((tok, LANES), F32)
+        se = se_ref[:, at].astype(F32)
         for tap in range(SE_LEN):
-            total = total + se_ref[tap : tap + 1, at] * short[tap : tap + tok, :]
+            total = total + se[tap : tap + 1, :] * short[tap : tap + tok, :]
         key_out[:, at] = (total * value_ref[:, at].astype(F32)).astype(BF16)
         value_out[:, at] = (total * key_ref[:, at].astype(F32)).astype(BF16)
 
@@ -425,12 +481,13 @@
         pltpu.VMEM((UNROLL, tok + W, LANES), BF16),
         pltpu.VMEM((UNROLL, tok + S, LANES), F32),
     ]
-    return call(backward_kernel, "backward", outs, scratch, medium_grad, halo, se, key_in, value_in, table)
-
-
-def finish_kernel(tokens, packed_ref, mr_out, se_out, gain_out):
-    tiles = packed_ref.shape[0] // (2 * GT)
-    rows = jnp.concatenate([packed_ref[2 * GT * i : 2 * GT * i + GT, :] for i in range(tiles)], axis=0)
+    return call(backward_kernel, "backward", 5.4, outs, scratch, medium_grad, halo, se, key_in, value_in, table)
+
+
+def finish_kernel(tokens, low_ref, high_ref, mr_out, se_out, gain_out):
+    packed = jnp.concatenate([low_ref[...], high_ref[...]], axis=0)
+    tiles = packed.shape[0] // (2 * GT)
+    rows = jnp.concatenate([packed[2 * GT * i : 2 * GT * i + GT, :] for i in range(tiles)], axis=0)
     row_ids = lax.broadcasted_iota(jnp.int32, (MR_LEN, MR_LEN), 0)
     col_ids = lax.broadcasted_iota(jnp.int32, (MR_LEN, MR_LEN), 1)
     flip = jnp.where(row_ids + col_ids == MR_LEN - 1, 1.0, 0.0).astype(F32)
@@ -440,11 +497,11 @@
     for i in range(tiles):
         at = slice(i * LANES, (i + 1) * LANES)
         low = 2 * GT * i + GT
-        se_out[:, at] = packed_ref[low : low + SE_LEN, :] * (1.0 / tokens**0.5)
-        gain_out[:, at] = packed_ref[low + SE_LEN : low + SE_LEN + 1, :] * (1.0 / tokens**0.5)
-
-
-def finish(packed, tokens, channels):
+        se_out[:, at] = packed[low : low + SE_LEN, :] * (1.0 / tokens**0.5)
+        gain_out[:, at] = packed[low + SE_LEN : low + SE_LEN + 1, :] * (1.0 / tokens**0.5)
+
+
+def finish(low, high, tokens, channels):
     return pl.pallas_call(
         functools.partial(finish_kernel, tokens),
         out_shape=[
@@ -453,8 +510,9 @@
             jax.ShapeDtypeStruct((1, channels), F32),
         ],
         compiler_params=params(),
+        cost_estimate=cost(0.9),
         name="finish",
-    )(packed)
+    )(low, high)
 
 
 def from_peers(x, axis):
@@ -462,25 +520,27 @@
     return [lax.ppermute(x, axis, [(i, (i + k) % peers) for i in range(peers)]) for k in range(1, peers)]
 
 
-def sum_over_ctx(packed, beside):
+def sum_over_ctx(packed):
     peers = lax.axis_size("ctx")
-    parts = packed.reshape(peers, packed.shape[0] // peers, packed.shape[1])
-    arrived, other = lax.optimization_barrier((lax.all_to_all(parts, "ctx", 0, 0), beside()))
-    mine = jnp.sum(arrived, axis=0)
-    everyone = lax.all_to_all(jnp.broadcast_to(mine[None], parts.shape), "ctx", 0, 0)
-    return everyone.reshape(packed.shape), other
+    half, lanes = packed.shape[0] // 2, packed.shape[1]
+    swap = [(i, i ^ 1) for i in range(peers)]
+    side = lax.axis_index("ctx") % 2
+    pair = packed + lax.ppermute(packed, "ctx", swap)
+    groups = [list(range(k, peers, 2)) for k in range(2)]
+    exchange = lambda x: lax.all_to_all(x, "ctx", 0, 0, axis_index_groups=groups)
+    parts = lax.dynamic_slice_in_dim(pair, side * half, half).reshape(peers // 2, 2 * half // peers, lanes)
+    mine = jnp.sum(exchange(parts), axis=0)
+    own = exchange(jnp.broadcast_to(mine[None], parts.shape)).reshape(half, lanes)
+    other = lax.ppermute(own, "ctx", swap)
+    return jnp.where(side == 0, own, other), jnp.where(side == 0, other, own)
 
 
 def local(query, key_in, value_in, out_grad, mr_filter, se_filter, gain):
     tok, channels = query.shape
     tokens_all = tok * lax.axis_size("ctx")
-    tail = (key_in[-HALO:].astype(F32) * value_in[-HALO:].astype(F32)).astype(BF16)
-    gated_halo = shifted(tail, 1)
-    taps = mr_filter.astype(F32).T
-    front = jnp.pad(jnp.flip(taps, axis=1), ((0, 0), (1, LANES - 1)))
-    back = jnp.pad(taps, ((0, 0), (0, LANES)))
-    front_table, back_table = tables(front, back)
-    se = jnp.pad(se_filter.astype(F32), ((0, 1), (0, 0)))
+    gated_halo = shifted(tail_rows(key_in, value_in), 1)
+    front_table, back_table = tables(mr_filter)
+    se = se_filter
     gain_row = gain[None, :]
     medium_high, short_high, wide_high, square, inner = early(
         key_in, value_in, query, out_grad, se, gain_row, front_table
@@ -515,10 +575,10 @@
         wide_low,
         wide_high,
     )
-    packed, (key_grad, value_grad) = sum_over_ctx(
-        packed, lambda: backward(medium_grad, grad_halo, se, key_in, value_in, back_table)
-    )
-    mr_grad, se_grad, gain_grad = finish(packed, tokens_all, channels)
+    key_grad, value_grad = backward(medium_grad, grad_halo, se, key_in, value_in, back_table)
+    packed, key_grad = lax.optimization_barrier((packed, key_grad))
+    low, high = sum_over_ctx(packed)
+    mr_grad, se_grad, gain_grad = finish(low, high, tokens_all, channels)
     return query_grad, key_grad, value_grad, mr_grad, se_grad, gain_grad[0]
 
 

time: 85.8 us -> 83.8 us (0.977)
  blocking collectives: 18.5 us -> 33.7 us
  starting transfers between devices: 24.5 us -> 14.5 us
  local copies, waits for them, and re-layouts: 8.64 us -> 0.06 us
  waiting for transfers between devices: 2.75 us -> 7.54 us
  other arithmetic: 2.44 us -> 0.06 us
    all_to_all x1 -> x2, blocking collectives: 18.5 us -> 33.7 us  [sum_over_ctx(): lax.all_to_all(x, 'ctx', 0, 0, axis_index_groups=groups)]
    all_to_all x1 -> x0, starting transfers between devices: 13 us -> none  [sum_over_ctx(): lax.all_to_all(parts, 'ctx', 0, 0)]
    unnamed x21 -> x14, local copies, waits for them, and re-layouts: 8.43 us -> 0.04 us
    ppermute x2, waiting for transfers between devices: 0.01 us -> 5.29 us  [shifted(): lax.ppermute(x, 'ctx', [(i, i + by) for i in range(peers) if 0 <= i + by...]
    pallas_call x7, Pallas kernels: 26.9 us -> 23.8 us  [call(): pl.pallas_call(body, in_specs=[VMEM] * len(args), out_specs=[VMEM] * len(...]
    ppermute x0 -> x2, starting transfers between devices: none -> 2.74 us  [the longest x1 2.74 us: sum_over_ctx(): other = lax.ppermute(own, 'ctx', swap)]
    all_to_all x1 -> x0, waiting for transfers between devices: 2.74 us -> none  [sum_over_ctx(): lax.all_to_all(parts, 'ctx', 0, 0)]
    convert_element_type x1 -> x0, other arithmetic: 2.34 us -> none  [local(): (key_in[-HALO:].astype(F32) * value_in[-HALO:].astype(F32)).astype(BF16)]
  transfers between devices with their start and end apart: 6 -> 7, of which waited for: 1 -> 4; matrix products, arithmetic and copies ran while one was open for 1% -> 0% of each run, Pallas kernels for 27% -> 18%
where the time goes in v3:
time: 83.8 us; the launch traced here: 83.6 us
  blocking collectives  33.7 us (40%)
  Pallas kernels  27 us (32%)
  starting transfers between devices  14.5 us (17%)
  waiting for transfers between devices  7.54 us (9%)
  between operations  0.84 us (1%)
    all_to_all x2, blocking collectives, sum_over_ctx(): lax.all_to_all(x, 'ctx', 0, 0, axis_index_groups=groups)  33.7 us
    pallas_call x7, Pallas kernels, call(): pl.pallas_call(body, in_specs=[VMEM] * len(args), out_specs=[VMEM] * len(...  23.8 us
    ppermute x2, starting transfers between devices, shifted(): lax.ppermute(x, 'ctx', [(i, i + by) for i in range(peers) if 0 <= i + by...  6.69 us
    ppermute x2, waiting for transfers between devices, shifted(): lax.ppermute(x, 'ctx', [(i, i + by) for i in range(peers) if 0 <= i + by...  5.29 us
    ppermute x3, starting transfers between devices, from_peers(): lax.ppermute(x, axis, [(i, (i + k) % peers) for i in range(peers)])  5.06 us
    ppermute x1, starting transfers between devices, sum_over_ctx(): other = lax.ppermute(own, 'ctx', swap)  2.74 us
    pallas_call x1, Pallas kernels, tail_rows(): pl.pallas_call(tail_kernel, in_specs=[anywhere, anywhere], out_specs=VMEM...  2.27 us
  transfers between devices with their start and end apart: 7, of which 4 were waited for; matrix products, arithmetic and copies ran while one was open for 0% of the time, Pallas kernels for 18%

profile of v3, /device:TPU:1, one launch (start us, length us, event | category | flops | bytes accessed | tf_op | source)
XLA Modules:
  0.0 83.6 jit_solution(11577203002130775003)
XLA Ops:
  0.6 0.0 copy-start.5
  0.6 2.3 %tail_rows.1 = bf16[144,2048]{1,0:T(8,128)(2,1)} custom-call(bf16[256,2048]{1,0:T(8,128)(2,1)} %key_ref.9, bf16[256,2048]{1,0:T(8,128)(2,1)} %value_ref.9), custom_call_target="tpu_custom_call" | custom-call | flops 1200000000 | tf_op jit(solution)/shard_map/tail_rows/pallas_call | solution.py:153
  2.9 0.0 copy-start
  2.9 0.0 copy-start.1
  2.9 0.0 copy-start.2
  3.0 0.0 copy-start.3
  3.0 0.0 copy-start.4
  3.0 0.0 copy-start.6
  3.0 4.8 %collective-permute-start = (bf16[144,2048]{1,0:T(8,128)(2,1)}, bf16[144,2048]{1,0:T(8,128)(2,1)S(1)}, u32[]{:S(2)}, u32[]{:S(2)}) collective-permute-start(bf16[144,2048]{1,0:T(8,128)(2,1)} %tail_rows.1), channel_id=1, source_target_pairs={{0,4},{4,8},{8,12},{12,16},{16,20},{20,24},{24,28},{28,32},{32,36}... | collective-permute-start | bytes 1769480 | tf_op jit(solution)/shard_map/ppermute | solution.py:69
  7.8 0.0 copy-done.5
  7.8 2.4 %filter_tables.1 = (bf16[4096,256]{1,0:T(8,128)(2,1)S(1)}, bf16[4096,256]{1,0:T(8,128)(2,1)S(1)}) custom-call(bf16[128,128]{1,0:T(8,128)(2,1)S(1)} %copy-done.5), custom_call_target="tpu_custom_call" | custom-call | flops 2400000000 | tf_op jit(solution)/shard_map/filter_tables/pallas_call | solution.py:55
  10.2 0.0 copy-done
  10.2 0.0 copy-done.1
  10.2 0.0 copy-done.2
  10.2 0.0 copy-done.3
  10.2 0.0 copy-done.4
  10.3 0.0 copy-done.6
  10.3 4.2 %early.1 = (f32[96,2048]{1,0:T(8,128)S(1)}, bf16[256,2048]{1,0:T(8,128)(2,1)S(1)}, f32[128,2048]{1,0:T(8,128)S(1)}, f32[96,128]{1,0:T(8,128)S(1)}, f32[96,128]{1,0:T(8,128)S(1)}) custom-call(bf16[256,2048]{1,0:T(8,128)(2,1)S(1)} %copy-done.3, bf16[256,2048]{1,0:T(8,128)(2,1)S(1)} %copy-done.4, bf16[256,2048]{1,0:T(8,128)(2,1)S(1)} %copy-done, ...), custom_call_target="tpu_custom_call" | custom-call | flops 4200000000 | tf_op jit(solution)/shard_map/early/pallas_call | solution.py:55
  14.5 0.4 collective-permute-done.halo_ref
  14.9 2.9 %late.1 = (f32[160,2048]{1,0:T(8,128)S(1)}, bf16[160,2048]{1,0:T(8,128)(2,1)S(1)}, f32[2,256]{1,0:T(2,128)S(1)}) custom-call(bf16[144,2048]{1,0:T(8,128)(2,1)S(1)} %collective-permute-done.halo_ref, bf16[256,2048]{1,0:T(8,128)(2,1)S(1)} %copy-done.3, bf16[256,2048]{1,0:T(8,128)(2,1)S(1)} %copy-done.4, bf16[256,2048]{1,0:T(8,128)(2,1)S(1)} %copy-done, ...), custom_call_target="tpu_custom_call" | custom-call | flops 2900000000 | tf_op jit(solution)/shard_map/late/pallas_call | solution.py:55
  17.7 1.4 %collective-permute-start.1 = (f32[2,256]{1,0:T(2,128)S(1)}, f32[2,256]{1,0:T(2,128)S(1)}, u32[]{:S(2)}, u32[]{:S(2)}) collective-permute-start(f32[2,256]{1,0:T(2,128)S(1)} %get-tuple-element.41.rest_0_), channel_id=1, source_target_pairs={{0,1},{1,2},{2,3},{3,0},{4,5},{5,6},{6,7},{7,4},{8,9},{9,10},{10,1... | collective-permute-start | bytes 6152 | tf_op jit(solution)/shard_map/ppermute | solution.py:520
  19.1 2.6 %collective-permute-start.2 = (f32[2,256]{1,0:T(2,128)S(1)}, f32[2,256]{1,0:T(2,128)S(1)}, u32[]{:S(2)}, u32[]{:S(2)}) collective-permute-start(f32[2,256]{1,0:T(2,128)S(1)} %get-tuple-element.41.rest_0_), channel_id=1, source_target_pairs={{0,2},{1,3},{2,0},{3,1},{4,6},{5,7},{6,4},{7,5},{8,10},{9,11},{10,... | collective-permute-start | bytes 6152 | tf_op jit(solution)/shard_map/ppermute | solution.py:520
  21.7 1.1 %collective-permute-start.3 = (f32[2,256]{1,0:T(2,128)S(1)}, f32[2,256]{1,0:T(2,128)S(1)}, u32[]{:S(2)}, u32[]{:S(2)}) collective-permute-start(f32[2,256]{1,0:T(2,128)S(1)} %get-tuple-element.41.rest_0_), channel_id=1, source_target_pairs={{0,3},{1,0},{2,1},{3,2},{4,7},{5,4},{6,5},{7,6},{8,11},{9,8},{10,9... | collective-permute-start | bytes 6152 | tf_op jit(solution)/shard_map/ppermute | solution.py:520
  22.8 2.0 %wide_gated.1.wide_low_ref = f32[160,2048]{1,0:T(8,128)S(1)} custom-call(bf16[144,2048]{1,0:T(8,128)(2,1)S(1)} %collective-permute-done.halo_ref, bf16[256,2048]{1,0:T(8,128)(2,1)S(1)} %copy-done.3, bf16[256,2048]{1,0:T(8,128)(2,1)S(1)} %copy-done.4, bf16[4096,256]{1,0:T(8,128)(2,1)S(1)} %get-tuple-element.31.table_ref), custom_call_target="tpu_custom_call" | custom-call | flops 2000000000 | tf_op jit(solution)/shard_map/wide_gated/pallas_call | solution.py:55
  24.8 0.0 collective-permute-done.1.rest_1_
  24.8 0.0 collective-permute-done.2.rest_2_
  24.9 0.0 collective-permute-done.3.rest_3_
  24.9 0.9 %head_rows.1 = bf16[144,2048]{1,0:T(8,128)(2,1)S(1)} custom-call(bf16[256,2048]{1,0:T(8,128)(2,1)S(1)} %copy-done, bf16[256,2048]{1,0:T(8,128)(2,1)S(1)} %copy-done.1, f32[160,2048]{1,0:T(8,128)S(1)} %get-tuple-element.35.medium_low_ref.medium_ref, f32[1,2048]{1,0:T(1,128)S(1)} %bitcast.6, f32[2,256]{1,0:T(2,128)S(1)} %get-tuple-element.41.rest_0_, ...), custom_call_target="tpu_custom_call" | custom-call | flops 900000000 | tf_op jit(solution)/shard_map/head_rows/pallas_call | solution.py:55
  25.8 1.9 %collective-permute-start.4 = (bf16[144,2048]{1,0:T(8,128)(2,1)S(1)}, bf16[144,2048]{1,0:T(8,128)(2,1)S(1)}, u32[]{:S(2)}, u32[]{:S(2)}) collective-permute-start(bf16[144,2048]{1,0:T(8,128)(2,1)S(1)} %head_rows.1), channel_id=1, source_target_pairs={{4,0},{8,4},{12,8},{16,12},{20,16},{24,20},{28,24},{32,28},{36,32}... | collective-permute-start | bytes 1769480 | tf_op jit(solution)/shard_map/ppermute | solution.py:69
  27.7 6.1 %gradients.1 = (bf16[256,2048]{1,0:T(8,128)(2,1)}, bf16[256,2048]{1,0:T(8,128)(2,1)S(1)}, f32[256,128]{1,0:T(8,128)S(1)}) custom-call(bf16[256,2048]{1,0:T(8,128)(2,1)S(1)} %copy-done, bf16[256,2048]{1,0:T(8,128)(2,1)S(1)} %copy-done.1, f32[160,2048]{1,0:T(8,128)S(1)} %get-tuple-element.35.medium_low_ref.medium_ref, ...), custom_call_target="tpu_custom_call" | custom-call | flops 6600000000 | tf_op jit(solution)/shard_map/gradients/pallas_call | solution.py:55
  33.7 4.9 %collective-permute-done.4.halo_ref = bf16[144,2048]{1,0:T(8,128)(2,1)S(1)} collective-permute-done((bf16[144,2048]{1,0:T(8,128)(2,1)S(1)}, bf16[144,2048]{1,0:T(8,128)(2,1)S(1)}, u32[]{:S(2)}, u32[]{:S(2)}) %collective-permute-start.4) | collective-permute-done | bytes 589856 | tf_op jit(solution)/shard_map/ppermute | solution.py:69
  38.6 5.4 %backward.1 = (bf16[256,2048]{1,0:T(8,128)(2,1)}, bf16[256,2048]{1,0:T(8,128)(2,1)}) custom-call(bf16[256,2048]{1,0:T(8,128)(2,1)S(1)} %get-tuple-element.47.grad_ref, bf16[144,2048]{1,0:T(8,128)(2,1)S(1)} %collective-permute-done.4.halo_ref, bf16[7,2048]{1,0:T(8,128)(2,1)S(1)} %copy-done.6, bf16[256,2048]{1,0:T(8,128)(2,1)S(1)} %copy-done.3, ...), custom_call_target="tpu_custom_call" | custom-call | flops 5400000000 | tf_op jit(solution)/shard_map/backward/pallas_call | solution.py:55
  44.0 0.0 collective-permute-start.5
  44.0 1.3 %collective-permute-done.5 = f32[256,128]{1,0:T(8,128)S(1)} collective-permute-done((f32[256,128]{1,0:T(8,128)S(1)}, f32[256,128]{1,0:T(8,128)S(1)}, u32[]{:S(2)}, u32[]{:S(2)}) %collective-permute-start.5) | collective-permute-done | bytes 131104 | tf_op jit(solution)/shard_map/ppermute | solution.py:528
  45.3 21.7 %all_to_all.10 = f32[32,4,128]{2,1,0:T(4,128)S(1)} all-to-all(f32[32,4,128]{2,1,0:T(4,128)S(1)} %bitcast.8), channel_id=1, replica_groups={{0,8,16,24,32,40,48,56,64,72,80,88,96,104,112,120,128,136,144,152,160,1..., dimensions={0} | all-to-all | bytes 131072 | tf_op jit(solution)/shard_map/all_to_all | solution.py:530
  67.1 11.9 %all_to_all.11 = f32[32,4,128]{2,1,0:T(4,128)S(1)} all-to-all(f32[32,4,128]{2,1,0:T(4,128)S(1)} %broadcast_in_dim.10), channel_id=1, replica_groups={{0,8,16,24,32,40,48,56,64,72,80,88,96,104,112,120,128,136,144,152,160,1..., dimensions={0} | all-to-all | bytes 131072 | tf_op jit(solution)/shard_map/all_to_all | solution.py:530
  79.0 2.7 %collective-permute-start.6 = (f32[128,128]{1,0:T(8,128)S(1)}, f32[128,128]{1,0:T(8,128)S(1)}, u32[]{:S(2)}, u32[]{:S(2)}) collective-permute-start(f32[128,128]{1,0:T(8,128)S(1)} %bitcast.9), channel_id=1, source_target_pairs={{0,4},{4,0},{8,12},{12,8},{16,20},{20,16},{24,28},{28,24},{32,36},... | collective-permute-start | bytes 196616 | tf_op jit(solution)/shard_map/ppermute | solution.py:534
  81.8 0.9 %collective-permute-done.6 = f32[128,128]{1,0:T(8,128)S(1)} collective-permute-done((f32[128,128]{1,0:T(8,128)S(1)}, f32[128,128]{1,0:T(8,128)S(1)}, u32[]{:S(2)}, u32[]{:S(2)}) %collective-permute-start.6) | collective-permute-done | bytes 65568 | tf_op jit(solution)/shard_map/ppermute | solution.py:534
  82.7 0.9 %finish.1 = (f32[128,128]{1,0:T(8,128)}, f32[7,2048]{1,0:T(8,128)}, f32[1,2048]{1,0:T(1,128)}) custom-call(f32[128,128]{1,0:T(8,128)S(1)} %get-tuple-element.57.low_ref, f32[128,128]{1,0:T(8,128)S(1)} %get-tuple-element.56.high_ref), custom_call_target="tpu_custom_call" | custom-call | flops 900000000 | tf_op jit(solution)/shard_map/finish/pallas_call | solution.py:505
  (4 shorter events, 0.1 us)
Async XLA Ops:
  0.6 7.1 %copy-start.5 = (bf16[128,128]{1,0:T(8,128)(2,1)S(1)}, bf16[128,128]{1,0:T(8,128)(2,1)}, u32[]{:S(2)}) copy-start(bf16[128,128]{1,0:T(8,128)(2,1)} %taps_ref.1) | copy-start | bytes 98308
  2.9 7.3 %copy-start = (bf16[256,2048]{1,0:T(8,128)(2,1)S(1)}, bf16[256,2048]{1,0:T(8,128)(2,1)}, u32[]{:S(2)}) copy-start(bf16[256,2048]{1,0:T(8,128)(2,1)} %query_ref.7) | copy-start | bytes 3145732
  2.9 7.3 %copy-start.1 = (bf16[256,2048]{1,0:T(8,128)(2,1)S(1)}, bf16[256,2048]{1,0:T(8,128)(2,1)}, u32[]{:S(2)}) copy-start(bf16[256,2048]{1,0:T(8,128)(2,1)} %out_grad_ref.7) | copy-start | bytes 3145732
  2.9 7.3 %copy-start.2 = (f32[2048]{0:T(1024)S(1)}, f32[2048]{0:T(1024)}, u32[]{:S(2)}) copy-start(f32[2048]{0:T(1024)} %param.13) | copy-start | bytes 24580
  3.0 7.3 %copy-start.3 = (bf16[256,2048]{1,0:T(8,128)(2,1)S(1)}, bf16[256,2048]{1,0:T(8,128)(2,1)}, u32[]{:S(2)}) copy-start(bf16[256,2048]{1,0:T(8,128)(2,1)} %key_ref.9) | copy-start | bytes 3145732
  3.0 7.3 %copy-start.4 = (bf16[256,2048]{1,0:T(8,128)(2,1)S(1)}, bf16[256,2048]{1,0:T(8,128)(2,1)}, u32[]{:S(2)}) copy-start(bf16[256,2048]{1,0:T(8,128)(2,1)} %value_ref.9) | copy-start | bytes 3145732
  3.0 7.3 %copy-start.6 = (bf16[7,2048]{1,0:T(8,128)(2,1)S(1)}, bf16[7,2048]{1,0:T(8,128)(2,1)}, u32[]{:S(2)}) copy-start(bf16[7,2048]{1,0:T(8,128)(2,1)} %se_ref.5) | copy-start | bytes 86020
  3.0 11.9 %collective-permute-start = (bf16[144,2048]{1,0:T(8,128)(2,1)}, bf16[144,2048]{1,0:T(8,128)(2,1)S(1)}, u32[]{:S(2)}, u32[]{:S(2)}) collective-permute-start(bf16[144,2048]{1,0:T(8,128)(2,1)} %tail_rows.1), channel_id=1, source_target_pairs={{0,4},{4,8},{8,12},{12,16},{16,20},{20,24},{24,28},{28,32},{32,36}... | collective-permute-start | bytes 1769480 | tf_op jit(solution)/shard_map/ppermute | solution.py:69
  17.7 7.1 %collective-permute-start.1 = (f32[2,256]{1,0:T(2,128)S(1)}, f32[2,256]{1,0:T(2,128)S(1)}, u32[]{:S(2)}, u32[]{:S(2)}) collective-permute-start(f32[2,256]{1,0:T(2,128)S(1)} %get-tuple-element.41.rest_0_), channel_id=1, source_target_pairs={{0,1},{1,2},{2,3},{3,0},{4,5},{5,6},{6,7},{7,4},{8,9},{9,10},{10,1... | collective-permute-start | bytes 6152 | tf_op jit(solution)/shard_map/ppermute | solution.py:520
  19.1 5.7 %collective-permute-start.2 = (f32[2,256]{1,0:T(2,128)S(1)}, f32[2,256]{1,0:T(2,128)S(1)}, u32[]{:S(2)}, u32[]{:S(2)}) collective-permute-start(f32[2,256]{1,0:T(2,128)S(1)} %get-tuple-element.41.rest_0_), channel_id=1, source_target_pairs={{0,2},{1,3},{2,0},{3,1},{4,6},{5,7},{6,4},{7,5},{8,10},{9,11},{10,... | collective-permute-start | bytes 6152 | tf_op jit(solution)/shard_map/ppermute | solution.py:520
  21.7 3.1 %collective-permute-start.3 = (f32[2,256]{1,0:T(2,128)S(1)}, f32[2,256]{1,0:T(2,128)S(1)}, u32[]{:S(2)}, u32[]{:S(2)}) collective-permute-start(f32[2,256]{1,0:T(2,128)S(1)} %get-tuple-element.41.rest_0_), channel_id=1, source_target_pairs={{0,3},{1,0},{2,1},{3,2},{4,7},{5,4},{6,5},{7,6},{8,11},{9,8},{10,9... | collective-permute-start | bytes 6152 | tf_op jit(solution)/shard_map/ppermute | solution.py:520
  25.8 12.9 %collective-permute-start.4 = (bf16[144,2048]{1,0:T(8,128)(2,1)S(1)}, bf16[144,2048]{1,0:T(8,128)(2,1)S(1)}, u32[]{:S(2)}, u32[]{:S(2)}) collective-permute-start(bf16[144,2048]{1,0:T(8,128)(2,1)S(1)} %head_rows.1), channel_id=1, source_target_pairs={{4,0},{8,4},{12,8},{16,12},{20,16},{24,20},{28,24},{32,28},{36,32}... | collective-permute-start | bytes 1769480 | tf_op jit(solution)/shard_map/ppermute | solution.py:69
  44.0 1.3 %collective-permute-start.5 = (f32[256,128]{1,0:T(8,128)S(1)}, f32[256,128]{1,0:T(8,128)S(1)}, u32[]{:S(2)}, u32[]{:S(2)}) collective-permute-start(f32[256,128]{1,0:T(8,128)S(1)} %get-tuple-element.52), channel_id=1, source_target_pairs={{0,4},{4,0},{8,12},{12,8},{16,20},{20,16},{24,28},{28,24},{32,36},... | collective-permute-start | bytes 393224 | tf_op jit(solution)/shard_map/ppermute | solution.py:528
  79.0 3.6 %collective-permute-start.6 = (f32[128,128]{1,0:T(8,128)S(1)}, f32[128,128]{1,0:T(8,128)S(1)}, u32[]{:S(2)}, u32[]{:S(2)}) collective-permute-start(f32[128,128]{1,0:T(8,128)S(1)} %bitcast.9), channel_id=1, source_target_pairs={{0,4},{4,0},{8,12},{12,8},{16,20},{20,16},{24,28},{28,24},{32,36},... | collective-permute-start | bytes 196616 | tf_op jit(solution)/shard_map/ppermute | solution.py:534

commit v4 on v3

--- a/solution.py
+++ b/solution.py
@@ -26,6 +26,9 @@
 
 UNROLL = 8
 TAIL_PARTS = 4
+BW = 512
+PARTS = 2
+NEAR = 8
 VMEM = pl.BlockSpec(memory_space=pltpu.VMEM)
 
 
@@ -38,13 +41,15 @@
 
 
 def each_tile(channels, body):
+    unroll = min(UNROLL, channels // LANES)
+
     def step(i, carry):
-        for slot in range(UNROLL):
-            tile = i * UNROLL + slot
+        for slot in range(unroll):
+            tile = i * unroll + slot
             body(pl.ds(pl.multiple_of(tile * LANES, LANES), LANES), tile, slot)
         return carry
 
-    lax.fori_loop(0, channels // LANES // UNROLL, step, 0)
+    lax.fori_loop(0, channels // LANES // unroll, step, 0)
 
 
 def of_tile(tile, rows):
@@ -450,9 +455,8 @@
     )
 
 
-def backward_kernel(
-    grad_ref, halo_ref, se_ref, key_ref, value_ref, table_ref, key_out, value_out, ext_ref, short_ref
-):
+def backward_kernel(grad_ref, halo_ref, se_ref, key_ref, value_ref, table_ref, *rest):
+    key_out, value_out, ext_ref, short_ref = rest[-4:]
     tok = key_ref.shape[0]
 
     def body(at, tile, slot):
@@ -474,18 +478,40 @@
     each_tile(key_ref.shape[1], body)
 
 
-def backward(medium_grad, halo, se, key_in, value_in, table):
+def backward(medium_grad, halo, se, key_in, value_in, table, part, done=()):
     tok, channels = key_in.shape
-    outs = [((tok, channels), BF16), ((tok, channels), BF16)]
-    scratch = [
-        pltpu.VMEM((UNROLL, tok + W, LANES), BF16),
-        pltpu.VMEM((UNROLL, tok + S, LANES), F32),
-    ]
-    return call(backward_kernel, "backward", 5.4, outs, scratch, medium_grad, halo, se, key_in, value_in, table)
-
-
-def finish_kernel(tokens, low_ref, high_ref, mr_out, se_out, gain_out):
-    packed = jnp.concatenate([low_ref[...], high_ref[...]], axis=0)
+    steps = channels // BW // PARTS
+    first = part * steps
+    col = lambda rows: pl.BlockSpec((rows, BW), lambda i: (0, first + i))
+    tiles = BW // LANES
+    shape = jax.ShapeDtypeStruct((tok, channels), BF16)
+    return pl.pallas_call(
+        backward_kernel,
+        grid=(steps,),
+        in_specs=[
+            col(tok),
+            col(HALO),
+            col(SE_LEN),
+            col(tok),
+            col(tok),
+            pl.BlockSpec((tiles * GT * S, 2 * LANES), lambda i: (first + i, 0)),
+        ]
+        + [pl.BlockSpec(memory_space=pltpu.HBM)] * len(done),
+        out_specs=[col(tok), col(tok)],
+        out_shape=[shape, shape],
+        scratch_shapes=[
+            pltpu.VMEM((tiles, tok + W, LANES), BF16),
+            pltpu.VMEM((tiles, tok + S, LANES), F32),
+        ],
+        input_output_aliases={6 + n: n for n in range(len(done))},
+        compiler_params=params(62),
+        cost_estimate=cost(3.5),
+        name="backward",
+    )(medium_grad, halo, se, key_in, value_in, table, *done)
+
+
+def finish_kernel(tokens, packed_ref, mr_out, se_out, gain_out):
+    packed = packed_ref[...]
     tiles = packed.shape[0] // (2 * GT)
     rows = jnp.concatenate([packed[2 * GT * i : 2 * GT * i + GT, :] for i in range(tiles)], axis=0)
     row_ids = lax.broadcasted_iota(jnp.int32, (MR_LEN, MR_LEN), 0)
@@ -501,7 +527,7 @@
         gain_out[:, at] = packed[low + SE_LEN : low + SE_LEN + 1, :] * (1.0 / tokens**0.5)
 
 
-def finish(low, high, tokens, channels):
+def finish(packed, tokens, channels):
     return pl.pallas_call(
         functools.partial(finish_kernel, tokens),
         out_shape=[
@@ -512,27 +538,33 @@
         compiler_params=params(),
         cost_estimate=cost(0.9),
         name="finish",
-    )(low, high)
-
-
-def from_peers(x, axis):
-    peers = lax.axis_size(axis)
-    return [lax.ppermute(x, axis, [(i, (i + k) % peers) for i in range(peers)]) for k in range(1, peers)]
-
-
-def sum_over_ctx(packed):
+    )(packed)
+
+
+def add_kernel(one_ref, other_ref, total_out):
+    total_out[...] = one_ref[...] + other_ref[...]
+
+
+def pair_up(x, partner):
+    return lax.ppermute(x, "tp", [(i, partner(i)) for i in range(lax.axis_size("tp"))])
+
+
+def spread(x, groups):
+    everyone = jnp.broadcast_to(x[None], (len(groups[0]),) + x.shape)
+    return lax.all_to_all(everyone, "ctx", 0, 0, axis_index_groups=groups)
+
+
+def sum_over_ctx(packed, beside):
     peers = lax.axis_size("ctx")
-    half, lanes = packed.shape[0] // 2, packed.shape[1]
-    swap = [(i, i ^ 1) for i in range(peers)]
-    side = lax.axis_index("ctx") % 2
-    pair = packed + lax.ppermute(packed, "ctx", swap)
-    groups = [list(range(k, peers, 2)) for k in range(2)]
-    exchange = lambda x: lax.all_to_all(x, "ctx", 0, 0, axis_index_groups=groups)
-    parts = lax.dynamic_slice_in_dim(pair, side * half, half).reshape(peers // 2, 2 * half // peers, lanes)
-    mine = jnp.sum(exchange(parts), axis=0)
-    own = exchange(jnp.broadcast_to(mine[None], parts.shape)).reshape(half, lanes)
-    other = lax.ppermute(own, "ctx", swap)
-    return jnp.where(side == 0, own, other), jnp.where(side == 0, other, own)
+    near = [list(range(first, first + NEAR)) for first in range(0, peers, NEAR)]
+    far = [list(range(first, peers, NEAR)) for first in range(NEAR)]
+    parts = packed.reshape(NEAR, packed.shape[0] // NEAR, packed.shape[1])
+    arrived = lax.all_to_all(parts, "ctx", 0, 0, axis_index_groups=near)
+    arrived, done = lax.optimization_barrier((arrived, beside(0)))
+    mine, done = lax.optimization_barrier((jnp.sum(arrived, axis=0), done))
+    arrived = spread(mine, far)
+    arrived, done = lax.optimization_barrier((arrived, beside(1, done)))
+    return spread(jnp.sum(arrived, axis=0), near).reshape(packed.shape), done
 
 
 def local(query, key_in, value_in, out_grad, mr_filter, se_filter, gain):
@@ -558,7 +590,8 @@
         square,
         inner,
     )
-    sums = [sums] + from_peers(sums, "tp")
+    sums = call(add_kernel, "pair_sums", 0.2, [((2, tok), F32)], [], sums, pair_up(sums, lambda i: i ^ 1))[0]
+    sums = [sums, pair_up(sums, lambda i: lax.axis_size("tp") - 1 - i)]
     wide_low = wide(gated_halo, key_in, value_in, front_table)
     sums, wide_low = lax.optimization_barrier((sums, wide_low))
     head_rows = head(sums, query, out_grad, medium_low, gain_row)
@@ -575,10 +608,10 @@
         wide_low,
         wide_high,
     )
-    key_grad, value_grad = backward(medium_grad, grad_halo, se, key_in, value_in, back_table)
-    packed, key_grad = lax.optimization_barrier((packed, key_grad))
-    low, high = sum_over_ctx(packed)
-    mr_grad, se_grad, gain_grad = finish(low, high, tokens_all, channels)
+    packed, (key_grad, value_grad) = sum_over_ctx(
+        packed, functools.partial(backward, medium_grad, grad_halo, se, key_in, value_in, back_table)
+    )
+    mr_grad, se_grad, gain_grad = finish(packed, tokens_all, channels)
     return query_grad, key_grad, value_grad, mr_grad, se_grad, gain_grad[0]
 
 

time: 83.8 us -> 79.1 us (0.944)
  blocking collectives: 33.7 us -> 11.4 us
  starting transfers between devices: 14.5 us -> 27.4 us
  local copies, waits for them, and re-layouts: 0.06 us -> 3.83 us
  Pallas kernels: 27 us -> 30.1 us
  waiting for transfers between devices: 7.54 us -> 5.05 us
    all_to_all x2 -> x1, blocking collectives: 33.7 us -> 11.4 us  [spread(): return lax.all_to_all(everyone, 'ctx', 0, 0, axis_index_groups=groups)]
    all_to_all x0 -> x2, starting transfers between devices: none -> 15.3 us  [the longest x1 10.4 us: spread(): return lax.all_to_all(everyone, 'ctx', 0, 0, axis_index_groups=groups)]
    pallas_call x0 -> x2, Pallas kernels: none -> 8.4 us  [backward(): pl.pallas_call(backward_kernel, grid=(steps,), in_specs=[col(tok), col(HA...]
    ppermute x2, waiting for transfers between devices: 5.29 us -> 0.01 us  [shifted(): lax.ppermute(x, 'ctx', [(i, i + by) for i in range(peers) if 0 <= i + by...]
    pallas_call x7, Pallas kernels: 23.8 us -> 18.5 us  [call(): pl.pallas_call(body, in_specs=[VMEM] * len(args), out_specs=[VMEM] * len(...]
    all_to_all x0 -> x2, waiting for transfers between devices: none -> 3.91 us  [the longest x1 3.64 us: spread(): return lax.all_to_all(everyone, 'ctx', 0, 0, axis_index_groups=groups)]
    ppermute x5 -> x2, starting transfers between devices: 7.8 us -> 4.12 us  [pair_up(): lax.ppermute(x, 'tp', [(i, partner(i)) for i in range(lax.axis_size('tp'))])]
    unnamed x14 -> x20, local copies, waits for them, and re-layouts: 0.04 us -> 3.15 us
  transfers between devices with their start and end apart: 7 -> 6, of which waited for: 4 -> 3; matrix products, arithmetic and copies ran while one was open for 0% -> 0% of each run, Pallas kernels for 18% -> 29%
where the time goes in v4:
time: 79.1 us; the launch traced here: 78.7 us
  Pallas kernels  30.1 us (38%)
  starting transfers between devices  27.4 us (35%)
  blocking collectives  11.4 us (14%)
  waiting for transfers between devices  5.05 us (6%)
  local copies, waits for them, and re-layouts  3.83 us (5%)
  between operations  0.82 us (1%)
    pallas_call x7, Pallas kernels, call(): pl.pallas_call(body, in_specs=[VMEM] * len(args), out_specs=[VMEM] * len(...  18.5 us
    all_to_all x1, blocking collectives, spread(): return lax.all_to_all(everyone, 'ctx', 0, 0, axis_index_groups=groups)  11.4 us
    all_to_all x1, starting transfers between devices, spread(): return lax.all_to_all(everyone, 'ctx', 0, 0, axis_index_groups=groups)  10.4 us
    pallas_call x2, Pallas kernels, backward(): pl.pallas_call(backward_kernel, grid=(steps,), in_specs=[col(tok), col(HA...  8.4 us
    ppermute x2, starting transfers between devices, shifted(): lax.ppermute(x, 'ctx', [(i, i + by) for i in range(peers) if 0 <= i + by...  7.9 us
    all_to_all x1, starting transfers between devices, sum_over_ctx(): arrived = lax.all_to_all(parts, 'ctx', 0, 0, axis_index_groups=near)  4.94 us
    ppermute x2, starting transfers between devices, pair_up(): lax.ppermute(x, 'tp', [(i, partner(i)) for i in range(lax.axis_size('tp'))])  4.12 us
    all_to_all x1, waiting for transfers between devices, spread(): return lax.all_to_all(everyone, 'ctx', 0, 0, axis_index_groups=groups)  3.64 us
  transfers between devices with their start and end apart: 6, of which 3 were waited for; matrix products, arithmetic and copies ran while one was open for 0% of the time, Pallas kernels for 29%

profile of v4, /device:TPU:1, one launch (start us, length us, event | category | flops | bytes accessed | tf_op | source)
XLA Modules:
  0.0 78.7 jit_solution(8057938666197275517)
XLA Ops:
  0.6 0.0 copy-start.5
  0.6 2.3 %tail_rows.1 = bf16[144,2048]{1,0:T(8,128)(2,1)} custom-call(bf16[256,2048]{1,0:T(8,128)(2,1)} %key_ref.11, bf16[256,2048]{1,0:T(8,128)(2,1)} %value_ref.11), custom_call_target="tpu_custom_call" | custom-call | flops 1200000000 | tf_op jit(solution)/shard_map/tail_rows/pallas_call | solution.py:158
  2.9 0.0 copy-start
  2.9 0.0 copy-start.1
  2.9 0.0 copy-start.2
  3.0 0.0 copy-start.3
  3.0 0.0 copy-start.4
  3.0 0.0 copy-start.6
  3.0 4.8 %collective-permute-start = (bf16[144,2048]{1,0:T(8,128)(2,1)}, bf16[144,2048]{1,0:T(8,128)(2,1)S(1)}, u32[]{:S(2)}, u32[]{:S(2)}) collective-permute-start(bf16[144,2048]{1,0:T(8,128)(2,1)} %tail_rows.1), channel_id=1, source_target_pairs={{0,4},{4,8},{8,12},{12,16},{16,20},{20,24},{24,28},{28,32},{32,36}... | collective-permute-start | bytes 1769480 | tf_op jit(solution)/shard_map/ppermute | solution.py:74
  7.8 0.0 copy-done.5
  7.8 2.4 %filter_tables.1 = (bf16[4096,256]{1,0:T(8,128)(2,1)S(1)}, bf16[4096,256]{1,0:T(8,128)(2,1)S(1)}) custom-call(bf16[128,128]{1,0:T(8,128)(2,1)S(1)} %copy-done.5), custom_call_target="tpu_custom_call" | custom-call | flops 2400000000 | tf_op jit(solution)/shard_map/filter_tables/pallas_call | solution.py:60
  10.2 0.0 copy-start.7
  10.2 1.3 %copy-done.7 = bf16[4096,256]{1,0:T(8,128)(2,1)} copy-done((bf16[4096,256]{1,0:T(8,128)(2,1)}, bf16[4096,256]{1,0:T(8,128)(2,1)S(1)}, u32[]{:S(2)}) %copy-start.7) | copy-done | bytes 2097176
  11.5 0.0 copy-done
  11.5 0.0 copy-done.1
  11.6 0.0 copy-done.2
  11.6 0.0 copy-done.3
  11.6 0.0 copy-done.4
  11.6 0.0 copy-done.6
  11.6 4.2 %early.1 = (f32[96,2048]{1,0:T(8,128)S(1)}, bf16[256,2048]{1,0:T(8,128)(2,1)S(1)}, f32[128,2048]{1,0:T(8,128)S(1)}, f32[96,128]{1,0:T(8,128)S(1)}, f32[96,128]{1,0:T(8,128)S(1)}) custom-call(bf16[256,2048]{1,0:T(8,128)(2,1)S(1)} %copy-done.3, bf16[256,2048]{1,0:T(8,128)(2,1)S(1)} %copy-done.4, bf16[256,2048]{1,0:T(8,128)(2,1)S(1)} %copy-done, ...), custom_call_target="tpu_custom_call" | custom-call | flops 4200000000 | tf_op jit(solution)/shard_map/early/pallas_call | solution.py:60
  15.8 0.0 collective-permute-done.halo_ref
  15.8 2.9 %late.1 = (f32[160,2048]{1,0:T(8,128)S(1)}, bf16[160,2048]{1,0:T(8,128)(2,1)S(1)}, f32[2,256]{1,0:T(2,128)S(1)}) custom-call(bf16[144,2048]{1,0:T(8,128)(2,1)S(1)} %collective-permute-done.halo_ref, bf16[256,2048]{1,0:T(8,128)(2,1)S(1)} %copy-done.3, bf16[256,2048]{1,0:T(8,128)(2,1)S(1)} %copy-done.4, bf16[256,2048]{1,0:T(8,128)(2,1)S(1)} %copy-done, ...), custom_call_target="tpu_custom_call" | custom-call | flops 2900000000 | tf_op jit(solution)/shard_map/late/pallas_call | solution.py:60
  18.7 1.4 %collective-permute-start.1 = (f32[2,256]{1,0:T(2,128)S(1)}, f32[2,256]{1,0:T(2,128)S(1)}, u32[]{:S(2)}, u32[]{:S(2)}) collective-permute-start(f32[2,256]{1,0:T(2,128)S(1)} %get-tuple-element.45.one_ref), channel_id=1, source_target_pairs={{0,1},{1,0},{2,3},{3,2},{4,5},{5,4},{6,7},{7,6},{8,9},{9,8},{10,11... | collective-permute-start | bytes 6152 | tf_op jit(solution)/shard_map/ppermute | solution.py:549
  20.1 1.1 %collective-permute-done.1.other_ref = f32[2,256]{1,0:T(2,128)S(1)} collective-permute-done((f32[2,256]{1,0:T(2,128)S(1)}, f32[2,256]{1,0:T(2,128)S(1)}, u32[]{:S(2)}, u32[]{:S(2)}) %collective-permute-start.1) | collective-permute-done | bytes 2080 | tf_op jit(solution)/shard_map/ppermute | solution.py:549
  21.3 2.7 %collective-permute-start.2 = (f32[2,256]{1,0:T(2,128)S(1)}, f32[2,256]{1,0:T(2,128)S(1)}, u32[]{:S(2)}, u32[]{:S(2)}) collective-permute-start(f32[2,256]{1,0:T(2,128)S(1)} %pair_sums.1.rest_0_), channel_id=1, source_target_pairs={{0,3},{1,2},{2,1},{3,0},{4,7},{5,6},{6,5},{7,4},{8,11},{9,10},{10,... | collective-permute-start | bytes 6152 | tf_op jit(solution)/shard_map/ppermute | solution.py:549
  24.0 2.0 %wide_gated.1.wide_low_ref = f32[160,2048]{1,0:T(8,128)S(1)} custom-call(bf16[144,2048]{1,0:T(8,128)(2,1)S(1)} %collective-permute-done.halo_ref, bf16[256,2048]{1,0:T(8,128)(2,1)S(1)} %copy-done.3, bf16[256,2048]{1,0:T(8,128)(2,1)S(1)} %copy-done.4, bf16[4096,256]{1,0:T(8,128)(2,1)S(1)} %get-tuple-element.38.table_ref), custom_call_target="tpu_custom_call" | custom-call | flops 2000000000 | tf_op jit(solution)/shard_map/wide_gated/pallas_call | solution.py:60
  26.0 0.0 collective-permute-done.2.rest_1_
  26.1 0.9 %head_rows.1 = bf16[144,2048]{1,0:T(8,128)(2,1)S(1)} custom-call(bf16[256,2048]{1,0:T(8,128)(2,1)S(1)} %copy-done, bf16[256,2048]{1,0:T(8,128)(2,1)S(1)} %copy-done.1, f32[160,2048]{1,0:T(8,128)S(1)} %get-tuple-element.42.medium_low_ref.medium_ref, f32[1,2048]{1,0:T(1,128)S(1)} %bitcast.7, f32[2,256]{1,0:T(2,128)S(1)} %pair_sums.1.rest_0_, ...), custom_call_target="tpu_custom_call" | custom-call | flops 900000000 | tf_op jit(solution)/shard_map/head_rows/pallas_call | solution.py:60
  26.9 3.1 %collective-permute-start.3 = (bf16[144,2048]{1,0:T(8,128)(2,1)S(1)}, bf16[144,2048]{1,0:T(8,128)(2,1)S(1)}, u32[]{:S(2)}, u32[]{:S(2)}) collective-permute-start(bf16[144,2048]{1,0:T(8,128)(2,1)S(1)} %head_rows.1), channel_id=1, source_target_pairs={{4,0},{8,4},{12,8},{16,12},{20,16},{24,20},{28,24},{32,28},{36,32}... | collective-permute-start | bytes 1769480 | tf_op jit(solution)/shard_map/ppermute | solution.py:74
  30.1 6.1 %gradients.1 = (bf16[256,2048]{1,0:T(8,128)(2,1)}, bf16[256,2048]{1,0:T(8,128)(2,1)S(1)}, f32[256,128]{1,0:T(8,128)}) custom-call(bf16[256,2048]{1,0:T(8,128)(2,1)S(1)} %copy-done, bf16[256,2048]{1,0:T(8,128)(2,1)S(1)} %copy-done.1, f32[160,2048]{1,0:T(8,128)S(1)} %get-tuple-element.42.medium_low_ref.medium_ref, ...), custom_call_target="tpu_custom_call" | custom-call | flops 6600000000 | tf_op jit(solution)/shard_map/gradients/pallas_call | solution.py:60
  36.2 0.0 copy-start.8
  36.2 1.0 %copy-done.8 = bf16[256,2048]{1,0:T(8,128)(2,1)} copy-done((bf16[256,2048]{1,0:T(8,128)(2,1)}, bf16[256,2048]{1,0:T(8,128)(2,1)S(1)}, u32[]{:S(2)}) %copy-start.8) | copy-done | bytes 1048600
  37.1 4.9 %all-to-all-start = ((f32[8,32,128]{2,1,0:T(8,128)}), f32[8,32,128]{2,1,0:T(8,128)S(1)}, u32[]{:S(2)}, u32[]{:S(2)}) async-start(f32[8,32,128]{2,1,0:T(8,128)} %bitcast.1), calls=%async_computation | async-start | bytes 262144 | tf_op jit(solution)/shard_map/all_to_all | solution.py:562
  42.1 0.0 collective-permute-done.3.halo_ref
  42.1 0.0 copy-start.9
  42.1 0.8 %copy-done.9 = bf16[144,2048]{1,0:T(8,128)(2,1)} copy-done((bf16[144,2048]{1,0:T(8,128)(2,1)}, bf16[144,2048]{1,0:T(8,128)(2,1)S(1)}, u32[]{:S(2)}) %copy-start.9) | copy-done | bytes 589848
  42.9 4.2 %backward.2 = (bf16[256,2048]{1,0:T(8,128)(2,1)}, bf16[256,2048]{1,0:T(8,128)(2,1)}) custom-call(bf16[256,2048]{1,0:T(8,128)(2,1)} %copy-done.8, bf16[144,2048]{1,0:T(8,128)(2,1)} %copy-done.9, bf16[7,2048]{1,0:T(8,128)(2,1)} %se_ref.7, bf16[256,2048]{1,0:T(8,128)(2,1)} %key_ref.11, bf16[256,2048]{1,0:T(8,128)(2,1)} %value_ref.11, bf16[4096,256]{1,0:T(8,128)(2,1)} %copy-done.7), custom_call_target="tpu_custom_call" | custom-call | flops 3500000000 | tf_op jit(solution)/shard_map/backward/pallas_call | solution.py:488
  47.1 0.3 all-to-all-done
  47.4 0.7 broadcast_in_dim.7
  48.0 10.4 %all-to-all-start.1 = ((f32[8,32,128]{2,1,0:T(8,128)}), f32[8,32,128]{2,1,0:T(8,128)S(1)}, u32[]{:S(2)}, u32[]{:S(2)}) async-start(f32[8,32,128]{2,1,0:T(8,128)} %broadcast_in_dim.7), calls=%async_computation.1 | async-start | bytes 262144 | tf_op jit(solution)/shard_map/all_to_all | solution.py:554
  58.4 4.2 %backward.3 = (bf16[256,2048]{1,0:T(8,128)(2,1)}, bf16[256,2048]{1,0:T(8,128)(2,1)}) custom-call(bf16[256,2048]{1,0:T(8,128)(2,1)} %copy-done.8, bf16[144,2048]{1,0:T(8,128)(2,1)} %copy-done.9, bf16[7,2048]{1,0:T(8,128)(2,1)} %se_ref.7, bf16[256,2048]{1,0:T(8,128)(2,1)} %key_ref.11, ...), custom_call_target="tpu_custom_call", output_to_operand_aliasing={{0}: (6, {}), {1}: (7, {})} | custom-call | flops 3500000000 | tf_op jit(solution)/shard_map/backward/pallas_call | solution.py:488
  62.6 3.6 %all-to-all-done.1 = f32[8,32,128]{2,1,0:T(8,128)S(1)} async-done(((f32[8,32,128]{2,1,0:T(8,128)}), f32[8,32,128]{2,1,0:T(8,128)S(1)}, u32[]{:S(2)}, u32[]{:S(2)}) %all-to-all-start.1) | async-done | bytes 131104 | tf_op jit(solution)/shard_map/all_to_all | solution.py:554
  66.3 11.4 %all_to_all.15 = f32[8,32,128]{2,1,0:T(8,128)S(1)} all-to-all(f32[8,32,128]{2,1,0:T(8,128)S(1)} %broadcast_in_dim.8), channel_id=1, replica_groups={{0,4,8,12,16,20,24,28},{32,36,40,44,48,52,56,60},{64,68,72,76,80,84,88,..., dimensions={0} | all-to-all | bytes 262144 | tf_op jit(solution)/shard_map/all_to_all | solution.py:554
  77.8 0.9 %finish.1 = (f32[128,128]{1,0:T(8,128)}, f32[7,2048]{1,0:T(8,128)}, f32[1,2048]{1,0:T(1,128)}) custom-call(f32[256,128]{1,0:T(8,128)S(1)} %bitcast.4), custom_call_target="tpu_custom_call" | custom-call | flops 900000000 | tf_op jit(solution)/shard_map/finish/pallas_call | solution.py:531
  (4 shorter events, 0.0 us)
Async XLA Ops:
  0.6 7.1 %copy-start.5 = (bf16[128,128]{1,0:T(8,128)(2,1)S(1)}, bf16[128,128]{1,0:T(8,128)(2,1)}, u32[]{:S(2)}) copy-start(bf16[128,128]{1,0:T(8,128)(2,1)} %taps_ref.1) | copy-start | bytes 98308
  2.9 8.6 %copy-start = (bf16[256,2048]{1,0:T(8,128)(2,1)S(1)}, bf16[256,2048]{1,0:T(8,128)(2,1)}, u32[]{:S(2)}) copy-start(bf16[256,2048]{1,0:T(8,128)(2,1)} %query_ref.7) | copy-start | bytes 3145732
  2.9 8.6 %copy-start.1 = (bf16[256,2048]{1,0:T(8,128)(2,1)S(1)}, bf16[256,2048]{1,0:T(8,128)(2,1)}, u32[]{:S(2)}) copy-start(bf16[256,2048]{1,0:T(8,128)(2,1)} %out_grad_ref.7) | copy-start | bytes 3145732
  2.9 8.6 %copy-start.2 = (f32[2048]{0:T(1024)S(1)}, f32[2048]{0:T(1024)}, u32[]{:S(2)}) copy-start(f32[2048]{0:T(1024)} %param.13) | copy-start | bytes 24580
  3.0 8.6 %copy-start.3 = (bf16[256,2048]{1,0:T(8,128)(2,1)S(1)}, bf16[256,2048]{1,0:T(8,128)(2,1)}, u32[]{:S(2)}) copy-start(bf16[256,2048]{1,0:T(8,128)(2,1)} %key_ref.11) | copy-start | bytes 3145732
  3.0 8.6 %copy-start.4 = (bf16[256,2048]{1,0:T(8,128)(2,1)S(1)}, bf16[256,2048]{1,0:T(8,128)(2,1)}, u32[]{:S(2)}) copy-start(bf16[256,2048]{1,0:T(8,128)(2,1)} %value_ref.11) | copy-start | bytes 3145732
  3.0 8.6 %copy-start.6 = (bf16[7,2048]{1,0:T(8,128)(2,1)S(1)}, bf16[7,2048]{1,0:T(8,128)(2,1)}, u32[]{:S(2)}) copy-start(bf16[7,2048]{1,0:T(8,128)(2,1)} %se_ref.7) | copy-start | bytes 86020
  3.0 12.8 %collective-permute-start = (bf16[144,2048]{1,0:T(8,128)(2,1)}, bf16[144,2048]{1,0:T(8,128)(2,1)S(1)}, u32[]{:S(2)}, u32[]{:S(2)}) collective-permute-start(bf16[144,2048]{1,0:T(8,128)(2,1)} %tail_rows.1), channel_id=1, source_target_pairs={{0,4},{4,8},{8,12},{12,16},{16,20},{20,24},{24,28},{28,32},{32,36}... | collective-permute-start | bytes 1769480 | tf_op jit(solution)/shard_map/ppermute | solution.py:74
  10.2 1.3 %copy-start.7 = (bf16[4096,256]{1,0:T(8,128)(2,1)}, bf16[4096,256]{1,0:T(8,128)(2,1)S(1)}, u32[]{:S(2)}) copy-start(bf16[4096,256]{1,0:T(8,128)(2,1)S(1)} %get-tuple-element.53.table_ref) | copy-start | bytes 6291460
  18.7 2.5 %collective-permute-start.1 = (f32[2,256]{1,0:T(2,128)S(1)}, f32[2,256]{1,0:T(2,128)S(1)}, u32[]{:S(2)}, u32[]{:S(2)}) collective-permute-start(f32[2,256]{1,0:T(2,128)S(1)} %get-tuple-element.45.one_ref), channel_id=1, source_target_pairs={{0,1},{1,0},{2,3},{3,2},{4,5},{5,4},{6,7},{7,6},{8,9},{9,8},{10,11... | collective-permute-start | bytes 6152 | tf_op jit(solution)/shard_map/ppermute | solution.py:549
  21.3 4.8 %collective-permute-start.2 = (f32[2,256]{1,0:T(2,128)S(1)}, f32[2,256]{1,0:T(2,128)S(1)}, u32[]{:S(2)}, u32[]{:S(2)}) collective-permute-start(f32[2,256]{1,0:T(2,128)S(1)} %pair_sums.1.rest_0_), channel_id=1, source_target_pairs={{0,3},{1,2},{2,1},{3,0},{4,7},{5,6},{6,5},{7,4},{8,11},{9,10},{10,... | collective-permute-start | bytes 6152 | tf_op jit(solution)/shard_map/ppermute | solution.py:549
  26.9 15.1 %collective-permute-start.3 = (bf16[144,2048]{1,0:T(8,128)(2,1)S(1)}, bf16[144,2048]{1,0:T(8,128)(2,1)S(1)}, u32[]{:S(2)}, u32[]{:S(2)}) collective-permute-start(bf16[144,2048]{1,0:T(8,128)(2,1)S(1)} %head_rows.1), channel_id=1, source_target_pairs={{4,0},{8,4},{12,8},{16,12},{20,16},{24,20},{28,24},{32,28},{36,32}... | collective-permute-start | bytes 1769480 | tf_op jit(solution)/shard_map/ppermute | solution.py:74
  36.2 1.0 %copy-start.8 = (bf16[256,2048]{1,0:T(8,128)(2,1)}, bf16[256,2048]{1,0:T(8,128)(2,1)S(1)}, u32[]{:S(2)}) copy-start(bf16[256,2048]{1,0:T(8,128)(2,1)S(1)} %get-tuple-element.52.grad_ref) | copy-start | bytes 3145732
  37.1 10.2 %all-to-all-start = ((f32[8,32,128]{2,1,0:T(8,128)}), f32[8,32,128]{2,1,0:T(8,128)S(1)}, u32[]{:S(2)}, u32[]{:S(2)}) async-start(f32[8,32,128]{2,1,0:T(8,128)} %bitcast.1), calls=%async_computation | async-start | bytes 262144 | tf_op jit(solution)/shard_map/all_to_all | solution.py:562
  42.1 0.8 %copy-start.9 = (bf16[144,2048]{1,0:T(8,128)(2,1)}, bf16[144,2048]{1,0:T(8,128)(2,1)S(1)}, u32[]{:S(2)}) copy-start(bf16[144,2048]{1,0:T(8,128)(2,1)S(1)} %collective-permute-done.3.halo_ref) | copy-start | bytes 1769476
  48.0 18.3 %all-to-all-start.1 = ((f32[8,32,128]{2,1,0:T(8,128)}), f32[8,32,128]{2,1,0:T(8,128)S(1)}, u32[]{:S(2)}, u32[]{:S(2)}) async-start(f32[8,32,128]{2,1,0:T(8,128)} %broadcast_in_dim.7), calls=%async_computation.1 | async-start | bytes 262144 | tf_op jit(solution)/shard_map/all_to_all | solution.py:554

commit v5 on v4

--- a/solution.py
+++ b/solution.py
@@ -30,23 +30,26 @@
 PARTS = 2
 NEAR = 8
 VMEM = pl.BlockSpec(memory_space=pltpu.VMEM)
+HBM = pl.BlockSpec(memory_space=pltpu.HBM)
 
 
 def params(limit=24):
-    return pltpu.CompilerParams(vmem_limit_bytes=limit * 1024 * 1024)
+    return pltpu.CompilerParams(vmem_limit_bytes=int(limit * 1024 * 1024))
 
 
 def cost(micros):
     return pl.CostEstimate(flops=int(micros * 1e9), bytes_accessed=0, transcendentals=0)
 
 
-def each_tile(channels, body):
+def each_tile(channels, body, after=None):
     unroll = min(UNROLL, channels // LANES)
 
     def step(i, carry):
         for slot in range(unroll):
             tile = i * unroll + slot
             body(pl.ds(pl.multiple_of(tile * LANES, LANES), LANES), tile, slot)
+        if after is not None:
+            after(i)
         return carry
 
     lax.fori_loop(0, channels // LANES // unroll, step, 0)
@@ -56,12 +59,15 @@
     return pl.ds(pl.multiple_of(tile * rows, rows), rows)
 
 
-def call(body, name, micros, outs, scratch, *args):
+def call(body, name, micros, outs, scratch, *args, out_specs=None):
     return pl.pallas_call(
         body,
         in_specs=[VMEM] * len(args),
-        out_specs=[VMEM] * len(outs),
-        out_shape=[jax.ShapeDtypeStruct(shape, dtype) for shape, dtype in outs],
+        out_specs=out_specs or [VMEM] * len(outs),
+        out_shape=[
+            (pltpu.HBM if out_specs and spec is HBM else jax.ShapeDtypeStruct)(shape, dtype)
+            for (shape, dtype), spec in zip(outs, out_specs or [VMEM] * len(outs))
+        ],
         scratch_shapes=scratch,
         compiler_params=params(),
         cost_estimate=cost(micros),
@@ -94,7 +100,7 @@
     return results
 
 
-def table_kernel(taps_ref, front_out, back_out, rows_ref):
+def table_kernel(taps_ref, front_out, back_out, rows_ref, back_ref, sem):
     taps = taps_ref[...]
     row_ids = lax.broadcasted_iota(jnp.int32, (MR_LEN, 2 * LANES), 0)
     col_ids = lax.broadcasted_iota(jnp.int32, (MR_LEN, 2 * LANES), 1)
@@ -102,23 +108,34 @@
         pick = jnp.where(col_ids == place, 1.0, 0.0).astype(BF16)
         rows_ref[n] = lax.dot_general(taps, pick, (((0,), (0,)), ((), ())), preferred_element_type=F32)
 
-    def one(g, carry):
-        for n, target in enumerate((front_out, back_out)):
+    def fill(n, target):
+        def one(g, carry):
             rows = rows_ref[n, of_tile(g, GT), :]
             for k in range(GT):
                 row = jnp.broadcast_to(rows[k : k + 1, :], (S, 2 * LANES))
                 turned = pltpu.roll(row, 0, 1, stride=1, stride_axis=0).astype(BF16)
                 target[of_tile(g * GT + k, S), :] = turned
-        return carry
-
-    lax.fori_loop(0, taps_ref.shape[1] // GT, one, 0)
+            return carry
+
+        lax.fori_loop(0, taps_ref.shape[1] // GT, one, 0)
+
+    fill(1, back_ref)
+    copy = pltpu.make_async_copy(back_ref, back_out, sem)
+    copy.start()
+    fill(0, front_out)
+    copy.wait()
 
 
 def tables(mr_filter):
     groups = mr_filter.shape[1]
     shape = ((groups * S, 2 * LANES), BF16)
-    scratch = [pltpu.VMEM((2, groups, 2 * LANES), F32)]
-    return call(table_kernel, "filter_tables", 2.4, [shape, shape], scratch, mr_filter)
+    scratch = [
+        pltpu.VMEM((2, groups, 2 * LANES), F32),
+        pltpu.VMEM((groups * S, 2 * LANES), BF16),
+        pltpu.SemaphoreType.DMA,
+    ]
+    specs = [VMEM, HBM]
+    return call(table_kernel, "filter_tables", 2.4, [shape, shape], scratch, mr_filter, out_specs=specs)
 
 
 def short_filter(se_ref, at, gated_ref, first, rows):
@@ -154,17 +171,16 @@
 
 def tail_rows(key_in, value_in):
     channels = key_in.shape[1]
-    anywhere = pl.BlockSpec(memory_space=pltpu.HBM)
     return pl.pallas_call(
         tail_kernel,
-        in_specs=[anywhere, anywhere],
+        in_specs=[HBM, HBM],
         out_specs=VMEM,
-        out_shape=jax.ShapeDtypeStruct((HALO, channels), BF16),
+        out_shape=pltpu.VMEM((HALO, channels), BF16),
         scratch_shapes=[
             pltpu.VMEM((2, HALO, channels), BF16),
             pltpu.SemaphoreType.DMA((2, TAIL_PARTS)),
         ],
-        compiler_params=params(63),
+        compiler_params=params(62),
         cost_estimate=cost(1.2),
         name="tail_rows",
     )(key_in, value_in)
@@ -373,9 +389,22 @@
     wide_high_ref,
     *rest,
 ):
-    query_grad_out, medium_grad_out, packed_out, scale_ref, slope_ref, cross_ref, wide_ref = rest[-7:]
+    *sums, query_grad_out, medium_grad_out, packed_out, scale_ref, slope_ref, cross_ref, wide_ref, held_ref, sems = rest
     tok, channels = query_ref.shape
-    spread_sums(rest[:-7], scale_ref, slope_ref, tok)
+    spread_sums(sums, scale_ref, slope_ref, tok)
+    width = UNROLL * LANES
+
+    def copies(i):
+        at = of_tile(i, width)
+        return [
+            pltpu.make_async_copy(held_ref.at[n, :, at], target.at[:, at], sems.at[n, i])
+            for n, target in enumerate((query_grad_out, medium_grad_out))
+        ]
+
+    def leave(i):
+        for copy in copies(i):
+            copy.start()
+
     blocks = tok // SG
     side = GT * SG
 
@@ -387,9 +416,9 @@
         norm_grad = out_grad * gain_ref[:, at]
         mixed = query * medium
         mixed_grad = inv * norm_grad - mixed * slope_ref[...]
-        query_grad_out[:, at] = (mixed_grad * medium).astype(BF16)
+        held_ref[0, :, at] = (mixed_grad * medium).astype(BF16)
         medium_grad = (mixed_grad * query).astype(BF16)
-        medium_grad_out[:, at] = medium_grad
+        held_ref[1, :, at] = medium_grad
         gain_row = jnp.sum(out_grad * mixed * inv, axis=0, keepdims=True)
         wide_grad = medium_grad.astype(F32)
         rows = wide_ref.at[slot]
@@ -420,7 +449,10 @@
             [total[:, :LANES]] + lines + [gain_row], axis=0
         )
 
-    each_tile(channels, body)
+    each_tile(channels, body, leave)
+    for i in range(channels // width):
+        for copy in copies(i):
+            copy.wait()
 
 
 def grads(sums, query, out_grad, medium_low, medium_high, gain, short_low, short_high, wide_low, wide_high):
@@ -435,6 +467,8 @@
         pltpu.VMEM((tok, LANES), F32),
         pltpu.VMEM((UNROLL, 2 * GT * SG, LANES), F32),
         pltpu.VMEM((UNROLL, tok + S, LANES), F32),
+        pltpu.VMEM((2, tok, channels), BF16),
+        pltpu.SemaphoreType.DMA((2, channels // LANES // UNROLL)),
     ]
     return call(
         grads_kernel,
@@ -452,6 +486,7 @@
         wide_low,
         wide_high,
         *sums,
+        out_specs=[HBM, HBM, VMEM],
     )
 
 
@@ -496,7 +531,7 @@
             col(tok),
             pl.BlockSpec((tiles * GT * S, 2 * LANES), lambda i: (first + i, 0)),
         ]
-        + [pl.BlockSpec(memory_space=pltpu.HBM)] * len(done),
+        + [HBM] * len(done),
         out_specs=[col(tok), col(tok)],
         out_shape=[shape, shape],
         scratch_shapes=[

time: 79.1 us -> 77.9 us (0.985)
  local copies, waits for them, and re-layouts: 3.83 us -> 1.53 us
  Pallas kernels: 30.1 us -> 31.1 us
    unnamed x20 -> x16, local copies, waits for them, and re-layouts: 3.15 us -> 0.85 us
    pallas_call x8, Pallas kernels: 20.8 us -> 21.8 us  [the longest x7 20.3 us: call(): pl.pallas_call(body, in_specs=[VMEM] * len(args), out_specs=out_specs or...]
  transfers between devices with their start and end apart: 6 -> 6, of which waited for: 3 -> 3; matrix products, arithmetic and copies ran while one was open for 0% -> 0% of each run, Pallas kernels for 29% -> 32%
where the time goes in v5:
time: 77.9 us; the launch traced here: 77.5 us
  Pallas kernels  31.1 us (40%)
  starting transfers between devices  27.5 us (35%)
  blocking collectives  11.4 us (15%)
  waiting for transfers between devices  5.05 us (6%)
  local copies, waits for them, and re-layouts  1.53 us (2%)
  between operations  0.84 us (1%)
    pallas_call x7, Pallas kernels, call(): pl.pallas_call(body, in_specs=[VMEM] * len(args), out_specs=out_specs or...  20.3 us
    all_to_all x1, blocking collectives, spread(): return lax.all_to_all(everyone, 'ctx', 0, 0, axis_index_groups=groups)  11.4 us
    all_to_all x1, starting transfers between devices, spread(): return lax.all_to_all(everyone, 'ctx', 0, 0, axis_index_groups=groups)  10.4 us
    pallas_call x2, Pallas kernels, backward(): pl.pallas_call(backward_kernel, grid=(steps,), in_specs=[col(tok), col(HA...  8.41 us
    ppermute x2, starting transfers between devices, shifted(): lax.ppermute(x, 'ctx', [(i, i + by) for i in range(peers) if 0 <= i + by...  7.92 us
    all_to_all x1, starting transfers between devices, sum_over_ctx(): arrived = lax.all_to_all(parts, 'ctx', 0, 0, axis_index_groups=near)  5.02 us
    ppermute x2, starting transfers between devices, pair_up(): lax.ppermute(x, 'tp', [(i, partner(i)) for i in range(lax.axis_size('tp'))])  4.11 us
    all_to_all x1, waiting for transfers between devices, spread(): return lax.all_to_all(everyone, 'ctx', 0, 0, axis_index_groups=groups)  3.64 us
  transfers between devices with their start and end apart: 6, of which 3 were waited for; matrix products, arithmetic and copies ran while one was open for 0% of the time, Pallas kernels for 32%

profile of v5, /device:TPU:1, one launch (start us, length us, event | category | flops | bytes accessed | tf_op | source)
XLA Modules:
  0.0 77.5 jit_solution(18399662155991218342)
XLA Ops:
  0.6 0.0 copy-start.5
  0.6 1.5 %tail_rows.1 = bf16[144,2048]{1,0:T(8,128)(2,1)S(1)} custom-call(bf16[256,2048]{1,0:T(8,128)(2,1)} %key_ref.11, bf16[256,2048]{1,0:T(8,128)(2,1)} %value_ref.11), custom_call_target="tpu_custom_call" | custom-call | flops 1200000000 | tf_op jit(solution)/shard_map/tail_rows/pallas_call | solution.py:174
  2.1 0.0 copy-start
  2.1 0.0 copy-start.1
  2.1 0.0 copy-start.2
  2.1 0.0 copy-start.3
  2.2 0.0 copy-start.4
  2.2 0.0 copy-start.6
  2.2 4.8 %collective-permute-start = (bf16[144,2048]{1,0:T(8,128)(2,1)S(1)}, bf16[144,2048]{1,0:T(8,128)(2,1)S(1)}, u32[]{:S(2)}, u32[]{:S(2)}) collective-permute-start(bf16[144,2048]{1,0:T(8,128)(2,1)S(1)} %tail_rows.1), channel_id=1, source_target_pairs={{0,4},{4,8},{8,12},{12,16},{16,20},{20,24},{24,28},{28,32},{32,36}... | collective-permute-start | bytes 1769480 | tf_op jit(solution)/shard_map/ppermute | solution.py:80
  7.0 0.0 copy-done.5
  7.0 3.5 %filter_tables.1 = (bf16[4096,256]{1,0:T(8,128)(2,1)S(1)}, bf16[4096,256]{1,0:T(8,128)(2,1)}) custom-call(bf16[128,128]{1,0:T(8,128)(2,1)S(1)} %copy-done.5), custom_call_target="tpu_custom_call" | custom-call | flops 2400000000 | tf_op jit(solution)/shard_map/filter_tables/pallas_call | solution.py:63
  10.5 0.0 copy-done
  10.5 0.0 copy-done.1
  10.5 0.0 copy-done.2
  10.6 0.0 copy-done.3
  10.6 0.0 copy-done.4
  10.6 0.0 copy-done.6
  10.6 4.1 %early.1 = (f32[96,2048]{1,0:T(8,128)S(1)}, bf16[256,2048]{1,0:T(8,128)(2,1)S(1)}, f32[128,2048]{1,0:T(8,128)S(1)}, f32[96,128]{1,0:T(8,128)S(1)}, f32[96,128]{1,0:T(8,128)S(1)}) custom-call(bf16[256,2048]{1,0:T(8,128)(2,1)S(1)} %copy-done.3, bf16[256,2048]{1,0:T(8,128)(2,1)S(1)} %copy-done.4, bf16[256,2048]{1,0:T(8,128)(2,1)S(1)} %copy-done, ...), custom_call_target="tpu_custom_call" | custom-call | flops 4200000000 | tf_op jit(solution)/shard_map/early/pallas_call | solution.py:63
  14.7 0.0 collective-permute-done.halo_ref
  14.7 2.9 %late.1 = (f32[160,2048]{1,0:T(8,128)S(1)}, bf16[160,2048]{1,0:T(8,128)(2,1)S(1)}, f32[2,256]{1,0:T(2,128)S(1)}) custom-call(bf16[144,2048]{1,0:T(8,128)(2,1)S(1)} %collective-permute-done.halo_ref, bf16[256,2048]{1,0:T(8,128)(2,1)S(1)} %copy-done.3, bf16[256,2048]{1,0:T(8,128)(2,1)S(1)} %copy-done.4, bf16[256,2048]{1,0:T(8,128)(2,1)S(1)} %copy-done, ...), custom_call_target="tpu_custom_call" | custom-call | flops 2900000000 | tf_op jit(solution)/shard_map/late/pallas_call | solution.py:63
  17.6 1.4 %collective-permute-start.1 = (f32[2,256]{1,0:T(2,128)S(1)}, f32[2,256]{1,0:T(2,128)S(1)}, u32[]{:S(2)}, u32[]{:S(2)}) collective-permute-start(f32[2,256]{1,0:T(2,128)S(1)} %get-tuple-element.45.one_ref), channel_id=1, source_target_pairs={{0,1},{1,0},{2,3},{3,2},{4,5},{5,4},{6,7},{7,6},{8,9},{9,8},{10,11... | collective-permute-start | bytes 6152 | tf_op jit(solution)/shard_map/ppermute | solution.py:584
  19.0 1.1 %collective-permute-done.1.other_ref = f32[2,256]{1,0:T(2,128)S(1)} collective-permute-done((f32[2,256]{1,0:T(2,128)S(1)}, f32[2,256]{1,0:T(2,128)S(1)}, u32[]{:S(2)}, u32[]{:S(2)}) %collective-permute-start.1) | collective-permute-done | bytes 2080 | tf_op jit(solution)/shard_map/ppermute | solution.py:584
  20.1 2.7 %collective-permute-start.2 = (f32[2,256]{1,0:T(2,128)S(1)}, f32[2,256]{1,0:T(2,128)S(1)}, u32[]{:S(2)}, u32[]{:S(2)}) collective-permute-start(f32[2,256]{1,0:T(2,128)S(1)} %pair_sums.1.rest_0_), channel_id=1, source_target_pairs={{0,3},{1,2},{2,1},{3,0},{4,7},{5,6},{6,5},{7,4},{8,11},{9,10},{10,... | collective-permute-start | bytes 6152 | tf_op jit(solution)/shard_map/ppermute | solution.py:584
  22.9 2.0 %wide_gated.1.wide_low_ref = f32[160,2048]{1,0:T(8,128)S(1)} custom-call(bf16[144,2048]{1,0:T(8,128)(2,1)S(1)} %collective-permute-done.halo_ref, bf16[256,2048]{1,0:T(8,128)(2,1)S(1)} %copy-done.3, bf16[256,2048]{1,0:T(8,128)(2,1)S(1)} %copy-done.4, bf16[4096,256]{1,0:T(8,128)(2,1)S(1)} %get-tuple-element.38.table_ref), custom_call_target="tpu_custom_call" | custom-call | flops 2000000000 | tf_op jit(solution)/shard_map/wide_gated/pallas_call | solution.py:63
  24.9 0.0 collective-permute-done.2.rest_1_
  24.9 0.9 %head_rows.1 = bf16[144,2048]{1,0:T(8,128)(2,1)S(1)} custom-call(bf16[256,2048]{1,0:T(8,128)(2,1)S(1)} %copy-done, bf16[256,2048]{1,0:T(8,128)(2,1)S(1)} %copy-done.1, f32[160,2048]{1,0:T(8,128)S(1)} %get-tuple-element.42.medium_low_ref.medium_ref, f32[1,2048]{1,0:T(1,128)S(1)} %bitcast.7, f32[2,256]{1,0:T(2,128)S(1)} %pair_sums.1.rest_0_, ...), custom_call_target="tpu_custom_call" | custom-call | flops 900000000 | tf_op jit(solution)/shard_map/head_rows/pallas_call | solution.py:63
  25.8 3.1 %collective-permute-start.3 = (bf16[144,2048]{1,0:T(8,128)(2,1)S(1)}, bf16[144,2048]{1,0:T(8,128)(2,1)S(1)}, u32[]{:S(2)}, u32[]{:S(2)}) collective-permute-start(bf16[144,2048]{1,0:T(8,128)(2,1)S(1)} %head_rows.1), channel_id=1, source_target_pairs={{4,0},{8,4},{12,8},{16,12},{20,16},{24,20},{28,24},{32,28},{36,32}... | collective-permute-start | bytes 1769480 | tf_op jit(solution)/shard_map/ppermute | solution.py:80
  28.9 6.9 %gradients.1 = (bf16[256,2048]{1,0:T(8,128)(2,1)}, bf16[256,2048]{1,0:T(8,128)(2,1)}, f32[256,128]{1,0:T(8,128)}) custom-call(bf16[256,2048]{1,0:T(8,128)(2,1)S(1)} %copy-done, bf16[256,2048]{1,0:T(8,128)(2,1)S(1)} %copy-done.1, f32[160,2048]{1,0:T(8,128)S(1)} %get-tuple-element.42.medium_low_ref.medium_ref, ...), custom_call_target="tpu_custom_call" | custom-call | flops 6600000000 | tf_op jit(solution)/shard_map/gradients/pallas_call | solution.py:63
  35.8 5.0 %all-to-all-start = ((f32[8,32,128]{2,1,0:T(8,128)}), f32[8,32,128]{2,1,0:T(8,128)S(1)}, u32[]{:S(2)}, u32[]{:S(2)}) async-start(f32[8,32,128]{2,1,0:T(8,128)} %bitcast.1), calls=%async_computation | async-start | bytes 262144 | tf_op jit(solution)/shard_map/all_to_all | solution.py:597
  40.9 0.0 collective-permute-done.3.halo_ref
  40.9 0.0 copy-start.7
  40.9 0.8 %copy-done.7 = bf16[144,2048]{1,0:T(8,128)(2,1)} copy-done((bf16[144,2048]{1,0:T(8,128)(2,1)}, bf16[144,2048]{1,0:T(8,128)(2,1)S(1)}, u32[]{:S(2)}) %copy-start.7) | copy-done | bytes 589848
  41.7 4.2 %backward.2 = (bf16[256,2048]{1,0:T(8,128)(2,1)}, bf16[256,2048]{1,0:T(8,128)(2,1)}) custom-call(bf16[256,2048]{1,0:T(8,128)(2,1)} %get-tuple-element.52.grad_ref, bf16[144,2048]{1,0:T(8,128)(2,1)} %copy-done.7, bf16[7,2048]{1,0:T(8,128)(2,1)} %se_ref.7, bf16[256,2048]{1,0:T(8,128)(2,1)} %key_ref.11, bf16[256,2048]{1,0:T(8,128)(2,1)} %value_ref.11, ...), custom_call_target="tpu_custom_call" | custom-call | flops 3500000000 | tf_op jit(solution)/shard_map/backward/pallas_call | solution.py:523
  45.9 0.3 all-to-all-done
  46.1 0.7 broadcast_in_dim.7
  46.8 10.4 %all-to-all-start.1 = ((f32[8,32,128]{2,1,0:T(8,128)}), f32[8,32,128]{2,1,0:T(8,128)S(1)}, u32[]{:S(2)}, u32[]{:S(2)}) async-start(f32[8,32,128]{2,1,0:T(8,128)} %broadcast_in_dim.7), calls=%async_computation.1 | async-start | bytes 262144 | tf_op jit(solution)/shard_map/all_to_all | solution.py:589
  57.2 4.2 %backward.3 = (bf16[256,2048]{1,0:T(8,128)(2,1)}, bf16[256,2048]{1,0:T(8,128)(2,1)}) custom-call(bf16[256,2048]{1,0:T(8,128)(2,1)} %get-tuple-element.52.grad_ref, bf16[144,2048]{1,0:T(8,128)(2,1)} %copy-done.7, bf16[7,2048]{1,0:T(8,128)(2,1)} %se_ref.7, bf16[256,2048]{1,0:T(8,128)(2,1)} %key_ref.11, ...), custom_call_target="tpu_custom_call", output_to_operand_aliasing={{0}: (6, {}), {1}: (7, {})} | custom-call | flops 3500000000 | tf_op jit(solution)/shard_map/backward/pallas_call | solution.py:523
  61.4 3.6 %all-to-all-done.1 = f32[8,32,128]{2,1,0:T(8,128)S(1)} async-done(((f32[8,32,128]{2,1,0:T(8,128)}), f32[8,32,128]{2,1,0:T(8,128)S(1)}, u32[]{:S(2)}, u32[]{:S(2)}) %all-to-all-start.1) | async-done | bytes 131104 | tf_op jit(solution)/shard_map/all_to_all | solution.py:589
  65.1 11.4 %all_to_all.15 = f32[8,32,128]{2,1,0:T(8,128)S(1)} all-to-all(f32[8,32,128]{2,1,0:T(8,128)S(1)} %broadcast_in_dim.8), channel_id=1, replica_groups={{0,4,8,12,16,20,24,28},{32,36,40,44,48,52,56,60},{64,68,72,76,80,84,88,..., dimensions={0} | all-to-all | bytes 262144 | tf_op jit(solution)/shard_map/all_to_all | solution.py:589
  76.6 0.9 %finish.1 = (f32[128,128]{1,0:T(8,128)}, f32[7,2048]{1,0:T(8,128)}, f32[1,2048]{1,0:T(1,128)}) custom-call(f32[256,128]{1,0:T(8,128)S(1)} %bitcast.4), custom_call_target="tpu_custom_call" | custom-call | flops 900000000 | tf_op jit(solution)/shard_map/finish/pallas_call | solution.py:566
  (4 shorter events, 0.0 us)
Async XLA Ops:
  0.6 6.3 %copy-start.5 = (bf16[128,128]{1,0:T(8,128)(2,1)S(1)}, bf16[128,128]{1,0:T(8,128)(2,1)}, u32[]{:S(2)}) copy-start(bf16[128,128]{1,0:T(8,128)(2,1)} %taps_ref.1) | copy-start | bytes 98308
  2.1 8.4 %copy-start = (bf16[256,2048]{1,0:T(8,128)(2,1)S(1)}, bf16[256,2048]{1,0:T(8,128)(2,1)}, u32[]{:S(2)}) copy-start(bf16[256,2048]{1,0:T(8,128)(2,1)} %query_ref.7) | copy-start | bytes 3145732
  2.1 8.4 %copy-start.1 = (bf16[256,2048]{1,0:T(8,128)(2,1)S(1)}, bf16[256,2048]{1,0:T(8,128)(2,1)}, u32[]{:S(2)}) copy-start(bf16[256,2048]{1,0:T(8,128)(2,1)} %out_grad_ref.7) | copy-start | bytes 3145732
  2.1 8.4 %copy-start.2 = (f32[2048]{0:T(1024)S(1)}, f32[2048]{0:T(1024)}, u32[]{:S(2)}) copy-start(f32[2048]{0:T(1024)} %param.13) | copy-start | bytes 24580
  2.1 8.4 %copy-start.3 = (bf16[256,2048]{1,0:T(8,128)(2,1)S(1)}, bf16[256,2048]{1,0:T(8,128)(2,1)}, u32[]{:S(2)}) copy-start(bf16[256,2048]{1,0:T(8,128)(2,1)} %key_ref.11) | copy-start | bytes 3145732
  2.2 8.4 %copy-start.4 = (bf16[256,2048]{1,0:T(8,128)(2,1)S(1)}, bf16[256,2048]{1,0:T(8,128)(2,1)}, u32[]{:S(2)}) copy-start(bf16[256,2048]{1,0:T(8,128)(2,1)} %value_ref.11) | copy-start | bytes 3145732
  2.2 8.4 %copy-start.6 = (bf16[7,2048]{1,0:T(8,128)(2,1)S(1)}, bf16[7,2048]{1,0:T(8,128)(2,1)}, u32[]{:S(2)}) copy-start(bf16[7,2048]{1,0:T(8,128)(2,1)} %se_ref.7) | copy-start | bytes 86020
  2.2 12.6 %collective-permute-start = (bf16[144,2048]{1,0:T(8,128)(2,1)S(1)}, bf16[144,2048]{1,0:T(8,128)(2,1)S(1)}, u32[]{:S(2)}, u32[]{:S(2)}) collective-permute-start(bf16[144,2048]{1,0:T(8,128)(2,1)S(1)} %tail_rows.1), channel_id=1, source_target_pairs={{0,4},{4,8},{8,12},{12,16},{16,20},{20,24},{24,28},{28,32},{32,36}... | collective-permute-start | bytes 1769480 | tf_op jit(solution)/shard_map/ppermute | solution.py:80
  17.6 2.5 %collective-permute-start.1 = (f32[2,256]{1,0:T(2,128)S(1)}, f32[2,256]{1,0:T(2,128)S(1)}, u32[]{:S(2)}, u32[]{:S(2)}) collective-permute-start(f32[2,256]{1,0:T(2,128)S(1)} %get-tuple-element.45.one_ref), channel_id=1, source_target_pairs={{0,1},{1,0},{2,3},{3,2},{4,5},{5,4},{6,7},{7,6},{8,9},{9,8},{10,11... | collective-permute-start | bytes 6152 | tf_op jit(solution)/shard_map/ppermute | solution.py:584
  20.1 4.8 %collective-permute-start.2 = (f32[2,256]{1,0:T(2,128)S(1)}, f32[2,256]{1,0:T(2,128)S(1)}, u32[]{:S(2)}, u32[]{:S(2)}) collective-permute-start(f32[2,256]{1,0:T(2,128)S(1)} %pair_sums.1.rest_0_), channel_id=1, source_target_pairs={{0,3},{1,2},{2,1},{3,0},{4,7},{5,6},{6,5},{7,4},{8,11},{9,10},{10,... | collective-permute-start | bytes 6152 | tf_op jit(solution)/shard_map/ppermute | solution.py:584
  25.8 15.1 %collective-permute-start.3 = (bf16[144,2048]{1,0:T(8,128)(2,1)S(1)}, bf16[144,2048]{1,0:T(8,128)(2,1)S(1)}, u32[]{:S(2)}, u32[]{:S(2)}) collective-permute-start(bf16[144,2048]{1,0:T(8,128)(2,1)S(1)} %head_rows.1), channel_id=1, source_target_pairs={{4,0},{8,4},{12,8},{16,12},{20,16},{24,20},{28,24},{32,28},{36,32}... | collective-permute-start | bytes 1769480 | tf_op jit(solution)/shard_map/ppermute | solution.py:80
  35.8 10.3 %all-to-all-start = ((f32[8,32,128]{2,1,0:T(8,128)}), f32[8,32,128]{2,1,0:T(8,128)S(1)}, u32[]{:S(2)}, u32[]{:S(2)}) async-start(f32[8,32,128]{2,1,0:T(8,128)} %bitcast.1), calls=%async_computation | async-start | bytes 262144 | tf_op jit(solution)/shard_map/all_to_all | solution.py:597
  40.9 0.8 %copy-start.7 = (bf16[144,2048]{1,0:T(8,128)(2,1)}, bf16[144,2048]{1,0:T(8,128)(2,1)S(1)}, u32[]{:S(2)}) copy-start(bf16[144,2048]{1,0:T(8,128)(2,1)S(1)} %collective-permute-done.3.halo_ref) | copy-start | bytes 1769476
  46.8 18.3 %all-to-all-start.1 = ((f32[8,32,128]{2,1,0:T(8,128)}), f32[8,32,128]{2,1,0:T(8,128)S(1)}, u32[]{:S(2)}, u32[]{:S(2)}) async-start(f32[8,32,128]{2,1,0:T(8,128)} %broadcast_in_dim.7), calls=%async_computation.1 | async-start | bytes 262144 | tf_op jit(solution)/shard_map/all_to_all | solution.py:589

commit v6 on v5

--- a/solution.py
+++ b/solution.py
@@ -27,7 +27,7 @@
 UNROLL = 8
 TAIL_PARTS = 4
 BW = 512
-PARTS = 2
+PARTS = (0, 1, 3, 4)
 NEAR = 8
 VMEM = pl.BlockSpec(memory_space=pltpu.VMEM)
 HBM = pl.BlockSpec(memory_space=pltpu.HBM)
@@ -41,15 +41,13 @@
     return pl.CostEstimate(flops=int(micros * 1e9), bytes_accessed=0, transcendentals=0)
 
 
-def each_tile(channels, body, after=None):
+def each_tile(channels, body):
     unroll = min(UNROLL, channels // LANES)
 
     def step(i, carry):
         for slot in range(unroll):
             tile = i * unroll + slot
             body(pl.ds(pl.multiple_of(tile * LANES, LANES), LANES), tile, slot)
-        if after is not None:
-            after(i)
         return carry
 
     lax.fori_loop(0, channels // LANES // unroll, step, 0)
@@ -59,14 +57,15 @@
     return pl.ds(pl.multiple_of(tile * rows, rows), rows)
 
 
-def call(body, name, micros, outs, scratch, *args, out_specs=None):
+def call(body, name, micros, outs, scratch, *args, out_specs=None, places=None):
+    out_specs = out_specs or [VMEM] * len(outs)
     return pl.pallas_call(
         body,
         in_specs=[VMEM] * len(args),
-        out_specs=out_specs or [VMEM] * len(outs),
+        out_specs=out_specs,
         out_shape=[
-            (pltpu.HBM if out_specs and spec is HBM else jax.ShapeDtypeStruct)(shape, dtype)
-            for (shape, dtype), spec in zip(outs, out_specs or [VMEM] * len(outs))
+            (pltpu.HBM if place is HBM else jax.ShapeDtypeStruct)(shape, dtype)
+            for (shape, dtype), place in zip(outs, places or out_specs)
         ],
         scratch_shapes=scratch,
         compiler_params=params(),
@@ -389,22 +388,9 @@
     wide_high_ref,
     *rest,
 ):
-    *sums, query_grad_out, medium_grad_out, packed_out, scale_ref, slope_ref, cross_ref, wide_ref, held_ref, sems = rest
+    query_grad_out, medium_grad_out, packed_out, scale_ref, slope_ref, cross_ref, wide_ref = rest[-7:]
     tok, channels = query_ref.shape
-    spread_sums(sums, scale_ref, slope_ref, tok)
-    width = UNROLL * LANES
-
-    def copies(i):
-        at = of_tile(i, width)
-        return [
-            pltpu.make_async_copy(held_ref.at[n, :, at], target.at[:, at], sems.at[n, i])
-            for n, target in enumerate((query_grad_out, medium_grad_out))
-        ]
-
-    def leave(i):
-        for copy in copies(i):
-            copy.start()
-
+    spread_sums(rest[:-7], scale_ref, slope_ref, tok)
     blocks = tok // SG
     side = GT * SG
 
@@ -416,9 +402,9 @@
         norm_grad = out_grad * gain_ref[:, at]
         mixed = query * medium
         mixed_grad = inv * norm_grad - mixed * slope_ref[...]
-        held_ref[0, :, at] = (mixed_grad * medium).astype(BF16)
+        query_grad_out[:, at] = (mixed_grad * medium).astype(BF16)
         medium_grad = (mixed_grad * query).astype(BF16)
-        held_ref[1, :, at] = medium_grad
+        medium_grad_out[:, at] = medium_grad
         gain_row = jnp.sum(out_grad * mixed * inv, axis=0, keepdims=True)
         wide_grad = medium_grad.astype(F32)
         rows = wide_ref.at[slot]
@@ -449,10 +435,7 @@
             [total[:, :LANES]] + lines + [gain_row], axis=0
         )
 
-    each_tile(channels, body, leave)
-    for i in range(channels // width):
-        for copy in copies(i):
-            copy.wait()
+    each_tile(channels, body)
 
 
 def grads(sums, query, out_grad, medium_low, medium_high, gain, short_low, short_high, wide_low, wide_high):
@@ -467,8 +450,6 @@
         pltpu.VMEM((tok, LANES), F32),
         pltpu.VMEM((UNROLL, 2 * GT * SG, LANES), F32),
         pltpu.VMEM((UNROLL, tok + S, LANES), F32),
-        pltpu.VMEM((2, tok, channels), BF16),
-        pltpu.SemaphoreType.DMA((2, channels // LANES // UNROLL)),
     ]
     return call(
         grads_kernel,
@@ -486,7 +467,7 @@
         wide_low,
         wide_high,
         *sums,
-        out_specs=[HBM, HBM, VMEM],
+        places=[HBM, HBM, VMEM],
     )
 
 
@@ -515,8 +496,7 @@
 
 def backward(medium_grad, halo, se, key_in, value_in, table, part, done=()):
     tok, channels = key_in.shape
-    steps = channels // BW // PARTS
-    first = part * steps
+    first, steps = PARTS[part], PARTS[part + 1] - PARTS[part]
     col = lambda rows: pl.BlockSpec((rows, BW), lambda i: (0, first + i))
     tiles = BW // LANES
     shape = jax.ShapeDtypeStruct((tok, channels), BF16)
@@ -540,7 +520,7 @@
         ],
         input_output_aliases={6 + n: n for n in range(len(done))},
         compiler_params=params(62),
-        cost_estimate=cost(3.5),
+        cost_estimate=cost(2.0 * steps),
         name="backward",
     )(medium_grad, halo, se, key_in, value_in, table, *done)
 
@@ -576,12 +556,9 @@
     )(packed)
 
 
-def add_kernel(one_ref, other_ref, total_out):
-    total_out[...] = one_ref[...] + other_ref[...]
-
-
-def pair_up(x, partner):
-    return lax.ppermute(x, "tp", [(i, partner(i)) for i in range(lax.axis_size("tp"))])
+def from_peers(x, axis):
+    peers = lax.axis_size(axis)
+    return [lax.ppermute(x, axis, [(i, (i + k) % peers) for i in range(peers)]) for k in range(1, peers)]
 
 
 def spread(x, groups):
@@ -599,7 +576,9 @@
     mine, done = lax.optimization_barrier((jnp.sum(arrived, axis=0), done))
     arrived = spread(mine, far)
     arrived, done = lax.optimization_barrier((arrived, beside(1, done)))
-    return spread(jnp.sum(arrived, axis=0), near).reshape(packed.shape), done
+    mine, done = lax.optimization_barrier((jnp.sum(arrived, axis=0), done))
+    everyone, done = lax.optimization_barrier((spread(mine, near), beside(2, done)))
+    return everyone.reshape(packed.shape), done
 
 
 def local(query, key_in, value_in, out_grad, mr_filter, se_filter, gain):
@@ -625,8 +604,7 @@
         square,
         inner,
     )
-    sums = call(add_kernel, "pair_sums", 0.2, [((2, tok), F32)], [], sums, pair_up(sums, lambda i: i ^ 1))[0]
-    sums = [sums, pair_up(sums, lambda i: lax.axis_size("tp") - 1 - i)]
+    sums = [sums] + from_peers(sums, "tp")
     wide_low = wide(gated_halo, key_in, value_in, front_table)
     sums, wide_low = lax.optimization_barrier((sums, wide_low))
     head_rows = head(sums, query, out_grad, medium_low, gain_row)

time: 77.9 us -> 77 us (0.988)
  blocking collectives: 11.4 us -> 0 us
  starting transfers between devices: 27.5 us -> 33.6 us
  waiting for transfers between devices: 5.05 us -> 7.11 us
  Pallas kernels: 31.1 us -> 32.7 us
    all_to_all x1 -> x0, blocking collectives: 11.4 us -> none  [spread(): return lax.all_to_all(everyone, 'ctx', 0, 0, axis_index_groups=groups)]
    all_to_all x1 -> x2, starting transfers between devices: 10.4 us -> 16 us  [spread(): return lax.all_to_all(everyone, 'ctx', 0, 0, axis_index_groups=groups)]
    all_to_all x1 -> x2, waiting for transfers between devices: 3.64 us -> 5.79 us  [spread(): return lax.all_to_all(everyone, 'ctx', 0, 0, axis_index_groups=groups)]
    pallas_call x2 -> x3, Pallas kernels: 8.41 us -> 10.5 us  [backward(): pl.pallas_call(backward_kernel, grid=(steps,), in_specs=[col(tok), col(HA...]
    ppermute x2, starting transfers between devices: 7.92 us -> 6.69 us  [shifted(): lax.ppermute(x, 'ctx', [(i, i + by) for i in range(peers) if 0 <= i + by...]
    ppermute x2 -> x3, waiting for transfers between devices: 1.14 us -> 0.01 us  [from_peers(): lax.ppermute(x, axis, [(i, (i + k) % peers) for i in range(peers)])]
    all_to_all x1, waiting for transfers between devices: 0.27 us -> 1.31 us  [sum_over_ctx(): arrived = lax.all_to_all(parts, 'ctx', 0, 0, axis_index_groups=near)]
    ppermute x2 -> x3, starting transfers between devices: 4.11 us -> 5.06 us  [from_peers(): lax.ppermute(x, axis, [(i, (i + k) % peers) for i in range(peers)])]
  transfers between devices with their start and end apart: 6 -> 8, of which waited for: 3 -> 3; matrix products, arithmetic and copies ran while one was open for 0% -> 0% of each run, Pallas kernels for 32% -> 35%
where the time goes in v6:
time: 77 us; the launch traced here: 76.5 us
  starting transfers between devices  33.6 us (44%)
  Pallas kernels  32.7 us (42%)
  waiting for transfers between devices  7.11 us (9%)
  local copies, waits for them, and re-layouts  2.15 us (3%)
  between operations  0.85 us (1%)
    pallas_call x6, Pallas kernels, call(): pl.pallas_call(body, in_specs=[VMEM] * len(args), out_specs=out_specs, ou...  19.9 us
    all_to_all x2, starting transfers between devices, spread(): return lax.all_to_all(everyone, 'ctx', 0, 0, axis_index_groups=groups)  16 us
    pallas_call x3, Pallas kernels, backward(): pl.pallas_call(backward_kernel, grid=(steps,), in_specs=[col(tok), col(HA...  10.5 us
    ppermute x2, starting transfers between devices, shifted(): lax.ppermute(x, 'ctx', [(i, i + by) for i in range(peers) if 0 <= i + by...  6.69 us
    all_to_all x1, starting transfers between devices, sum_over_ctx(): arrived = lax.all_to_all(parts, 'ctx', 0, 0, axis_index_groups=near)  5.85 us
    all_to_all x2, waiting for transfers between devices, spread(): return lax.all_to_all(everyone, 'ctx', 0, 0, axis_index_groups=groups)  5.79 us
    ppermute x3, starting transfers between devices, from_peers(): lax.ppermute(x, axis, [(i, (i + k) % peers) for i in range(peers)])  5.06 us
  transfers between devices with their start and end apart: 8, of which 3 were waited for; matrix products, arithmetic and copies ran while one was open for 0% of the time, Pallas kernels for 35%

profile of v6, /device:TPU:1, one launch (start us, length us, event | category | flops | bytes accessed | tf_op | source)
XLA Modules:
  0.0 76.5 jit_solution(16746557900362918701)
XLA Ops:
  0.6 0.0 copy-start.6
  0.6 1.5 %tail_rows.1 = bf16[144,2048]{1,0:T(8,128)(2,1)S(1)} custom-call(bf16[256,2048]{1,0:T(8,128)(2,1)} %key_ref.13, bf16[256,2048]{1,0:T(8,128)(2,1)} %value_ref.13), custom_call_target="tpu_custom_call" | custom-call | flops 1200000000 | tf_op jit(solution)/shard_map/tail_rows/pallas_call | solution.py:173
  2.1 0.0 copy-start
  2.1 0.0 copy-start.1
  2.1 0.0 copy-start.2
  2.1 0.0 copy-start.3
  2.2 0.0 copy-start.4
  2.2 0.0 copy-start.5
  2.2 4.8 %collective-permute-start = (bf16[144,2048]{1,0:T(8,128)(2,1)S(1)}, bf16[144,2048]{1,0:T(8,128)(2,1)S(1)}, u32[]{:S(2)}, u32[]{:S(2)}) collective-permute-start(bf16[144,2048]{1,0:T(8,128)(2,1)S(1)} %tail_rows.1), channel_id=1, source_target_pairs={{0,4},{4,8},{8,12},{12,16},{16,20},{20,24},{24,28},{28,32},{32,36}... | collective-permute-start | bytes 1769480 | tf_op jit(solution)/shard_map/ppermute | solution.py:79
  7.0 0.0 copy-done.6
  7.0 3.5 %filter_tables.1 = (bf16[4096,256]{1,0:T(8,128)(2,1)S(1)}, bf16[4096,256]{1,0:T(8,128)(2,1)}) custom-call(bf16[128,128]{1,0:T(8,128)(2,1)S(1)} %copy-done.6), custom_call_target="tpu_custom_call" | custom-call | flops 2400000000 | tf_op jit(solution)/shard_map/filter_tables/pallas_call | solution.py:62
  10.5 0.0 copy-done
  10.5 0.0 copy-done.1
  10.5 0.0 copy-done.2
  10.6 0.0 copy-done.3
  10.6 0.0 copy-done.4
  10.6 0.0 copy-done.5
  10.6 4.1 %early.1 = (f32[96,2048]{1,0:T(8,128)S(1)}, bf16[256,2048]{1,0:T(8,128)(2,1)S(1)}, f32[128,2048]{1,0:T(8,128)S(1)}, f32[96,128]{1,0:T(8,128)S(1)}, f32[96,128]{1,0:T(8,128)S(1)}) custom-call(bf16[256,2048]{1,0:T(8,128)(2,1)S(1)} %copy-done, bf16[256,2048]{1,0:T(8,128)(2,1)S(1)} %copy-done.1, bf16[256,2048]{1,0:T(8,128)(2,1)S(1)} %copy-done.2, ...), custom_call_target="tpu_custom_call" | custom-call | flops 4200000000 | tf_op jit(solution)/shard_map/early/pallas_call | solution.py:62
  14.7 0.0 collective-permute-done.halo_ref
  14.7 2.8 %late.1 = (f32[160,2048]{1,0:T(8,128)S(1)}, bf16[160,2048]{1,0:T(8,128)(2,1)S(1)}, f32[2,256]{1,0:T(2,128)S(1)}) custom-call(bf16[144,2048]{1,0:T(8,128)(2,1)S(1)} %collective-permute-done.halo_ref, bf16[256,2048]{1,0:T(8,128)(2,1)S(1)} %copy-done, bf16[256,2048]{1,0:T(8,128)(2,1)S(1)} %copy-done.1, bf16[256,2048]{1,0:T(8,128)(2,1)S(1)} %copy-done.2, ...), custom_call_target="tpu_custom_call" | custom-call | flops 2900000000 | tf_op jit(solution)/shard_map/late/pallas_call | solution.py:62
  17.5 1.4 %collective-permute-start.1 = (f32[2,256]{1,0:T(2,128)S(1)}, f32[2,256]{1,0:T(2,128)S(1)}, u32[]{:S(2)}, u32[]{:S(2)}) collective-permute-start(f32[2,256]{1,0:T(2,128)S(1)} %get-tuple-element.58.rest_0_), channel_id=1, source_target_pairs={{0,1},{1,2},{2,3},{3,0},{4,5},{5,6},{6,7},{7,4},{8,9},{9,10},{10,1... | collective-permute-start | bytes 6152 | tf_op jit(solution)/shard_map/ppermute | solution.py:561
  18.9 2.6 %collective-permute-start.2 = (f32[2,256]{1,0:T(2,128)S(1)}, f32[2,256]{1,0:T(2,128)S(1)}, u32[]{:S(2)}, u32[]{:S(2)}) collective-permute-start(f32[2,256]{1,0:T(2,128)S(1)} %get-tuple-element.58.rest_0_), channel_id=1, source_target_pairs={{0,2},{1,3},{2,0},{3,1},{4,6},{5,7},{6,4},{7,5},{8,10},{9,11},{10,... | collective-permute-start | bytes 6152 | tf_op jit(solution)/shard_map/ppermute | solution.py:561
  21.5 1.1 %collective-permute-start.3 = (f32[2,256]{1,0:T(2,128)S(1)}, f32[2,256]{1,0:T(2,128)S(1)}, u32[]{:S(2)}, u32[]{:S(2)}) collective-permute-start(f32[2,256]{1,0:T(2,128)S(1)} %get-tuple-element.58.rest_0_), channel_id=1, source_target_pairs={{0,3},{1,0},{2,1},{3,2},{4,7},{5,4},{6,5},{7,6},{8,11},{9,8},{10,9... | collective-permute-start | bytes 6152 | tf_op jit(solution)/shard_map/ppermute | solution.py:561
  22.6 2.0 %wide_gated.1.wide_low_ref = f32[160,2048]{1,0:T(8,128)S(1)} custom-call(bf16[144,2048]{1,0:T(8,128)(2,1)S(1)} %collective-permute-done.halo_ref, bf16[256,2048]{1,0:T(8,128)(2,1)S(1)} %copy-done, bf16[256,2048]{1,0:T(8,128)(2,1)S(1)} %copy-done.1, bf16[4096,256]{1,0:T(8,128)(2,1)S(1)} %get-tuple-element.48.table_ref), custom_call_target="tpu_custom_call" | custom-call | flops 2000000000 | tf_op jit(solution)/shard_map/wide_gated/pallas_call | solution.py:62
  24.6 0.0 collective-permute-done.1.rest_1_
  24.6 0.0 collective-permute-done.2.rest_2_
  24.6 0.0 collective-permute-done.3.rest_3_
  24.6 0.9 %head_rows.1 = bf16[144,2048]{1,0:T(8,128)(2,1)S(1)} custom-call(bf16[256,2048]{1,0:T(8,128)(2,1)S(1)} %copy-done.2, bf16[256,2048]{1,0:T(8,128)(2,1)S(1)} %copy-done.3, f32[160,2048]{1,0:T(8,128)S(1)} %get-tuple-element.52.medium_low_ref.medium_ref, f32[1,2048]{1,0:T(1,128)S(1)} %bitcast.7, f32[2,256]{1,0:T(2,128)S(1)} %get-tuple-element.58.rest_0_, ...), custom_call_target="tpu_custom_call" | custom-call | flops 900000000 | tf_op jit(solution)/shard_map/head_rows/pallas_call | solution.py:62
  25.5 1.9 %collective-permute-start.4 = (bf16[144,2048]{1,0:T(8,128)(2,1)S(1)}, bf16[144,2048]{1,0:T(8,128)(2,1)S(1)}, u32[]{:S(2)}, u32[]{:S(2)}) collective-permute-start(bf16[144,2048]{1,0:T(8,128)(2,1)S(1)} %head_rows.1), channel_id=1, source_target_pairs={{4,0},{8,4},{12,8},{16,12},{20,16},{24,20},{28,24},{32,28},{36,32}... | collective-permute-start | bytes 1769480 | tf_op jit(solution)/shard_map/ppermute | solution.py:79
  27.4 6.5 %gradients.1 = (bf16[256,2048]{1,0:T(8,128)(2,1)}, bf16[256,2048]{1,0:T(8,128)(2,1)}, f32[256,128]{1,0:T(8,128)}) custom-call(bf16[256,2048]{1,0:T(8,128)(2,1)S(1)} %copy-done.2, bf16[256,2048]{1,0:T(8,128)(2,1)S(1)} %copy-done.3, f32[160,2048]{1,0:T(8,128)S(1)} %get-tuple-element.52.medium_low_ref.medium_ref, ...), custom_call_target="tpu_custom_call" | custom-call | flops 6600000000 | tf_op jit(solution)/shard_map/gradients/pallas_call | solution.py:62
  34.0 5.9 %all-to-all-start = ((f32[8,32,128]{2,1,0:T(8,128)}), f32[8,32,128]{2,1,0:T(8,128)S(1)}, u32[]{:S(2)}, u32[]{:S(2)}) async-start(f32[8,32,128]{2,1,0:T(8,128)} %bitcast.1), calls=%async_computation | async-start | bytes 262144 | tf_op jit(solution)/shard_map/all_to_all | solution.py:574
  39.8 0.0 collective-permute-done.4.halo_ref
  39.8 0.0 copy-start.7
  39.8 0.8 %copy-done.7 = bf16[144,2048]{1,0:T(8,128)(2,1)} copy-done((bf16[144,2048]{1,0:T(8,128)(2,1)}, bf16[144,2048]{1,0:T(8,128)(2,1)S(1)}, u32[]{:S(2)}) %copy-start.7) | copy-done | bytes 589848
  40.6 3.1 %backward.3 = (bf16[256,2048]{1,0:T(8,128)(2,1)}, bf16[256,2048]{1,0:T(8,128)(2,1)}) custom-call(bf16[256,2048]{1,0:T(8,128)(2,1)} %get-tuple-element.64.grad_ref, bf16[144,2048]{1,0:T(8,128)(2,1)} %copy-done.7, bf16[7,2048]{1,0:T(8,128)(2,1)} %se_ref.9, bf16[256,2048]{1,0:T(8,128)(2,1)} %key_ref.13, bf16[256,2048]{1,0:T(8,128)(2,1)} %value_ref.13, ...), custom_call_target="tpu_custom_call" | custom-call | flops 2000000000 | tf_op jit(solution)/shard_map/backward/pallas_call | solution.py:503
  43.8 1.3 %all-to-all-done = f32[8,32,128]{2,1,0:T(8,128)S(1)} async-done(((f32[8,32,128]{2,1,0:T(8,128)}), f32[8,32,128]{2,1,0:T(8,128)S(1)}, u32[]{:S(2)}, u32[]{:S(2)}) %all-to-all-start) | async-done | bytes 131104 | tf_op jit(solution)/shard_map/all_to_all | solution.py:574
  45.1 0.7 broadcast_in_dim.7
  45.7 10.4 %all-to-all-start.1 = ((f32[8,32,128]{2,1,0:T(8,128)}), f32[8,32,128]{2,1,0:T(8,128)S(1)}, u32[]{:S(2)}, u32[]{:S(2)}) async-start(f32[8,32,128]{2,1,0:T(8,128)} %broadcast_in_dim.7), calls=%async_computation.1 | async-start | bytes 262144 | tf_op jit(solution)/shard_map/all_to_all | solution.py:566
  56.1 4.2 %backward.4 = (bf16[256,2048]{1,0:T(8,128)(2,1)}, bf16[256,2048]{1,0:T(8,128)(2,1)}) custom-call(bf16[256,2048]{1,0:T(8,128)(2,1)} %get-tuple-element.64.grad_ref, bf16[144,2048]{1,0:T(8,128)(2,1)} %copy-done.7, bf16[7,2048]{1,0:T(8,128)(2,1)} %se_ref.9, bf16[256,2048]{1,0:T(8,128)(2,1)} %key_ref.13, ...), custom_call_target="tpu_custom_call", output_to_operand_aliasing={{0}: (6, {}), {1}: (7, {})} | custom-call | flops 4000000000 | tf_op jit(solution)/shard_map/backward/pallas_call | solution.py:503
  60.4 3.6 %all-to-all-done.1 = f32[8,32,128]{2,1,0:T(8,128)S(1)} async-done(((f32[8,32,128]{2,1,0:T(8,128)}), f32[8,32,128]{2,1,0:T(8,128)S(1)}, u32[]{:S(2)}, u32[]{:S(2)}) %all-to-all-start.1) | async-done | bytes 131104 | tf_op jit(solution)/shard_map/all_to_all | solution.py:566
  64.0 0.7 broadcast_in_dim.8
  64.7 5.6 %all-to-all-start.2 = ((f32[8,32,128]{2,1,0:T(8,128)}), f32[8,32,128]{2,1,0:T(8,128)S(1)}, u32[]{:S(2)}, u32[]{:S(2)}) async-start(f32[8,32,128]{2,1,0:T(8,128)} %broadcast_in_dim.8), calls=%async_computation.2 | async-start | bytes 262144 | tf_op jit(solution)/shard_map/all_to_all | solution.py:566
  70.3 3.1 %backward.5 = (bf16[256,2048]{1,0:T(8,128)(2,1)}, bf16[256,2048]{1,0:T(8,128)(2,1)}) custom-call(bf16[256,2048]{1,0:T(8,128)(2,1)} %get-tuple-element.64.grad_ref, bf16[144,2048]{1,0:T(8,128)(2,1)} %copy-done.7, bf16[7,2048]{1,0:T(8,128)(2,1)} %se_ref.9, bf16[256,2048]{1,0:T(8,128)(2,1)} %key_ref.13, ...), custom_call_target="tpu_custom_call", output_to_operand_aliasing={{0}: (6, {}), {1}: (7, {})} | custom-call | flops 2000000000 | tf_op jit(solution)/shard_map/backward/pallas_call | solution.py:503
  73.5 2.1 %all-to-all-done.2 = f32[8,32,128]{2,1,0:T(8,128)S(1)} async-done(((f32[8,32,128]{2,1,0:T(8,128)}), f32[8,32,128]{2,1,0:T(8,128)S(1)}, u32[]{:S(2)}, u32[]{:S(2)}) %all-to-all-start.2) | async-done | bytes 131104 | tf_op jit(solution)/shard_map/all_to_all | solution.py:566
  75.6 0.9 %finish.1 = (f32[128,128]{1,0:T(8,128)}, f32[7,2048]{1,0:T(8,128)}, f32[1,2048]{1,0:T(1,128)}) custom-call(f32[256,128]{1,0:T(8,128)S(1)} %bitcast.4), custom_call_target="tpu_custom_call" | custom-call | flops 900000000 | tf_op jit(solution)/shard_map/finish/pallas_call | solution.py:546
  (2 shorter events, 0.0 us)
Async XLA Ops:
  0.6 6.3 %copy-start.6 = (bf16[128,128]{1,0:T(8,128)(2,1)S(1)}, bf16[128,128]{1,0:T(8,128)(2,1)}, u32[]{:S(2)}) copy-start(bf16[128,128]{1,0:T(8,128)(2,1)} %taps_ref.1) | copy-start | bytes 98308
  2.1 8.4 %copy-start = (bf16[256,2048]{1,0:T(8,128)(2,1)S(1)}, bf16[256,2048]{1,0:T(8,128)(2,1)}, u32[]{:S(2)}) copy-start(bf16[256,2048]{1,0:T(8,128)(2,1)} %key_ref.13) | copy-start | bytes 3145732
  2.1 8.4 %copy-start.1 = (bf16[256,2048]{1,0:T(8,128)(2,1)S(1)}, bf16[256,2048]{1,0:T(8,128)(2,1)}, u32[]{:S(2)}) copy-start(bf16[256,2048]{1,0:T(8,128)(2,1)} %value_ref.13) | copy-start | bytes 3145732
  2.1 8.4 %copy-start.2 = (bf16[256,2048]{1,0:T(8,128)(2,1)S(1)}, bf16[256,2048]{1,0:T(8,128)(2,1)}, u32[]{:S(2)}) copy-start(bf16[256,2048]{1,0:T(8,128)(2,1)} %query_ref.7) | copy-start | bytes 3145732
  2.1 8.4 %copy-start.3 = (bf16[256,2048]{1,0:T(8,128)(2,1)S(1)}, bf16[256,2048]{1,0:T(8,128)(2,1)}, u32[]{:S(2)}) copy-start(bf16[256,2048]{1,0:T(8,128)(2,1)} %out_grad_ref.7) | copy-start | bytes 3145732
  2.2 8.4 %copy-start.4 = (bf16[7,2048]{1,0:T(8,128)(2,1)S(1)}, bf16[7,2048]{1,0:T(8,128)(2,1)}, u32[]{:S(2)}) copy-start(bf16[7,2048]{1,0:T(8,128)(2,1)} %se_ref.9) | copy-start | bytes 86020
  2.2 8.4 %copy-start.5 = (f32[2048]{0:T(1024)S(1)}, f32[2048]{0:T(1024)}, u32[]{:S(2)}) copy-start(f32[2048]{0:T(1024)} %param.13) | copy-start | bytes 24580
  2.2 12.5 %collective-permute-start = (bf16[144,2048]{1,0:T(8,128)(2,1)S(1)}, bf16[144,2048]{1,0:T(8,128)(2,1)S(1)}, u32[]{:S(2)}, u32[]{:S(2)}) collective-permute-start(bf16[144,2048]{1,0:T(8,128)(2,1)S(1)} %tail_rows.1), channel_id=1, source_target_pairs={{0,4},{4,8},{8,12},{12,16},{16,20},{20,24},{24,28},{28,32},{32,36}... | collective-permute-start | bytes 1769480 | tf_op jit(solution)/shard_map/ppermute | solution.py:79
  17.5 7.1 %collective-permute-start.1 = (f32[2,256]{1,0:T(2,128)S(1)}, f32[2,256]{1,0:T(2,128)S(1)}, u32[]{:S(2)}, u32[]{:S(2)}) collective-permute-start(f32[2,256]{1,0:T(2,128)S(1)} %get-tuple-element.58.rest_0_), channel_id=1, source_target_pairs={{0,1},{1,2},{2,3},{3,0},{4,5},{5,6},{6,7},{7,4},{8,9},{9,10},{10,1... | collective-permute-start | bytes 6152 | tf_op jit(solution)/shard_map/ppermute | solution.py:561
  18.9 5.7 %collective-permute-start.2 = (f32[2,256]{1,0:T(2,128)S(1)}, f32[2,256]{1,0:T(2,128)S(1)}, u32[]{:S(2)}, u32[]{:S(2)}) collective-permute-start(f32[2,256]{1,0:T(2,128)S(1)} %get-tuple-element.58.rest_0_), channel_id=1, source_target_pairs={{0,2},{1,3},{2,0},{3,1},{4,6},{5,7},{6,4},{7,5},{8,10},{9,11},{10,... | collective-permute-start | bytes 6152 | tf_op jit(solution)/shard_map/ppermute | solution.py:561
  21.5 3.1 %collective-permute-start.3 = (f32[2,256]{1,0:T(2,128)S(1)}, f32[2,256]{1,0:T(2,128)S(1)}, u32[]{:S(2)}, u32[]{:S(2)}) collective-permute-start(f32[2,256]{1,0:T(2,128)S(1)} %get-tuple-element.58.rest_0_), channel_id=1, source_target_pairs={{0,3},{1,0},{2,1},{3,2},{4,7},{5,4},{6,5},{7,6},{8,11},{9,8},{10,9... | collective-permute-start | bytes 6152 | tf_op jit(solution)/shard_map/ppermute | solution.py:561
  25.5 14.3 %collective-permute-start.4 = (bf16[144,2048]{1,0:T(8,128)(2,1)S(1)}, bf16[144,2048]{1,0:T(8,128)(2,1)S(1)}, u32[]{:S(2)}, u32[]{:S(2)}) collective-permute-start(bf16[144,2048]{1,0:T(8,128)(2,1)S(1)} %head_rows.1), channel_id=1, source_target_pairs={{4,0},{8,4},{12,8},{16,12},{20,16},{24,20},{28,24},{32,28},{36,32}... | collective-permute-start | bytes 1769480 | tf_op jit(solution)/shard_map/ppermute | solution.py:79
  34.0 11.1 %all-to-all-start = ((f32[8,32,128]{2,1,0:T(8,128)}), f32[8,32,128]{2,1,0:T(8,128)S(1)}, u32[]{:S(2)}, u32[]{:S(2)}) async-start(f32[8,32,128]{2,1,0:T(8,128)} %bitcast.1), calls=%async_computation | async-start | bytes 262144 | tf_op jit(solution)/shard_map/all_to_all | solution.py:574
  39.8 0.8 %copy-start.7 = (bf16[144,2048]{1,0:T(8,128)(2,1)}, bf16[144,2048]{1,0:T(8,128)(2,1)S(1)}, u32[]{:S(2)}) copy-start(bf16[144,2048]{1,0:T(8,128)(2,1)S(1)} %collective-permute-done.4.halo_ref) | copy-start | bytes 1769476
  45.7 18.2 %all-to-all-start.1 = ((f32[8,32,128]{2,1,0:T(8,128)}), f32[8,32,128]{2,1,0:T(8,128)S(1)}, u32[]{:S(2)}, u32[]{:S(2)}) async-start(f32[8,32,128]{2,1,0:T(8,128)} %broadcast_in_dim.7), calls=%async_computation.1 | async-start | bytes 262144 | tf_op jit(solution)/shard_map/all_to_all | solution.py:566
  64.7 10.9 %all-to-all-start.2 = ((f32[8,32,128]{2,1,0:T(8,128)}), f32[8,32,128]{2,1,0:T(8,128)S(1)}, u32[]{:S(2)}, u32[]{:S(2)}) async-start(f32[8,32,128]{2,1,0:T(8,128)} %broadcast_in_dim.8), calls=%async_computation.2 | async-start | bytes 262144 | tf_op jit(solution)/shard_map/all_to_all | solution.py:566

commit v7 on v6

--- a/solution.py
+++ b/solution.py
@@ -27,8 +27,8 @@
 UNROLL = 8
 TAIL_PARTS = 4
 BW = 512
-PARTS = (0, 1, 3, 4)
-NEAR = 8
+PARTS = (0, 2, 4)
+WIRE = jnp.bfloat16
 VMEM = pl.BlockSpec(memory_space=pltpu.VMEM)
 HBM = pl.BlockSpec(memory_space=pltpu.HBM)
 
@@ -433,7 +433,7 @@
             total = total + pltpu.roll(part, 2 * LANES - 1 - s, 1)
         packed_out[of_tile(tile, 2 * GT), :] = jnp.concatenate(
             [total[:, :LANES]] + lines + [gain_row], axis=0
-        )
+        ).astype(WIRE)
 
     each_tile(channels, body)
 
@@ -443,7 +443,7 @@
     outs = [
         ((tok, channels), BF16),
         ((tok, channels), BF16),
-        ((2 * GT * channels // LANES, LANES), F32),
+        ((2 * GT * channels // LANES, LANES), WIRE),
     ]
     scratch = [
         pltpu.VMEM((tok, LANES), F32),
@@ -526,14 +526,14 @@
 
 
 def finish_kernel(tokens, packed_ref, mr_out, se_out, gain_out):
-    packed = packed_ref[...]
+    packed = packed_ref[...].astype(F32)
     tiles = packed.shape[0] // (2 * GT)
     rows = jnp.concatenate([packed[2 * GT * i : 2 * GT * i + GT, :] for i in range(tiles)], axis=0)
     row_ids = lax.broadcasted_iota(jnp.int32, (MR_LEN, MR_LEN), 0)
     col_ids = lax.broadcasted_iota(jnp.int32, (MR_LEN, MR_LEN), 1)
-    flip = jnp.where(row_ids + col_ids == MR_LEN - 1, 1.0, 0.0).astype(F32)
+    flip = jnp.where(row_ids + col_ids == MR_LEN - 1, 1.0, 0.0).astype(WIRE)
     mr_out[...] = lax.dot_general(
-        flip, rows, (((1,), (1,)), ((), ())), preferred_element_type=F32, precision=lax.Precision.HIGHEST
+        flip, rows.astype(WIRE), (((1,), (1,)), ((), ())), preferred_element_type=F32
     ) * (1.0 / (tokens * GROUP) ** 0.5)
     for i in range(tiles):
         at = slice(i * LANES, (i + 1) * LANES)
@@ -561,23 +561,14 @@
     return [lax.ppermute(x, axis, [(i, (i + k) % peers) for i in range(peers)]) for k in range(1, peers)]
 
 
-def spread(x, groups):
-    everyone = jnp.broadcast_to(x[None], (len(groups[0]),) + x.shape)
-    return lax.all_to_all(everyone, "ctx", 0, 0, axis_index_groups=groups)
-
-
 def sum_over_ctx(packed, beside):
     peers = lax.axis_size("ctx")
-    near = [list(range(first, first + NEAR)) for first in range(0, peers, NEAR)]
-    far = [list(range(first, peers, NEAR)) for first in range(NEAR)]
-    parts = packed.reshape(NEAR, packed.shape[0] // NEAR, packed.shape[1])
-    arrived = lax.all_to_all(parts, "ctx", 0, 0, axis_index_groups=near)
-    arrived, done = lax.optimization_barrier((arrived, beside(0)))
-    mine, done = lax.optimization_barrier((jnp.sum(arrived, axis=0), done))
-    arrived = spread(mine, far)
-    arrived, done = lax.optimization_barrier((arrived, beside(1, done)))
-    mine, done = lax.optimization_barrier((jnp.sum(arrived, axis=0), done))
-    everyone, done = lax.optimization_barrier((spread(mine, near), beside(2, done)))
+    parts = packed.astype(WIRE).reshape(peers, packed.shape[0] // peers, packed.shape[1])
+    arrived, done = lax.optimization_barrier((lax.all_to_all(parts, "ctx", 0, 0), beside(0)))
+    mine = jnp.sum(arrived.astype(F32), axis=0).astype(WIRE)
+    mine, done = lax.optimization_barrier((mine, done))
+    everyone = lax.all_to_all(jnp.broadcast_to(mine[None], parts.shape), "ctx", 0, 0)
+    everyone, done = lax.optimization_barrier((everyone, beside(1, done)))
     return everyone.reshape(packed.shape), done
 
 

time: 77 us -> 75.2 us (0.977)
  waiting for transfers between devices: 7.11 us -> 11 us
  starting transfers between devices: 33.6 us -> 30.9 us
  Pallas kernels: 32.7 us -> 30.7 us
    all_to_all x3 -> x2, waiting for transfers between devices: 7.1 us -> 10.9 us  [the longest x1 5.87 us: sum_over_ctx(): lax.all_to_all(jnp.broadcast_to(mine[None], parts.shape), 'ctx', 0, 0)]
    all_to_all x3 -> x2, starting transfers between devices: 21.9 us -> 19.1 us  [the longest x1 13.9 us: sum_over_ctx(): lax.all_to_all(parts, 'ctx', 0, 0)]
    pallas_call x3 -> x2, Pallas kernels: 10.5 us -> 8.41 us  [backward(): pl.pallas_call(backward_kernel, grid=(steps,), in_specs=[col(tok), col(HA...]
  transfers between devices with their start and end apart: 8 -> 7, of which waited for: 3 -> 2; matrix products, arithmetic and copies ran while one was open for 0% -> 0% of each run, Pallas kernels for 35% -> 33%
where the time goes in v7:
time: 75.2 us; the launch traced here: 74.9 us
  starting transfers between devices  30.9 us (41%)
  Pallas kernels  30.7 us (41%)
  waiting for transfers between devices  11 us (15%)
  local copies, waits for them, and re-layouts  1.5 us (2%)
  between operations  0.87 us (1%)
    pallas_call x6, Pallas kernels, call(): pl.pallas_call(body, in_specs=[VMEM] * len(args), out_specs=out_specs, ou...  20 us
    all_to_all x1, starting transfers between devices, sum_over_ctx(): lax.all_to_all(parts, 'ctx', 0, 0)  13.9 us
    pallas_call x2, Pallas kernels, backward(): pl.pallas_call(backward_kernel, grid=(steps,), in_specs=[col(tok), col(HA...  8.41 us
    ppermute x2, starting transfers between devices, shifted(): lax.ppermute(x, 'ctx', [(i, i + by) for i in range(peers) if 0 <= i + by...  6.69 us
    all_to_all x1, waiting for transfers between devices, sum_over_ctx(): lax.all_to_all(jnp.broadcast_to(mine[None], parts.shape), 'ctx', 0, 0)  5.87 us
    all_to_all x1, starting transfers between devices, sum_over_ctx(): lax.all_to_all(jnp.broadcast_to(mine[None], parts.shape), 'ctx', 0, 0)  5.24 us
    all_to_all x1, waiting for transfers between devices, sum_over_ctx(): lax.all_to_all(parts, 'ctx', 0, 0)  5.07 us
    ppermute x3, starting transfers between devices, from_peers(): lax.ppermute(x, axis, [(i, (i + k) % peers) for i in range(peers)])  5.06 us
  transfers between devices with their start and end apart: 7, of which 2 were waited for; matrix products, arithmetic and copies ran while one was open for 0% of the time, Pallas kernels for 33%

profile of v7, /device:TPU:1, one launch (start us, length us, event | category | flops | bytes accessed | tf_op | source)
XLA Modules:
  0.0 74.9 jit_solution(2476652391752788563)
XLA Ops:
  0.6 0.0 copy-start.5
  0.6 1.5 %tail_rows.1 = bf16[144,2048]{1,0:T(8,128)(2,1)S(1)} custom-call(bf16[256,2048]{1,0:T(8,128)(2,1)} %key_ref.11, bf16[256,2048]{1,0:T(8,128)(2,1)} %value_ref.11), custom_call_target="tpu_custom_call" | custom-call | flops 1200000000 | tf_op jit(solution)/shard_map/tail_rows/pallas_call | solution.py:173
  2.1 0.0 copy-start
  2.1 0.0 copy-start.1
  2.1 0.0 copy-start.2
  2.1 0.0 copy-start.3
  2.2 0.0 copy-start.4
  2.2 0.0 copy-start.6
  2.2 4.8 %collective-permute-start = (bf16[144,2048]{1,0:T(8,128)(2,1)S(1)}, bf16[144,2048]{1,0:T(8,128)(2,1)S(1)}, u32[]{:S(2)}, u32[]{:S(2)}) collective-permute-start(bf16[144,2048]{1,0:T(8,128)(2,1)S(1)} %tail_rows.1), channel_id=1, source_target_pairs={{0,4},{4,8},{8,12},{12,16},{16,20},{20,24},{24,28},{28,32},{32,36}... | collective-permute-start | bytes 1769480 | tf_op jit(solution)/shard_map/ppermute | solution.py:79
  7.0 0.0 copy-done.5
  7.0 3.5 %filter_tables.1 = (bf16[4096,256]{1,0:T(8,128)(2,1)S(1)}, bf16[4096,256]{1,0:T(8,128)(2,1)}) custom-call(bf16[128,128]{1,0:T(8,128)(2,1)S(1)} %copy-done.5), custom_call_target="tpu_custom_call" | custom-call | flops 2400000000 | tf_op jit(solution)/shard_map/filter_tables/pallas_call | solution.py:62
  10.5 0.0 copy-done
  10.5 0.0 copy-done.1
  10.5 0.0 copy-done.2
  10.6 0.0 copy-done.3
  10.6 0.0 copy-done.4
  10.6 0.0 copy-done.6
  10.6 4.1 %early.1 = (f32[96,2048]{1,0:T(8,128)S(1)}, bf16[256,2048]{1,0:T(8,128)(2,1)S(1)}, f32[128,2048]{1,0:T(8,128)S(1)}, f32[96,128]{1,0:T(8,128)S(1)}, f32[96,128]{1,0:T(8,128)S(1)}) custom-call(bf16[256,2048]{1,0:T(8,128)(2,1)S(1)} %copy-done.3, bf16[256,2048]{1,0:T(8,128)(2,1)S(1)} %copy-done.4, bf16[256,2048]{1,0:T(8,128)(2,1)S(1)} %copy-done, ...), custom_call_target="tpu_custom_call" | custom-call | flops 4200000000 | tf_op jit(solution)/shard_map/early/pallas_call | solution.py:62
  14.7 0.0 collective-permute-done.halo_ref
  14.7 2.8 %late.1 = (f32[160,2048]{1,0:T(8,128)S(1)}, bf16[160,2048]{1,0:T(8,128)(2,1)S(1)}, f32[2,256]{1,0:T(2,128)S(1)}) custom-call(bf16[144,2048]{1,0:T(8,128)(2,1)S(1)} %collective-permute-done.halo_ref, bf16[256,2048]{1,0:T(8,128)(2,1)S(1)} %copy-done.3, bf16[256,2048]{1,0:T(8,128)(2,1)S(1)} %copy-done.4, bf16[256,2048]{1,0:T(8,128)(2,1)S(1)} %copy-done, ...), custom_call_target="tpu_custom_call" | custom-call | flops 2900000000 | tf_op jit(solution)/shard_map/late/pallas_call | solution.py:62
  17.5 1.4 %collective-permute-start.1 = (f32[2,256]{1,0:T(2,128)S(1)}, f32[2,256]{1,0:T(2,128)S(1)}, u32[]{:S(2)}, u32[]{:S(2)}) collective-permute-start(f32[2,256]{1,0:T(2,128)S(1)} %get-tuple-element.50.rest_0_), channel_id=1, source_target_pairs={{0,1},{1,2},{2,3},{3,0},{4,5},{5,6},{6,7},{7,4},{8,9},{9,10},{10,1... | collective-permute-start | bytes 6152 | tf_op jit(solution)/shard_map/ppermute | solution.py:561
  18.9 2.6 %collective-permute-start.2 = (f32[2,256]{1,0:T(2,128)S(1)}, f32[2,256]{1,0:T(2,128)S(1)}, u32[]{:S(2)}, u32[]{:S(2)}) collective-permute-start(f32[2,256]{1,0:T(2,128)S(1)} %get-tuple-element.50.rest_0_), channel_id=1, source_target_pairs={{0,2},{1,3},{2,0},{3,1},{4,6},{5,7},{6,4},{7,5},{8,10},{9,11},{10,... | collective-permute-start | bytes 6152 | tf_op jit(solution)/shard_map/ppermute | solution.py:561
  21.5 1.1 %collective-permute-start.3 = (f32[2,256]{1,0:T(2,128)S(1)}, f32[2,256]{1,0:T(2,128)S(1)}, u32[]{:S(2)}, u32[]{:S(2)}) collective-permute-start(f32[2,256]{1,0:T(2,128)S(1)} %get-tuple-element.50.rest_0_), channel_id=1, source_target_pairs={{0,3},{1,0},{2,1},{3,2},{4,7},{5,4},{6,5},{7,6},{8,11},{9,8},{10,9... | collective-permute-start | bytes 6152 | tf_op jit(solution)/shard_map/ppermute | solution.py:561
  22.6 2.0 %wide_gated.1.wide_low_ref = f32[160,2048]{1,0:T(8,128)S(1)} custom-call(bf16[144,2048]{1,0:T(8,128)(2,1)S(1)} %collective-permute-done.halo_ref, bf16[256,2048]{1,0:T(8,128)(2,1)S(1)} %copy-done.3, bf16[256,2048]{1,0:T(8,128)(2,1)S(1)} %copy-done.4, bf16[4096,256]{1,0:T(8,128)(2,1)S(1)} %get-tuple-element.40.table_ref), custom_call_target="tpu_custom_call" | custom-call | flops 2000000000 | tf_op jit(solution)/shard_map/wide_gated/pallas_call | solution.py:62
  24.6 0.0 collective-permute-done.1.rest_1_
  24.6 0.0 collective-permute-done.2.rest_2_
  24.6 0.0 collective-permute-done.3.rest_3_
  24.6 0.9 %head_rows.1 = bf16[144,2048]{1,0:T(8,128)(2,1)S(1)} custom-call(bf16[256,2048]{1,0:T(8,128)(2,1)S(1)} %copy-done, bf16[256,2048]{1,0:T(8,128)(2,1)S(1)} %copy-done.1, f32[160,2048]{1,0:T(8,128)S(1)} %get-tuple-element.44.medium_low_ref.medium_ref, f32[1,2048]{1,0:T(1,128)S(1)} %bitcast.7, f32[2,256]{1,0:T(2,128)S(1)} %get-tuple-element.50.rest_0_, ...), custom_call_target="tpu_custom_call" | custom-call | flops 900000000 | tf_op jit(solution)/shard_map/head_rows/pallas_call | solution.py:62
  25.5 1.9 %collective-permute-start.4 = (bf16[144,2048]{1,0:T(8,128)(2,1)S(1)}, bf16[144,2048]{1,0:T(8,128)(2,1)S(1)}, u32[]{:S(2)}, u32[]{:S(2)}) collective-permute-start(bf16[144,2048]{1,0:T(8,128)(2,1)S(1)} %head_rows.1), channel_id=1, source_target_pairs={{4,0},{8,4},{12,8},{16,12},{20,16},{24,20},{28,24},{32,28},{36,32}... | collective-permute-start | bytes 1769480 | tf_op jit(solution)/shard_map/ppermute | solution.py:79
  27.4 6.7 %gradients.1 = (bf16[256,2048]{1,0:T(8,128)(2,1)}, bf16[256,2048]{1,0:T(8,128)(2,1)}, bf16[256,128]{1,0:T(8,128)(2,1)}) custom-call(bf16[256,2048]{1,0:T(8,128)(2,1)S(1)} %copy-done, bf16[256,2048]{1,0:T(8,128)(2,1)S(1)} %copy-done.1, f32[160,2048]{1,0:T(8,128)S(1)} %get-tuple-element.44.medium_low_ref.medium_ref, ...), custom_call_target="tpu_custom_call" | custom-call | flops 6600000000 | tf_op jit(solution)/shard_map/gradients/pallas_call | solution.py:62
  34.1 13.9 %all-to-all-start = ((bf16[64,4,128]{2,1,0:T(4,128)(2,1)}), bf16[64,4,128]{2,1,0:T(4,128)(2,1)S(1)}, u32[]{:S(2)}, u32[]{:S(2)}) async-start(bf16[64,4,128]{2,1,0:T(4,128)(2,1)} %bitcast.1), calls=%async_computation | async-start | bytes 131072 | tf_op jit(solution)/shard_map/all_to_all | solution.py:567
  48.0 0.0 collective-permute-done.4.halo_ref
  48.0 0.0 copy-start.7
  48.0 0.8 %copy-done.7 = bf16[144,2048]{1,0:T(8,128)(2,1)} copy-done((bf16[144,2048]{1,0:T(8,128)(2,1)}, bf16[144,2048]{1,0:T(8,128)(2,1)S(1)}, u32[]{:S(2)}) %copy-start.7) | copy-done | bytes 589848
  48.8 4.2 %backward.2 = (bf16[256,2048]{1,0:T(8,128)(2,1)}, bf16[256,2048]{1,0:T(8,128)(2,1)}) custom-call(bf16[256,2048]{1,0:T(8,128)(2,1)} %get-tuple-element.56.grad_ref, bf16[144,2048]{1,0:T(8,128)(2,1)} %copy-done.7, bf16[7,2048]{1,0:T(8,128)(2,1)} %se_ref.7, bf16[256,2048]{1,0:T(8,128)(2,1)} %key_ref.11, bf16[256,2048]{1,0:T(8,128)(2,1)} %value_ref.11, ...), custom_call_target="tpu_custom_call" | custom-call | flops 4000000000 | tf_op jit(solution)/shard_map/backward/pallas_call | solution.py:503
  53.0 5.1 %all-to-all-done = bf16[64,4,128]{2,1,0:T(4,128)(2,1)S(1)} async-done(((bf16[64,4,128]{2,1,0:T(4,128)(2,1)}), bf16[64,4,128]{2,1,0:T(4,128)(2,1)S(1)}, u32[]{:S(2)}, u32[]{:S(2)}) %all-to-all-start) | async-done | bytes 65568 | tf_op jit(solution)/shard_map/all_to_all | solution.py:567
  58.1 0.1 reduce_sum.12
  58.2 0.7 broadcast_in_dim.10
  58.8 5.2 %all-to-all-start.1 = ((bf16[64,4,128]{2,1,0:T(4,128)(2,1)}), bf16[64,4,128]{2,1,0:T(4,128)(2,1)S(1)}, u32[]{:S(2)}, u32[]{:S(2)}) async-start(bf16[64,4,128]{2,1,0:T(4,128)(2,1)} %broadcast_in_dim.10), calls=%async_computation.1 | async-start | bytes 131072 | tf_op jit(solution)/shard_map/all_to_all | solution.py:570
  64.1 4.2 %backward.3 = (bf16[256,2048]{1,0:T(8,128)(2,1)}, bf16[256,2048]{1,0:T(8,128)(2,1)}) custom-call(bf16[256,2048]{1,0:T(8,128)(2,1)} %get-tuple-element.56.grad_ref, bf16[144,2048]{1,0:T(8,128)(2,1)} %copy-done.7, bf16[7,2048]{1,0:T(8,128)(2,1)} %se_ref.7, bf16[256,2048]{1,0:T(8,128)(2,1)} %key_ref.11, ...), custom_call_target="tpu_custom_call", output_to_operand_aliasing={{0}: (6, {}), {1}: (7, {})} | custom-call | flops 4000000000 | tf_op jit(solution)/shard_map/backward/pallas_call | solution.py:503
  68.3 5.9 %all-to-all-done.1 = bf16[64,4,128]{2,1,0:T(4,128)(2,1)S(1)} async-done(((bf16[64,4,128]{2,1,0:T(4,128)(2,1)}), bf16[64,4,128]{2,1,0:T(4,128)(2,1)S(1)}, u32[]{:S(2)}, u32[]{:S(2)}) %all-to-all-start.1) | async-done | bytes 65568 | tf_op jit(solution)/shard_map/all_to_all | solution.py:570
  74.2 0.8 %finish.1 = (f32[128,128]{1,0:T(8,128)}, f32[7,2048]{1,0:T(8,128)}, f32[1,2048]{1,0:T(1,128)}) custom-call(bf16[256,128]{1,0:T(8,128)(2,1)S(1)} %bitcast.4), custom_call_target="tpu_custom_call" | custom-call | flops 900000000 | tf_op jit(solution)/shard_map/finish/pallas_call | solution.py:546
Async XLA Ops:
  0.6 6.3 %copy-start.5 = (bf16[128,128]{1,0:T(8,128)(2,1)S(1)}, bf16[128,128]{1,0:T(8,128)(2,1)}, u32[]{:S(2)}) copy-start(bf16[128,128]{1,0:T(8,128)(2,1)} %taps_ref.1) | copy-start | bytes 98308
  2.1 8.4 %copy-start = (bf16[256,2048]{1,0:T(8,128)(2,1)S(1)}, bf16[256,2048]{1,0:T(8,128)(2,1)}, u32[]{:S(2)}) copy-start(bf16[256,2048]{1,0:T(8,128)(2,1)} %query_ref.7) | copy-start | bytes 3145732
  2.1 8.4 %copy-start.1 = (bf16[256,2048]{1,0:T(8,128)(2,1)S(1)}, bf16[256,2048]{1,0:T(8,128)(2,1)}, u32[]{:S(2)}) copy-start(bf16[256,2048]{1,0:T(8,128)(2,1)} %out_grad_ref.7) | copy-start | bytes 3145732
  2.1 8.4 %copy-start.2 = (f32[2048]{0:T(1024)S(1)}, f32[2048]{0:T(1024)}, u32[]{:S(2)}) copy-start(f32[2048]{0:T(1024)} %param.13) | copy-start | bytes 24580
  2.1 8.4 %copy-start.3 = (bf16[256,2048]{1,0:T(8,128)(2,1)S(1)}, bf16[256,2048]{1,0:T(8,128)(2,1)}, u32[]{:S(2)}) copy-start(bf16[256,2048]{1,0:T(8,128)(2,1)} %key_ref.11) | copy-start | bytes 3145732
  2.2 8.4 %copy-start.4 = (bf16[256,2048]{1,0:T(8,128)(2,1)S(1)}, bf16[256,2048]{1,0:T(8,128)(2,1)}, u32[]{:S(2)}) copy-start(bf16[256,2048]{1,0:T(8,128)(2,1)} %value_ref.11) | copy-start | bytes 3145732
  2.2 8.4 %copy-start.6 = (bf16[7,2048]{1,0:T(8,128)(2,1)S(1)}, bf16[7,2048]{1,0:T(8,128)(2,1)}, u32[]{:S(2)}) copy-start(bf16[7,2048]{1,0:T(8,128)(2,1)} %se_ref.7) | copy-start | bytes 86020
  2.2 12.5 %collective-permute-start = (bf16[144,2048]{1,0:T(8,128)(2,1)S(1)}, bf16[144,2048]{1,0:T(8,128)(2,1)S(1)}, u32[]{:S(2)}, u32[]{:S(2)}) collective-permute-start(bf16[144,2048]{1,0:T(8,128)(2,1)S(1)} %tail_rows.1), channel_id=1, source_target_pairs={{0,4},{4,8},{8,12},{12,16},{16,20},{20,24},{24,28},{28,32},{32,36}... | collective-permute-start | bytes 1769480 | tf_op jit(solution)/shard_map/ppermute | solution.py:79
  17.5 7.1 %collective-permute-start.1 = (f32[2,256]{1,0:T(2,128)S(1)}, f32[2,256]{1,0:T(2,128)S(1)}, u32[]{:S(2)}, u32[]{:S(2)}) collective-permute-start(f32[2,256]{1,0:T(2,128)S(1)} %get-tuple-element.50.rest_0_), channel_id=1, source_target_pairs={{0,1},{1,2},{2,3},{3,0},{4,5},{5,6},{6,7},{7,4},{8,9},{9,10},{10,1... | collective-permute-start | bytes 6152 | tf_op jit(solution)/shard_map/ppermute | solution.py:561
  18.9 5.7 %collective-permute-start.2 = (f32[2,256]{1,0:T(2,128)S(1)}, f32[2,256]{1,0:T(2,128)S(1)}, u32[]{:S(2)}, u32[]{:S(2)}) collective-permute-start(f32[2,256]{1,0:T(2,128)S(1)} %get-tuple-element.50.rest_0_), channel_id=1, source_target_pairs={{0,2},{1,3},{2,0},{3,1},{4,6},{5,7},{6,4},{7,5},{8,10},{9,11},{10,... | collective-permute-start | bytes 6152 | tf_op jit(solution)/shard_map/ppermute | solution.py:561
  21.5 3.1 %collective-permute-start.3 = (f32[2,256]{1,0:T(2,128)S(1)}, f32[2,256]{1,0:T(2,128)S(1)}, u32[]{:S(2)}, u32[]{:S(2)}) collective-permute-start(f32[2,256]{1,0:T(2,128)S(1)} %get-tuple-element.50.rest_0_), channel_id=1, source_target_pairs={{0,3},{1,0},{2,1},{3,2},{4,7},{5,4},{6,5},{7,6},{8,11},{9,8},{10,9... | collective-permute-start | bytes 6152 | tf_op jit(solution)/shard_map/ppermute | solution.py:561
  25.5 22.5 %collective-permute-start.4 = (bf16[144,2048]{1,0:T(8,128)(2,1)S(1)}, bf16[144,2048]{1,0:T(8,128)(2,1)S(1)}, u32[]{:S(2)}, u32[]{:S(2)}) collective-permute-start(bf16[144,2048]{1,0:T(8,128)(2,1)S(1)} %head_rows.1), channel_id=1, source_target_pairs={{4,0},{8,4},{12,8},{16,12},{20,16},{24,20},{28,24},{32,28},{36,32}... | collective-permute-start | bytes 1769480 | tf_op jit(solution)/shard_map/ppermute | solution.py:79
  34.1 24.0 %all-to-all-start = ((bf16[64,4,128]{2,1,0:T(4,128)(2,1)}), bf16[64,4,128]{2,1,0:T(4,128)(2,1)S(1)}, u32[]{:S(2)}, u32[]{:S(2)}) async-start(bf16[64,4,128]{2,1,0:T(4,128)(2,1)} %bitcast.1), calls=%async_computation | async-start | bytes 131072 | tf_op jit(solution)/shard_map/all_to_all | solution.py:567
  48.0 0.8 %copy-start.7 = (bf16[144,2048]{1,0:T(8,128)(2,1)}, bf16[144,2048]{1,0:T(8,128)(2,1)S(1)}, u32[]{:S(2)}) copy-start(bf16[144,2048]{1,0:T(8,128)(2,1)S(1)} %collective-permute-done.4.halo_ref) | copy-start | bytes 1769476
  58.8 15.3 %all-to-all-start.1 = ((bf16[64,4,128]{2,1,0:T(4,128)(2,1)}), bf16[64,4,128]{2,1,0:T(4,128)(2,1)S(1)}, u32[]{:S(2)}, u32[]{:S(2)}) async-start(bf16[64,4,128]{2,1,0:T(4,128)(2,1)} %broadcast_in_dim.10), calls=%async_computation.1 | async-start | bytes 131072 | tf_op jit(solution)/shard_map/all_to_all | solution.py:570

commit v8 on v7

--- a/solution.py
+++ b/solution.py
@@ -27,7 +27,7 @@
 UNROLL = 8
 TAIL_PARTS = 4
 BW = 512
-PARTS = (0, 2, 4)
+PARTS = (0, 1, 4)
 WIRE = jnp.bfloat16
 VMEM = pl.BlockSpec(memory_space=pltpu.VMEM)
 HBM = pl.BlockSpec(memory_space=pltpu.HBM)
@@ -328,11 +328,10 @@
 
 def spread_sums(parts, scale_ref, slope_ref, rows):
     sums = functools.reduce(jnp.add, [part[...] for part in parts])
-    square = jnp.broadcast_to(sums[0:1, :], (LANES, sums.shape[1])).T[:rows]
-    inner = jnp.broadcast_to(sums[1:2, :], (LANES, sums.shape[1])).T[:rows]
-    inv = lax.rsqrt(square / D + EPS)
-    scale_ref[...] = inv
-    slope_ref[...] = inv * inv * inv * inner / D
+    scale = lax.rsqrt(sums[0:1, :] * (1.0 / D) + EPS)
+    slope = scale * scale * scale * sums[1:2, :] * (1.0 / D)
+    for line, target in ((scale, scale_ref), (slope, slope_ref)):
+        target[...] = jnp.broadcast_to(line, (LANES, line.shape[1])).T[:rows]
 
 
 def head_kernel(query_ref, out_grad_ref, medium_ref, gain_ref, *rest):

time: 75.2 us -> 74.5 us (level)
  starting transfers between devices: 30.9 us -> 30.1 us
    all_to_all x1, waiting for transfers between devices: 5.87 us -> 4.37 us  [sum_over_ctx(): lax.all_to_all(jnp.broadcast_to(mine[None], parts.shape), 'ctx', 0, 0)]
    all_to_all x1, waiting for transfers between devices: 5.07 us -> 6.12 us  [sum_over_ctx(): lax.all_to_all(parts, 'ctx', 0, 0)]
    all_to_all x1, starting transfers between devices: 5.24 us -> 4.44 us  [sum_over_ctx(): lax.all_to_all(jnp.broadcast_to(mine[None], parts.shape), 'ctx', 0, 0)]
  transfers between devices with their start and end apart: 7 -> 7, of which waited for: 2 -> 2; matrix products, arithmetic and copies ran while one was open for 0% -> 0% of each run, Pallas kernels for 33% -> 34%
where the time goes in v8:
time: 74.5 us; the launch traced here: 74.2 us
  Pallas kernels  31.2 us (42%)
  starting transfers between devices  30.1 us (40%)
  waiting for transfers between devices  10.5 us (14%)
  local copies, waits for them, and re-layouts  1.5 us (2%)
  between operations  0.87 us (1%)
    pallas_call x6, Pallas kernels, call(): pl.pallas_call(body, in_specs=[VMEM] * len(args), out_specs=out_specs, ou...  20 us
    all_to_all x1, starting transfers between devices, sum_over_ctx(): lax.all_to_all(parts, 'ctx', 0, 0)  13.9 us
    pallas_call x2, Pallas kernels, backward(): pl.pallas_call(backward_kernel, grid=(steps,), in_specs=[col(tok), col(HA...  8.91 us
    ppermute x2, starting transfers between devices, shifted(): lax.ppermute(x, 'ctx', [(i, i + by) for i in range(peers) if 0 <= i + by...  6.69 us
    all_to_all x1, waiting for transfers between devices, sum_over_ctx(): lax.all_to_all(parts, 'ctx', 0, 0)  6.12 us
    ppermute x3, starting transfers between devices, from_peers(): lax.ppermute(x, axis, [(i, (i + k) % peers) for i in range(peers)])  5.06 us
    all_to_all x1, starting transfers between devices, sum_over_ctx(): lax.all_to_all(jnp.broadcast_to(mine[None], parts.shape), 'ctx', 0, 0)  4.44 us
    all_to_all x1, waiting for transfers between devices, sum_over_ctx(): lax.all_to_all(jnp.broadcast_to(mine[None], parts.shape), 'ctx', 0, 0)  4.37 us
  transfers between devices with their start and end apart: 7, of which 2 were waited for; matrix products, arithmetic and copies ran while one was open for 0% of the time, Pallas kernels for 34%

profile of v8, /device:TPU:1, one launch (start us, length us, event | category | flops | bytes accessed | tf_op | source)
XLA Modules:
  0.0 74.2 jit_solution(14498834662326945949)
XLA Ops:
  0.6 0.0 copy-start.5
  0.6 1.5 %tail_rows.1 = bf16[144,2048]{1,0:T(8,128)(2,1)S(1)} custom-call(bf16[256,2048]{1,0:T(8,128)(2,1)} %key_ref.11, bf16[256,2048]{1,0:T(8,128)(2,1)} %value_ref.11), custom_call_target="tpu_custom_call" | custom-call | flops 1200000000 | tf_op jit(solution)/shard_map/tail_rows/pallas_call | solution.py:173
  2.1 0.0 copy-start
  2.1 0.0 copy-start.1
  2.1 0.0 copy-start.2
  2.1 0.0 copy-start.3
  2.2 0.0 copy-start.4
  2.2 0.0 copy-start.6
  2.2 4.8 %collective-permute-start = (bf16[144,2048]{1,0:T(8,128)(2,1)S(1)}, bf16[144,2048]{1,0:T(8,128)(2,1)S(1)}, u32[]{:S(2)}, u32[]{:S(2)}) collective-permute-start(bf16[144,2048]{1,0:T(8,128)(2,1)S(1)} %tail_rows.1), channel_id=1, source_target_pairs={{0,4},{4,8},{8,12},{12,16},{16,20},{20,24},{24,28},{28,32},{32,36}... | collective-permute-start | bytes 1769480 | tf_op jit(solution)/shard_map/ppermute | solution.py:79
  7.0 0.0 copy-done.5
  7.0 3.5 %filter_tables.1 = (bf16[4096,256]{1,0:T(8,128)(2,1)S(1)}, bf16[4096,256]{1,0:T(8,128)(2,1)}) custom-call(bf16[128,128]{1,0:T(8,128)(2,1)S(1)} %copy-done.5), custom_call_target="tpu_custom_call" | custom-call | flops 2400000000 | tf_op jit(solution)/shard_map/filter_tables/pallas_call | solution.py:62
  10.5 0.0 copy-done
  10.5 0.0 copy-done.1
  10.5 0.0 copy-done.2
  10.6 0.0 copy-done.3
  10.6 0.0 copy-done.4
  10.6 0.0 copy-done.6
  10.6 4.1 %early.1 = (f32[96,2048]{1,0:T(8,128)S(1)}, bf16[256,2048]{1,0:T(8,128)(2,1)S(1)}, f32[128,2048]{1,0:T(8,128)S(1)}, f32[96,128]{1,0:T(8,128)S(1)}, f32[96,128]{1,0:T(8,128)S(1)}) custom-call(bf16[256,2048]{1,0:T(8,128)(2,1)S(1)} %copy-done.3, bf16[256,2048]{1,0:T(8,128)(2,1)S(1)} %copy-done.4, bf16[256,2048]{1,0:T(8,128)(2,1)S(1)} %copy-done, ...), custom_call_target="tpu_custom_call" | custom-call | flops 4200000000 | tf_op jit(solution)/shard_map/early/pallas_call | solution.py:62
  14.7 0.0 collective-permute-done.halo_ref
  14.7 2.8 %late.1 = (f32[160,2048]{1,0:T(8,128)S(1)}, bf16[160,2048]{1,0:T(8,128)(2,1)S(1)}, f32[2,256]{1,0:T(2,128)S(1)}) custom-call(bf16[144,2048]{1,0:T(8,128)(2,1)S(1)} %collective-permute-done.halo_ref, bf16[256,2048]{1,0:T(8,128)(2,1)S(1)} %copy-done.3, bf16[256,2048]{1,0:T(8,128)(2,1)S(1)} %copy-done.4, bf16[256,2048]{1,0:T(8,128)(2,1)S(1)} %copy-done, ...), custom_call_target="tpu_custom_call" | custom-call | flops 2900000000 | tf_op jit(solution)/shard_map/late/pallas_call | solution.py:62
  17.5 1.4 %collective-permute-start.1 = (f32[2,256]{1,0:T(2,128)S(1)}, f32[2,256]{1,0:T(2,128)S(1)}, u32[]{:S(2)}, u32[]{:S(2)}) collective-permute-start(f32[2,256]{1,0:T(2,128)S(1)} %get-tuple-element.50.rest_0_), channel_id=1, source_target_pairs={{0,1},{1,2},{2,3},{3,0},{4,5},{5,6},{6,7},{7,4},{8,9},{9,10},{10,1... | collective-permute-start | bytes 6152 | tf_op jit(solution)/shard_map/ppermute | solution.py:560
  18.9 2.6 %collective-permute-start.2 = (f32[2,256]{1,0:T(2,128)S(1)}, f32[2,256]{1,0:T(2,128)S(1)}, u32[]{:S(2)}, u32[]{:S(2)}) collective-permute-start(f32[2,256]{1,0:T(2,128)S(1)} %get-tuple-element.50.rest_0_), channel_id=1, source_target_pairs={{0,2},{1,3},{2,0},{3,1},{4,6},{5,7},{6,4},{7,5},{8,10},{9,11},{10,... | collective-permute-start | bytes 6152 | tf_op jit(solution)/shard_map/ppermute | solution.py:560
  21.5 1.1 %collective-permute-start.3 = (f32[2,256]{1,0:T(2,128)S(1)}, f32[2,256]{1,0:T(2,128)S(1)}, u32[]{:S(2)}, u32[]{:S(2)}) collective-permute-start(f32[2,256]{1,0:T(2,128)S(1)} %get-tuple-element.50.rest_0_), channel_id=1, source_target_pairs={{0,3},{1,0},{2,1},{3,2},{4,7},{5,4},{6,5},{7,6},{8,11},{9,8},{10,9... | collective-permute-start | bytes 6152 | tf_op jit(solution)/shard_map/ppermute | solution.py:560
  22.6 2.0 %wide_gated.1.wide_low_ref = f32[160,2048]{1,0:T(8,128)S(1)} custom-call(bf16[144,2048]{1,0:T(8,128)(2,1)S(1)} %collective-permute-done.halo_ref, bf16[256,2048]{1,0:T(8,128)(2,1)S(1)} %copy-done.3, bf16[256,2048]{1,0:T(8,128)(2,1)S(1)} %copy-done.4, bf16[4096,256]{1,0:T(8,128)(2,1)S(1)} %get-tuple-element.40.table_ref), custom_call_target="tpu_custom_call" | custom-call | flops 2000000000 | tf_op jit(solution)/shard_map/wide_gated/pallas_call | solution.py:62
  24.6 0.0 collective-permute-done.1.rest_1_
  24.6 0.0 collective-permute-done.2.rest_2_
  24.6 0.0 collective-permute-done.3.rest_3_
  24.6 0.9 %head_rows.1 = bf16[144,2048]{1,0:T(8,128)(2,1)S(1)} custom-call(bf16[256,2048]{1,0:T(8,128)(2,1)S(1)} %copy-done, bf16[256,2048]{1,0:T(8,128)(2,1)S(1)} %copy-done.1, f32[160,2048]{1,0:T(8,128)S(1)} %get-tuple-element.44.medium_low_ref.medium_ref, f32[1,2048]{1,0:T(1,128)S(1)} %bitcast.7, f32[2,256]{1,0:T(2,128)S(1)} %get-tuple-element.50.rest_0_, ...), custom_call_target="tpu_custom_call" | custom-call | flops 900000000 | tf_op jit(solution)/shard_map/head_rows/pallas_call | solution.py:62
  25.5 1.9 %collective-permute-start.4 = (bf16[144,2048]{1,0:T(8,128)(2,1)S(1)}, bf16[144,2048]{1,0:T(8,128)(2,1)S(1)}, u32[]{:S(2)}, u32[]{:S(2)}) collective-permute-start(bf16[144,2048]{1,0:T(8,128)(2,1)S(1)} %head_rows.1), channel_id=1, source_target_pairs={{4,0},{8,4},{12,8},{16,12},{20,16},{24,20},{28,24},{32,28},{36,32}... | collective-permute-start | bytes 1769480 | tf_op jit(solution)/shard_map/ppermute | solution.py:79
  27.4 6.7 %gradients.1 = (bf16[256,2048]{1,0:T(8,128)(2,1)}, bf16[256,2048]{1,0:T(8,128)(2,1)}, bf16[256,128]{1,0:T(8,128)(2,1)}) custom-call(bf16[256,2048]{1,0:T(8,128)(2,1)S(1)} %copy-done, bf16[256,2048]{1,0:T(8,128)(2,1)S(1)} %copy-done.1, f32[160,2048]{1,0:T(8,128)S(1)} %get-tuple-element.44.medium_low_ref.medium_ref, ...), custom_call_target="tpu_custom_call" | custom-call | flops 6600000000 | tf_op jit(solution)/shard_map/gradients/pallas_call | solution.py:62
  34.1 13.9 %all-to-all-start = ((bf16[64,4,128]{2,1,0:T(4,128)(2,1)}), bf16[64,4,128]{2,1,0:T(4,128)(2,1)S(1)}, u32[]{:S(2)}, u32[]{:S(2)}) async-start(bf16[64,4,128]{2,1,0:T(4,128)(2,1)} %bitcast.1), calls=%async_computation | async-start | bytes 131072 | tf_op jit(solution)/shard_map/all_to_all | solution.py:566
  48.0 0.0 collective-permute-done.4.halo_ref
  48.0 0.0 copy-start.7
  48.0 0.8 %copy-done.7 = bf16[144,2048]{1,0:T(8,128)(2,1)} copy-done((bf16[144,2048]{1,0:T(8,128)(2,1)}, bf16[144,2048]{1,0:T(8,128)(2,1)S(1)}, u32[]{:S(2)}) %copy-start.7) | copy-done | bytes 589848
  48.8 3.1 %backward.2 = (bf16[256,2048]{1,0:T(8,128)(2,1)}, bf16[256,2048]{1,0:T(8,128)(2,1)}) custom-call(bf16[256,2048]{1,0:T(8,128)(2,1)} %get-tuple-element.56.grad_ref, bf16[144,2048]{1,0:T(8,128)(2,1)} %copy-done.7, bf16[7,2048]{1,0:T(8,128)(2,1)} %se_ref.7, bf16[256,2048]{1,0:T(8,128)(2,1)} %key_ref.11, bf16[256,2048]{1,0:T(8,128)(2,1)} %value_ref.11, ...), custom_call_target="tpu_custom_call" | custom-call | flops 2000000000 | tf_op jit(solution)/shard_map/backward/pallas_call | solution.py:502
  52.0 6.1 %all-to-all-done = bf16[64,4,128]{2,1,0:T(4,128)(2,1)S(1)} async-done(((bf16[64,4,128]{2,1,0:T(4,128)(2,1)}), bf16[64,4,128]{2,1,0:T(4,128)(2,1)S(1)}, u32[]{:S(2)}, u32[]{:S(2)}) %all-to-all-start) | async-done | bytes 65568 | tf_op jit(solution)/shard_map/all_to_all | solution.py:566
  58.1 0.1 reduce_sum.12
  58.2 0.7 broadcast_in_dim.10
  58.8 4.4 %all-to-all-start.1 = ((bf16[64,4,128]{2,1,0:T(4,128)(2,1)}), bf16[64,4,128]{2,1,0:T(4,128)(2,1)S(1)}, u32[]{:S(2)}, u32[]{:S(2)}) async-start(bf16[64,4,128]{2,1,0:T(4,128)(2,1)} %broadcast_in_dim.10), calls=%async_computation.1 | async-start | bytes 131072 | tf_op jit(solution)/shard_map/all_to_all | solution.py:569
  63.3 5.8 %backward.3 = (bf16[256,2048]{1,0:T(8,128)(2,1)}, bf16[256,2048]{1,0:T(8,128)(2,1)}) custom-call(bf16[256,2048]{1,0:T(8,128)(2,1)} %get-tuple-element.56.grad_ref, bf16[144,2048]{1,0:T(8,128)(2,1)} %copy-done.7, bf16[7,2048]{1,0:T(8,128)(2,1)} %se_ref.7, bf16[256,2048]{1,0:T(8,128)(2,1)} %key_ref.11, ...), custom_call_target="tpu_custom_call", output_to_operand_aliasing={{0}: (6, {}), {1}: (7, {})} | custom-call | flops 6000000000 | tf_op jit(solution)/shard_map/backward/pallas_call | solution.py:502
  69.1 4.4 %all-to-all-done.1 = bf16[64,4,128]{2,1,0:T(4,128)(2,1)S(1)} async-done(((bf16[64,4,128]{2,1,0:T(4,128)(2,1)}), bf16[64,4,128]{2,1,0:T(4,128)(2,1)S(1)}, u32[]{:S(2)}, u32[]{:S(2)}) %all-to-all-start.1) | async-done | bytes 65568 | tf_op jit(solution)/shard_map/all_to_all | solution.py:569
  73.4 0.8 %finish.1 = (f32[128,128]{1,0:T(8,128)}, f32[7,2048]{1,0:T(8,128)}, f32[1,2048]{1,0:T(1,128)}) custom-call(bf16[256,128]{1,0:T(8,128)(2,1)S(1)} %bitcast.4), custom_call_target="tpu_custom_call" | custom-call | flops 900000000 | tf_op jit(solution)/shard_map/finish/pallas_call | solution.py:545
Async XLA Ops:
  0.6 6.3 %copy-start.5 = (bf16[128,128]{1,0:T(8,128)(2,1)S(1)}, bf16[128,128]{1,0:T(8,128)(2,1)}, u32[]{:S(2)}) copy-start(bf16[128,128]{1,0:T(8,128)(2,1)} %taps_ref.1) | copy-start | bytes 98308
  2.1 8.4 %copy-start = (bf16[256,2048]{1,0:T(8,128)(2,1)S(1)}, bf16[256,2048]{1,0:T(8,128)(2,1)}, u32[]{:S(2)}) copy-start(bf16[256,2048]{1,0:T(8,128)(2,1)} %query_ref.7) | copy-start | bytes 3145732
  2.1 8.4 %copy-start.1 = (bf16[256,2048]{1,0:T(8,128)(2,1)S(1)}, bf16[256,2048]{1,0:T(8,128)(2,1)}, u32[]{:S(2)}) copy-start(bf16[256,2048]{1,0:T(8,128)(2,1)} %out_grad_ref.7) | copy-start | bytes 3145732
  2.1 8.4 %copy-start.2 = (f32[2048]{0:T(1024)S(1)}, f32[2048]{0:T(1024)}, u32[]{:S(2)}) copy-start(f32[2048]{0:T(1024)} %param.13) | copy-start | bytes 24580
  2.1 8.4 %copy-start.3 = (bf16[256,2048]{1,0:T(8,128)(2,1)S(1)}, bf16[256,2048]{1,0:T(8,128)(2,1)}, u32[]{:S(2)}) copy-start(bf16[256,2048]{1,0:T(8,128)(2,1)} %key_ref.11) | copy-start | bytes 3145732
  2.2 8.4 %copy-start.4 = (bf16[256,2048]{1,0:T(8,128)(2,1)S(1)}, bf16[256,2048]{1,0:T(8,128)(2,1)}, u32[]{:S(2)}) copy-start(bf16[256,2048]{1,0:T(8,128)(2,1)} %value_ref.11) | copy-start | bytes 3145732
  2.2 8.4 %copy-start.6 = (bf16[7,2048]{1,0:T(8,128)(2,1)S(1)}, bf16[7,2048]{1,0:T(8,128)(2,1)}, u32[]{:S(2)}) copy-start(bf16[7,2048]{1,0:T(8,128)(2,1)} %se_ref.7) | copy-start | bytes 86020
  2.2 12.5 %collective-permute-start = (bf16[144,2048]{1,0:T(8,128)(2,1)S(1)}, bf16[144,2048]{1,0:T(8,128)(2,1)S(1)}, u32[]{:S(2)}, u32[]{:S(2)}) collective-permute-start(bf16[144,2048]{1,0:T(8,128)(2,1)S(1)} %tail_rows.1), channel_id=1, source_target_pairs={{0,4},{4,8},{8,12},{12,16},{16,20},{20,24},{24,28},{28,32},{32,36}... | collective-permute-start | bytes 1769480 | tf_op jit(solution)/shard_map/ppermute | solution.py:79
  17.5 7.1 %collective-permute-start.1 = (f32[2,256]{1,0:T(2,128)S(1)}, f32[2,256]{1,0:T(2,128)S(1)}, u32[]{:S(2)}, u32[]{:S(2)}) collective-permute-start(f32[2,256]{1,0:T(2,128)S(1)} %get-tuple-element.50.rest_0_), channel_id=1, source_target_pairs={{0,1},{1,2},{2,3},{3,0},{4,5},{5,6},{6,7},{7,4},{8,9},{9,10},{10,1... | collective-permute-start | bytes 6152 | tf_op jit(solution)/shard_map/ppermute | solution.py:560
  18.9 5.7 %collective-permute-start.2 = (f32[2,256]{1,0:T(2,128)S(1)}, f32[2,256]{1,0:T(2,128)S(1)}, u32[]{:S(2)}, u32[]{:S(2)}) collective-permute-start(f32[2,256]{1,0:T(2,128)S(1)} %get-tuple-element.50.rest_0_), channel_id=1, source_target_pairs={{0,2},{1,3},{2,0},{3,1},{4,6},{5,7},{6,4},{7,5},{8,10},{9,11},{10,... | collective-permute-start | bytes 6152 | tf_op jit(solution)/shard_map/ppermute | solution.py:560
  21.5 3.1 %collective-permute-start.3 = (f32[2,256]{1,0:T(2,128)S(1)}, f32[2,256]{1,0:T(2,128)S(1)}, u32[]{:S(2)}, u32[]{:S(2)}) collective-permute-start(f32[2,256]{1,0:T(2,128)S(1)} %get-tuple-element.50.rest_0_), channel_id=1, source_target_pairs={{0,3},{1,0},{2,1},{3,2},{4,7},{5,4},{6,5},{7,6},{8,11},{9,8},{10,9... | collective-permute-start | bytes 6152 | tf_op jit(solution)/shard_map/ppermute | solution.py:560
  25.5 22.5 %collective-permute-start.4 = (bf16[144,2048]{1,0:T(8,128)(2,1)S(1)}, bf16[144,2048]{1,0:T(8,128)(2,1)S(1)}, u32[]{:S(2)}, u32[]{:S(2)}) collective-permute-start(bf16[144,2048]{1,0:T(8,128)(2,1)S(1)} %head_rows.1), channel_id=1, source_target_pairs={{4,0},{8,4},{12,8},{16,12},{20,16},{24,20},{28,24},{32,28},{36,32}... | collective-permute-start | bytes 1769480 | tf_op jit(solution)/shard_map/ppermute | solution.py:79
  34.1 24.0 %all-to-all-start = ((bf16[64,4,128]{2,1,0:T(4,128)(2,1)}), bf16[64,4,128]{2,1,0:T(4,128)(2,1)S(1)}, u32[]{:S(2)}, u32[]{:S(2)}) async-start(bf16[64,4,128]{2,1,0:T(4,128)(2,1)} %bitcast.1), calls=%async_computation | async-start | bytes 131072 | tf_op jit(solution)/shard_map/all_to_all | solution.py:566
  48.0 0.8 %copy-start.7 = (bf16[144,2048]{1,0:T(8,128)(2,1)}, bf16[144,2048]{1,0:T(8,128)(2,1)S(1)}, u32[]{:S(2)}) copy-start(bf16[144,2048]{1,0:T(8,128)(2,1)S(1)} %collective-permute-done.4.halo_ref) | copy-start | bytes 1769476
  58.8 14.6 %all-to-all-start.1 = ((bf16[64,4,128]{2,1,0:T(4,128)(2,1)}), bf16[64,4,128]{2,1,0:T(4,128)(2,1)S(1)}, u32[]{:S(2)}, u32[]{:S(2)}) async-start(bf16[64,4,128]{2,1,0:T(4,128)(2,1)} %broadcast_in_dim.10), calls=%async_computation.1 | async-start | bytes 131072 | tf_op jit(solution)/shard_map/all_to_all | solution.py:569

commit v9 on v8

--- a/solution.py
+++ b/solution.py
@@ -25,7 +25,7 @@
 
 
 UNROLL = 8
-TAIL_PARTS = 4
+TAIL_PARTS = 2
 BW = 512
 PARTS = (0, 1, 4)
 WIRE = jnp.bfloat16

time: 74.5 us -> 74.4 us (level)
  no operation moved by 1% of the time
where the time goes in v9:
time: 74.4 us; the launch traced here: 74.1 us
  Pallas kernels  31.1 us (42%)
  starting transfers between devices  30.1 us (40%)
  waiting for transfers between devices  10.5 us (14%)
  local copies, waits for them, and re-layouts  1.5 us (2%)
  between operations  0.87 us (1%)
    pallas_call x6, Pallas kernels, call(): pl.pallas_call(body, in_specs=[VMEM] * len(args), out_specs=out_specs, ou...  20 us
    all_to_all x1, starting transfers between devices, sum_over_ctx(): lax.all_to_all(parts, 'ctx', 0, 0)  13.9 us
    pallas_call x2, Pallas kernels, backward(): pl.pallas_call(backward_kernel, grid=(steps,), in_specs=[col(tok), col(HA...  8.91 us
    ppermute x2, starting transfers between devices, shifted(): lax.ppermute(x, 'ctx', [(i, i + by) for i in range(peers) if 0 <= i + by...  6.69 us
    all_to_all x1, waiting for transfers between devices, sum_over_ctx(): lax.all_to_all(parts, 'ctx', 0, 0)  6.12 us
    ppermute x3, starting transfers between devices, from_peers(): lax.ppermute(x, axis, [(i, (i + k) % peers) for i in range(peers)])  5.05 us
    all_to_all x1, starting transfers between devices, sum_over_ctx(): lax.all_to_all(jnp.broadcast_to(mine[None], parts.shape), 'ctx', 0, 0)  4.44 us
    all_to_all x1, waiting for transfers between devices, sum_over_ctx(): lax.all_to_all(jnp.broadcast_to(mine[None], parts.shape), 'ctx', 0, 0)  4.37 us
  transfers between devices with their start and end apart: 7, of which 2 were waited for; matrix products, arithmetic and copies ran while one was open for 0% of the time, Pallas kernels for 34%

profile of v9, /device:TPU:1, one launch (start us, length us, event | category | flops | bytes accessed | tf_op | source)
XLA Modules:
  0.0 74.1 jit_solution(591200001062121993)
XLA Ops:
  0.6 0.0 copy-start.5
  0.6 1.3 %tail_rows.1 = bf16[144,2048]{1,0:T(8,128)(2,1)S(1)} custom-call(bf16[256,2048]{1,0:T(8,128)(2,1)} %key_ref.11, bf16[256,2048]{1,0:T(8,128)(2,1)} %value_ref.11), custom_call_target="tpu_custom_call" | custom-call | flops 1200000000 | tf_op jit(solution)/shard_map/tail_rows/pallas_call | solution.py:173
  2.0 0.0 copy-start
  2.0 0.0 copy-start.1
  2.0 0.0 copy-start.2
  2.0 0.0 copy-start.3
  2.0 0.0 copy-start.4
  2.0 0.0 copy-start.6
  2.1 4.8 %collective-permute-start = (bf16[144,2048]{1,0:T(8,128)(2,1)S(1)}, bf16[144,2048]{1,0:T(8,128)(2,1)S(1)}, u32[]{:S(2)}, u32[]{:S(2)}) collective-permute-start(bf16[144,2048]{1,0:T(8,128)(2,1)S(1)} %tail_rows.1), channel_id=1, source_target_pairs={{0,4},{4,8},{8,12},{12,16},{16,20},{20,24},{24,28},{28,32},{32,36}... | collective-permute-start | bytes 1769480 | tf_op jit(solution)/shard_map/ppermute | solution.py:79
  6.8 0.0 copy-done.5
  6.8 3.5 %filter_tables.1 = (bf16[4096,256]{1,0:T(8,128)(2,1)S(1)}, bf16[4096,256]{1,0:T(8,128)(2,1)}) custom-call(bf16[128,128]{1,0:T(8,128)(2,1)S(1)} %copy-done.5), custom_call_target="tpu_custom_call" | custom-call | flops 2400000000 | tf_op jit(solution)/shard_map/filter_tables/pallas_call | solution.py:62
  10.4 0.0 copy-done
  10.4 0.0 copy-done.1
  10.4 0.0 copy-done.2
  10.4 0.0 copy-done.3
  10.4 0.0 copy-done.4
  10.5 0.0 copy-done.6
  10.5 4.1 %early.1 = (f32[96,2048]{1,0:T(8,128)S(1)}, bf16[256,2048]{1,0:T(8,128)(2,1)S(1)}, f32[128,2048]{1,0:T(8,128)S(1)}, f32[96,128]{1,0:T(8,128)S(1)}, f32[96,128]{1,0:T(8,128)S(1)}) custom-call(bf16[256,2048]{1,0:T(8,128)(2,1)S(1)} %copy-done.3, bf16[256,2048]{1,0:T(8,128)(2,1)S(1)} %copy-done.4, bf16[256,2048]{1,0:T(8,128)(2,1)S(1)} %copy-done, ...), custom_call_target="tpu_custom_call" | custom-call | flops 4200000000 | tf_op jit(solution)/shard_map/early/pallas_call | solution.py:62
  14.6 0.0 collective-permute-done.halo_ref
  14.6 2.8 %late.1 = (f32[160,2048]{1,0:T(8,128)S(1)}, bf16[160,2048]{1,0:T(8,128)(2,1)S(1)}, f32[2,256]{1,0:T(2,128)S(1)}) custom-call(bf16[144,2048]{1,0:T(8,128)(2,1)S(1)} %collective-permute-done.halo_ref, bf16[256,2048]{1,0:T(8,128)(2,1)S(1)} %copy-done.3, bf16[256,2048]{1,0:T(8,128)(2,1)S(1)} %copy-done.4, bf16[256,2048]{1,0:T(8,128)(2,1)S(1)} %copy-done, ...), custom_call_target="tpu_custom_call" | custom-call | flops 2900000000 | tf_op jit(solution)/shard_map/late/pallas_call | solution.py:62
  17.4 1.4 %collective-permute-start.1 = (f32[2,256]{1,0:T(2,128)S(1)}, f32[2,256]{1,0:T(2,128)S(1)}, u32[]{:S(2)}, u32[]{:S(2)}) collective-permute-start(f32[2,256]{1,0:T(2,128)S(1)} %get-tuple-element.50.rest_0_), channel_id=1, source_target_pairs={{0,1},{1,2},{2,3},{3,0},{4,5},{5,6},{6,7},{7,4},{8,9},{9,10},{10,1... | collective-permute-start | bytes 6152 | tf_op jit(solution)/shard_map/ppermute | solution.py:560
  18.8 2.6 %collective-permute-start.2 = (f32[2,256]{1,0:T(2,128)S(1)}, f32[2,256]{1,0:T(2,128)S(1)}, u32[]{:S(2)}, u32[]{:S(2)}) collective-permute-start(f32[2,256]{1,0:T(2,128)S(1)} %get-tuple-element.50.rest_0_), channel_id=1, source_target_pairs={{0,2},{1,3},{2,0},{3,1},{4,6},{5,7},{6,4},{7,5},{8,10},{9,11},{10,... | collective-permute-start | bytes 6152 | tf_op jit(solution)/shard_map/ppermute | solution.py:560
  21.4 1.1 %collective-permute-start.3 = (f32[2,256]{1,0:T(2,128)S(1)}, f32[2,256]{1,0:T(2,128)S(1)}, u32[]{:S(2)}, u32[]{:S(2)}) collective-permute-start(f32[2,256]{1,0:T(2,128)S(1)} %get-tuple-element.50.rest_0_), channel_id=1, source_target_pairs={{0,3},{1,0},{2,1},{3,2},{4,7},{5,4},{6,5},{7,6},{8,11},{9,8},{10,9... | collective-permute-start | bytes 6152 | tf_op jit(solution)/shard_map/ppermute | solution.py:560
  22.5 2.0 %wide_gated.1.wide_low_ref = f32[160,2048]{1,0:T(8,128)S(1)} custom-call(bf16[144,2048]{1,0:T(8,128)(2,1)S(1)} %collective-permute-done.halo_ref, bf16[256,2048]{1,0:T(8,128)(2,1)S(1)} %copy-done.3, bf16[256,2048]{1,0:T(8,128)(2,1)S(1)} %copy-done.4, bf16[4096,256]{1,0:T(8,128)(2,1)S(1)} %get-tuple-element.40.table_ref), custom_call_target="tpu_custom_call" | custom-call | flops 2000000000 | tf_op jit(solution)/shard_map/wide_gated/pallas_call | solution.py:62
  24.5 0.0 collective-permute-done.1.rest_1_
  24.5 0.0 collective-permute-done.2.rest_2_
  24.5 0.0 collective-permute-done.3.rest_3_
  24.5 0.9 %head_rows.1 = bf16[144,2048]{1,0:T(8,128)(2,1)S(1)} custom-call(bf16[256,2048]{1,0:T(8,128)(2,1)S(1)} %copy-done, bf16[256,2048]{1,0:T(8,128)(2,1)S(1)} %copy-done.1, f32[160,2048]{1,0:T(8,128)S(1)} %get-tuple-element.44.medium_low_ref.medium_ref, f32[1,2048]{1,0:T(1,128)S(1)} %bitcast.7, f32[2,256]{1,0:T(2,128)S(1)} %get-tuple-element.50.rest_0_, ...), custom_call_target="tpu_custom_call" | custom-call | flops 900000000 | tf_op jit(solution)/shard_map/head_rows/pallas_call | solution.py:62
  25.4 1.9 %collective-permute-start.4 = (bf16[144,2048]{1,0:T(8,128)(2,1)S(1)}, bf16[144,2048]{1,0:T(8,128)(2,1)S(1)}, u32[]{:S(2)}, u32[]{:S(2)}) collective-permute-start(bf16[144,2048]{1,0:T(8,128)(2,1)S(1)} %head_rows.1), channel_id=1, source_target_pairs={{4,0},{8,4},{12,8},{16,12},{20,16},{24,20},{28,24},{32,28},{36,32}... | collective-permute-start | bytes 1769480 | tf_op jit(solution)/shard_map/ppermute | solution.py:79
  27.3 6.7 %gradients.1 = (bf16[256,2048]{1,0:T(8,128)(2,1)}, bf16[256,2048]{1,0:T(8,128)(2,1)}, bf16[256,128]{1,0:T(8,128)(2,1)}) custom-call(bf16[256,2048]{1,0:T(8,128)(2,1)S(1)} %copy-done, bf16[256,2048]{1,0:T(8,128)(2,1)S(1)} %copy-done.1, f32[160,2048]{1,0:T(8,128)S(1)} %get-tuple-element.44.medium_low_ref.medium_ref, ...), custom_call_target="tpu_custom_call" | custom-call | flops 6600000000 | tf_op jit(solution)/shard_map/gradients/pallas_call | solution.py:62
  34.0 13.9 %all-to-all-start = ((bf16[64,4,128]{2,1,0:T(4,128)(2,1)}), bf16[64,4,128]{2,1,0:T(4,128)(2,1)S(1)}, u32[]{:S(2)}, u32[]{:S(2)}) async-start(bf16[64,4,128]{2,1,0:T(4,128)(2,1)} %bitcast.1), calls=%async_computation | async-start | bytes 131072 | tf_op jit(solution)/shard_map/all_to_all | solution.py:566
  47.9 0.0 collective-permute-done.4.halo_ref
  47.9 0.0 copy-start.7
  47.9 0.8 %copy-done.7 = bf16[144,2048]{1,0:T(8,128)(2,1)} copy-done((bf16[144,2048]{1,0:T(8,128)(2,1)}, bf16[144,2048]{1,0:T(8,128)(2,1)S(1)}, u32[]{:S(2)}) %copy-start.7) | copy-done | bytes 589848
  48.7 3.1 %backward.2 = (bf16[256,2048]{1,0:T(8,128)(2,1)}, bf16[256,2048]{1,0:T(8,128)(2,1)}) custom-call(bf16[256,2048]{1,0:T(8,128)(2,1)} %get-tuple-element.56.grad_ref, bf16[144,2048]{1,0:T(8,128)(2,1)} %copy-done.7, bf16[7,2048]{1,0:T(8,128)(2,1)} %se_ref.7, bf16[256,2048]{1,0:T(8,128)(2,1)} %key_ref.11, bf16[256,2048]{1,0:T(8,128)(2,1)} %value_ref.11, ...), custom_call_target="tpu_custom_call" | custom-call | flops 2000000000 | tf_op jit(solution)/shard_map/backward/pallas_call | solution.py:502
  51.9 6.1 %all-to-all-done = bf16[64,4,128]{2,1,0:T(4,128)(2,1)S(1)} async-done(((bf16[64,4,128]{2,1,0:T(4,128)(2,1)}), bf16[64,4,128]{2,1,0:T(4,128)(2,1)S(1)}, u32[]{:S(2)}, u32[]{:S(2)}) %all-to-all-start) | async-done | bytes 65568 | tf_op jit(solution)/shard_map/all_to_all | solution.py:566
  58.0 0.1 reduce_sum.12
  58.1 0.7 broadcast_in_dim.10
  58.7 4.4 %all-to-all-start.1 = ((bf16[64,4,128]{2,1,0:T(4,128)(2,1)}), bf16[64,4,128]{2,1,0:T(4,128)(2,1)S(1)}, u32[]{:S(2)}, u32[]{:S(2)}) async-start(bf16[64,4,128]{2,1,0:T(4,128)(2,1)} %broadcast_in_dim.10), calls=%async_computation.1 | async-start | bytes 131072 | tf_op jit(solution)/shard_map/all_to_all | solution.py:569
  63.2 5.8 %backward.3 = (bf16[256,2048]{1,0:T(8,128)(2,1)}, bf16[256,2048]{1,0:T(8,128)(2,1)}) custom-call(bf16[256,2048]{1,0:T(8,128)(2,1)} %get-tuple-element.56.grad_ref, bf16[144,2048]{1,0:T(8,128)(2,1)} %copy-done.7, bf16[7,2048]{1,0:T(8,128)(2,1)} %se_ref.7, bf16[256,2048]{1,0:T(8,128)(2,1)} %key_ref.11, ...), custom_call_target="tpu_custom_call", output_to_operand_aliasing={{0}: (6, {}), {1}: (7, {})} | custom-call | flops 6000000000 | tf_op jit(solution)/shard_map/backward/pallas_call | solution.py:502
  68.9 4.4 %all-to-all-done.1 = bf16[64,4,128]{2,1,0:T(4,128)(2,1)S(1)} async-done(((bf16[64,4,128]{2,1,0:T(4,128)(2,1)}), bf16[64,4,128]{2,1,0:T(4,128)(2,1)S(1)}, u32[]{:S(2)}, u32[]{:S(2)}) %all-to-all-start.1) | async-done | bytes 65568 | tf_op jit(solution)/shard_map/all_to_all | solution.py:569
  73.3 0.8 %finish.1 = (f32[128,128]{1,0:T(8,128)}, f32[7,2048]{1,0:T(8,128)}, f32[1,2048]{1,0:T(1,128)}) custom-call(bf16[256,128]{1,0:T(8,128)(2,1)S(1)} %bitcast.4), custom_call_target="tpu_custom_call" | custom-call | flops 900000000 | tf_op jit(solution)/shard_map/finish/pallas_call | solution.py:545
Async XLA Ops:
  0.6 6.2 %copy-start.5 = (bf16[128,128]{1,0:T(8,128)(2,1)S(1)}, bf16[128,128]{1,0:T(8,128)(2,1)}, u32[]{:S(2)}) copy-start(bf16[128,128]{1,0:T(8,128)(2,1)} %taps_ref.1) | copy-start | bytes 98308
  2.0 8.4 %copy-start = (bf16[256,2048]{1,0:T(8,128)(2,1)S(1)}, bf16[256,2048]{1,0:T(8,128)(2,1)}, u32[]{:S(2)}) copy-start(bf16[256,2048]{1,0:T(8,128)(2,1)} %query_ref.7) | copy-start | bytes 3145732
  2.0 8.4 %copy-start.1 = (bf16[256,2048]{1,0:T(8,128)(2,1)S(1)}, bf16[256,2048]{1,0:T(8,128)(2,1)}, u32[]{:S(2)}) copy-start(bf16[256,2048]{1,0:T(8,128)(2,1)} %out_grad_ref.7) | copy-start | bytes 3145732
  2.0 8.4 %copy-start.2 = (f32[2048]{0:T(1024)S(1)}, f32[2048]{0:T(1024)}, u32[]{:S(2)}) copy-start(f32[2048]{0:T(1024)} %param.13) | copy-start | bytes 24580
  2.0 8.4 %copy-start.3 = (bf16[256,2048]{1,0:T(8,128)(2,1)S(1)}, bf16[256,2048]{1,0:T(8,128)(2,1)}, u32[]{:S(2)}) copy-start(bf16[256,2048]{1,0:T(8,128)(2,1)} %key_ref.11) | copy-start | bytes 3145732
  2.0 8.4 %copy-start.4 = (bf16[256,2048]{1,0:T(8,128)(2,1)S(1)}, bf16[256,2048]{1,0:T(8,128)(2,1)}, u32[]{:S(2)}) copy-start(bf16[256,2048]{1,0:T(8,128)(2,1)} %value_ref.11) | copy-start | bytes 3145732
  2.0 8.4 %copy-start.6 = (bf16[7,2048]{1,0:T(8,128)(2,1)S(1)}, bf16[7,2048]{1,0:T(8,128)(2,1)}, u32[]{:S(2)}) copy-start(bf16[7,2048]{1,0:T(8,128)(2,1)} %se_ref.7) | copy-start | bytes 86020
  2.1 12.5 %collective-permute-start = (bf16[144,2048]{1,0:T(8,128)(2,1)S(1)}, bf16[144,2048]{1,0:T(8,128)(2,1)S(1)}, u32[]{:S(2)}, u32[]{:S(2)}) collective-permute-start(bf16[144,2048]{1,0:T(8,128)(2,1)S(1)} %tail_rows.1), channel_id=1, source_target_pairs={{0,4},{4,8},{8,12},{12,16},{16,20},{20,24},{24,28},{28,32},{32,36}... | collective-permute-start | bytes 1769480 | tf_op jit(solution)/shard_map/ppermute | solution.py:79
  17.4 7.1 %collective-permute-start.1 = (f32[2,256]{1,0:T(2,128)S(1)}, f32[2,256]{1,0:T(2,128)S(1)}, u32[]{:S(2)}, u32[]{:S(2)}) collective-permute-start(f32[2,256]{1,0:T(2,128)S(1)} %get-tuple-element.50.rest_0_), channel_id=1, source_target_pairs={{0,1},{1,2},{2,3},{3,0},{4,5},{5,6},{6,7},{7,4},{8,9},{9,10},{10,1... | collective-permute-start | bytes 6152 | tf_op jit(solution)/shard_map/ppermute | solution.py:560
  18.8 5.7 %collective-permute-start.2 = (f32[2,256]{1,0:T(2,128)S(1)}, f32[2,256]{1,0:T(2,128)S(1)}, u32[]{:S(2)}, u32[]{:S(2)}) collective-permute-start(f32[2,256]{1,0:T(2,128)S(1)} %get-tuple-element.50.rest_0_), channel_id=1, source_target_pairs={{0,2},{1,3},{2,0},{3,1},{4,6},{5,7},{6,4},{7,5},{8,10},{9,11},{10,... | collective-permute-start | bytes 6152 | tf_op jit(solution)/shard_map/ppermute | solution.py:560
  21.4 3.1 %collective-permute-start.3 = (f32[2,256]{1,0:T(2,128)S(1)}, f32[2,256]{1,0:T(2,128)S(1)}, u32[]{:S(2)}, u32[]{:S(2)}) collective-permute-start(f32[2,256]{1,0:T(2,128)S(1)} %get-tuple-element.50.rest_0_), channel_id=1, source_target_pairs={{0,3},{1,0},{2,1},{3,2},{4,7},{5,4},{6,5},{7,6},{8,11},{9,8},{10,9... | collective-permute-start | bytes 6152 | tf_op jit(solution)/shard_map/ppermute | solution.py:560
  25.4 22.5 %collective-permute-start.4 = (bf16[144,2048]{1,0:T(8,128)(2,1)S(1)}, bf16[144,2048]{1,0:T(8,128)(2,1)S(1)}, u32[]{:S(2)}, u32[]{:S(2)}) collective-permute-start(bf16[144,2048]{1,0:T(8,128)(2,1)S(1)} %head_rows.1), channel_id=1, source_target_pairs={{4,0},{8,4},{12,8},{16,12},{20,16},{24,20},{28,24},{32,28},{36,32}... | collective-permute-start | bytes 1769480 | tf_op jit(solution)/shard_map/ppermute | solution.py:79
  34.0 24.0 %all-to-all-start = ((bf16[64,4,128]{2,1,0:T(4,128)(2,1)}), bf16[64,4,128]{2,1,0:T(4,128)(2,1)S(1)}, u32[]{:S(2)}, u32[]{:S(2)}) async-start(bf16[64,4,128]{2,1,0:T(4,128)(2,1)} %bitcast.1), calls=%async_computation | async-start | bytes 131072 | tf_op jit(solution)/shard_map/all_to_all | solution.py:566
  47.9 0.8 %copy-start.7 = (bf16[144,2048]{1,0:T(8,128)(2,1)}, bf16[144,2048]{1,0:T(8,128)(2,1)S(1)}, u32[]{:S(2)}) copy-start(bf16[144,2048]{1,0:T(8,128)(2,1)S(1)} %collective-permute-done.4.halo_ref) | copy-start | bytes 1769476
  58.7 14.6 %all-to-all-start.1 = ((bf16[64,4,128]{2,1,0:T(4,128)(2,1)}), bf16[64,4,128]{2,1,0:T(4,128)(2,1)S(1)}, u32[]{:S(2)}, u32[]{:S(2)}) async-start(bf16[64,4,128]{2,1,0:T(4,128)(2,1)} %broadcast_in_dim.10), calls=%async_computation.1 | async-start | bytes 131072 | tf_op jit(solution)/shard_map/all_to_all | solution.py:569
